TPU v7x, 128 devices: a whole 4x4x4 slice. The times are simulated.
128 devices in a mesh: row: 8 (over z_hi, x), col: 16 (over y, z_lo, core).
Axes of the slice: x: 4, y: 4, z: 4 (z_hi: 2, z_lo: 2; z = z_hi * 2 + z_lo), core: 2. Of those that a mesh axis runs over, the one named last changes fastest.
Arguments:
- view_one: bfloat16 [1024, 16384], P(('row', 'col')), may hold values from -70 to 70
- view_two: bfloat16 [1024, 16384], P(('row', 'col')), may hold values from -70 to 70
Outputs:
- grad_one: float32 [1024, 16384], P(('row', 'col'))
- grad_two: float32 [1024, 16384], P(('row', 'col'))
- total_loss: float32 [], replicated
All inputs are finite; a program needn't handle non-finite values.
Results may differ from a plain program's by a relative error of at most 0.0031.
Values may be sent and summed in bfloat16 or wider, within the bound.
No kernel may reach another device: no remote copies, remote signals or barrier semaphores. Data moves between devices by JAX's collectives and lax.ppermute only.
A program may use at most 128 MiB of HBM per device.

v0:
```python
import jax
import jax.numpy as jnp
from jax import lax
from jax.sharding import PartitionSpec as P

epsilon = 0.0001
inv_weight = 25.0
var_weight = 25.0
cov_weight = 1.0
out_scale = 25.0


def center(raw_block, batch_rows):
    values = raw_block.astype(jnp.float32)
    col_total = jnp.sum(values, axis=0) / batch_rows
    centered = values - col_total
    spread = jnp.sqrt(jnp.sum(centered * centered, axis=0) / (batch_rows - 1) + epsilon)
    return (centered, spread)


def feature_part(x_raw, y_raw, row_idx, col_idx, row_devices, col_devices):
    batch_rows = x_raw.shape[0]
    row_width = x_raw.shape[1]
    col_width = y_raw.shape[1]
    shard_rows = batch_rows // (row_devices * col_devices)
    x_cent, x_spread = center(x_raw, batch_rows)
    y_cent, y_spread = center(y_raw, batch_rows)
    x_round = x_cent.astype(jnp.bfloat16)
    y_round = y_cent.astype(jnp.bfloat16)
    cov_tile = lax.dot_general(
        x_round, y_round, (((0,), (0,)), ((), ())), preferred_element_type=jnp.float32
    ) / (batch_rows - 1)
    row_ids = row_idx * row_width + jnp.arange(row_width, dtype=jnp.int32)
    col_ids = col_idx * col_width + jnp.arange(col_width, dtype=jnp.int32)
    off_diag = jnp.where(row_ids[:, None] == col_ids[None, :], 0.0, cov_tile)
    cov_sum = jnp.sum(off_diag * off_diag)
    tile_round = off_diag.astype(jnp.bfloat16)
    hinge_sum = jnp.sum(jnp.maximum(1.0 - y_spread, 0.0))
    factor_cov = 4.0 * cov_weight * batch_rows / (batch_rows - 1)
    factor_var = var_weight * batch_rows / (batch_rows - 1)
    permuted = y_round.reshape(row_devices, col_devices, shard_rows, col_width)
    permuted = permuted.transpose(1, 0, 2, 3).reshape(batch_rows, col_width)
    summed = lax.psum_scatter(
        lax.dot_general(
            permuted, tile_round, (((1,), (1,)), ((), ())), preferred_element_type=jnp.float32
        ),
        "col",
        scatter_dimension=0,
        tiled=True,
    )
    chosen = lax.dynamic_index_in_dim(
        x_cent.reshape(row_devices, col_devices, shard_rows, row_width), col_idx, 1, keepdims=False
    )
    chosen = chosen.reshape(batch_rows // col_devices, row_width)
    grad_part = factor_cov * summed - factor_var * jnp.where(x_spread < 1.0, chosen / x_spread, 0.0)
    return (grad_part, cov_sum, hinge_sum)


def body(view_one, view_two):
    shard_rows = view_one.shape[0]
    feature_count = view_one.shape[1]
    row_devices = lax.axis_size("row")
    col_devices = lax.axis_size("col")
    row_idx = lax.axis_index("row")
    col_idx = lax.axis_index("col")
    col_split_data = (
        lax.all_to_all(view_one, "col", split_axis=1, concat_axis=0, tiled=True),
        lax.all_to_all(view_two, "col", split_axis=1, concat_axis=0, tiled=True),
    )
    col_blocks_data = (
        lax.all_gather(col_split_data[0], "row", axis=0, tiled=True),
        lax.all_gather(col_split_data[1], "row", axis=0, tiled=True),
    )
    full_rows = (
        lax.all_gather(view_one, "col", axis=0, tiled=True),
        lax.all_gather(view_two, "col", axis=0, tiled=True),
    )
    row_blocks_data = (
        lax.all_to_all(full_rows[0], "row", split_axis=1, concat_axis=0, tiled=True),
        lax.all_to_all(full_rows[1], "row", split_axis=1, concat_axis=0, tiled=True),
    )
    part_first, cov_first, hinge_first = feature_part(
        row_blocks_data[0], col_blocks_data[0], row_idx, col_idx, row_devices, col_devices
    )
    part_second, cov_second, hinge_second = feature_part(
        row_blocks_data[1], col_blocks_data[1], row_idx, col_idx, row_devices, col_devices
    )
    returned = (
        lax.all_to_all(part_first, "row", split_axis=0, concat_axis=1, tiled=True),
        lax.all_to_all(part_second, "row", split_axis=0, concat_axis=1, tiled=True),
    )
    view_diff = view_one.astype(jnp.float32) - view_two.astype(jnp.float32)
    inv_local = jnp.sum(view_diff * view_diff)
    hinge_local = jnp.where(row_idx == 0, hinge_first + hinge_second, 0.0)
    sums = lax.psum((inv_local, hinge_local, cov_first + cov_second), ("row", "col"))
    batch_rows = shard_rows * row_devices * col_devices
    total_loss = (
        inv_weight * sums[0] / (batch_rows * feature_count)
        + var_weight * sums[1] / feature_count
        + cov_weight * sums[2] / feature_count
    )
    grad_one = (returned[0] + 2.0 * inv_weight * view_diff) / out_scale
    grad_two = (returned[1] - 2.0 * inv_weight * view_diff) / out_scale
    return (grad_one, grad_two, total_loss)


def solution(mesh):
    in_specs = (P(("row", "col"), None), P(("row", "col"), None))
    out_specs = (P(("row", "col"), None), P(("row", "col"), None), P())
    return jax.shard_map(body, mesh=mesh, in_specs=in_specs, out_specs=out_specs, check_vma=False)
```

profile of v0, /device:TPU:0, one launch (start us, length us, event | category | flops | bytes accessed | tf_op | source)
XLA Modules:
  0.0 581.6 jit_solution(16622424866850729736)
XLA Ops:
  7.9 13.8 %all_to_all.102 = bf16[8,16,1024]{2,0,1:T(8,128)(2,1)} all-to-all(bf16[8,16,1024]{2,0,1:T(8,128)(2,1)} %bitcast.79), channel_id=1, replica_groups=mesh['row'=8,'col'=16] {'col'}, dimensions={1} | all-to-all | bytes 524288 | tf_op jit(solution)/shard_map/all_to_all | solution.py:67
  26.1 26.1 %all-gather.7.cloned.1.call-done = bf16[128,16384]{1,0:T(8,128)(2,1)} async-done(((bf16[8,16384]{1,0:T(8,128)(2,1)}), bf16[128,16384]{1,0:T(8,128)(2,1)}) %all-gather.7.cloned.1.call-update) | async-done | bytes 4194320 | tf_op jit(solution)/shard_map/all_gather | solution.py:75
  52.2 6.4 %copy.14 = bf16[128,16384]{0,1:T(8,128)(2,1)} copy(bf16[128,16384]{1,0:T(8,128)(2,1)} %all-gather.7.cloned.1.call-done) | data formatting | bytes 8388608 | tf_op jit(solution)/shard_map/all_gather | solution.py:75
  59.3 6.5 %all-to-all-start.1 = ((bf16[128,8,2048]{0,2,1:T(8,128)(2,1)}), bf16[128,8,2048]{0,2,1:T(8,128)(2,1)}, u32[]{:S(2)}, u32[]{:S(2)}) async-start(bf16[128,8,2048]{0,2,1:T(8,128)(2,1)} %bitcast.74), calls=%async_computation.1 | async-start | bytes 8388608 | tf_op jit(solution)/shard_map/all_to_all | solution.py:79
  66.4 84.5 %all-gather.5.cloned.1.call-done = bf16[1024,1024]{1,0:T(8,128)(2,1)} async-done(((bf16[128,1024]{1,0:T(8,128)(2,1)}), bf16[1024,1024]{1,0:T(8,128)(2,1)}) %all-gather.5.cloned.1.call-update) | async-done | bytes 2097168 | tf_op jit(solution)/shard_map/all_gather | solution.py:71
  156.8 5.9 %convert_bitcast_fusion.1 = f32[8,128,2048]{1,2,0:T(8,128)} fusion(bf16[128,8,2048]{0,2,1:T(8,128)(2,1)} %all-to-all-done.1), kind=kLoop, calls=%fused_computation.5 | loop fusion | flops 2097152 | bytes 12582912 | tf_op jit(solution)/shard_map/convert_element_type | solution.py:14
  162.7 9.2 %copy.15 = f32[8,128,2048]{2,1,0:T(8,128)} copy(f32[8,128,2048]{1,2,0:T(8,128)} %convert_bitcast_fusion.1) | data formatting | bytes 16777216 | tf_op jit(solution)/shard_map/convert_element_type | solution.py:14
  174.8 4.7 fusion.5
  179.5 4.6 fusion.43
  187.3 6.9 %fusion.16 = f32[1024,2048]{1,0:T(8,128)} fusion(bf16[1024,1024]{1,0:T(8,128)(2,1)S(1)} %bitcast.81, f32[2048,1024]{1,0:T(8,128)S(1)} %fusion.43, s32[1024]{0:T(1024)S(1)} %iota_add_fusion.1, s32[2048]{0:T(1024)S(1)} %iota_add_fusion), kind=kOutput, calls=%fused_computation.31 | convolution fusion | flops 4303355904 | bytes 18886656 | tf_op jit(solution)/shard_map/dot_general | solution.py:44
  194.3 6.4 %copy.18 = bf16[128,16384]{0,1:T(8,128)(2,1)} copy(bf16[128,16384]{1,0:T(8,128)(2,1)} %all-gather.11.cloned.1.call-done) | data formatting | bytes 8388608 | tf_op jit(solution)/shard_map/all_gather | solution.py:76
  200.7 4.5 all-to-all-start.4
  205.5 82.3 %all-gather.9.cloned.1.call-done = bf16[1024,1024]{1,0:T(8,128)(2,1)} async-done(((bf16[128,1024]{1,0:T(8,128)(2,1)}), bf16[1024,1024]{1,0:T(8,128)(2,1)}) %all-gather.9.cloned.1.call-update) | async-done | bytes 2097168 | tf_op jit(solution)/shard_map/all_gather | solution.py:72
  293.6 5.9 %convert_bitcast_fusion = f32[8,128,2048]{1,2,0:T(8,128)} fusion(bf16[128,8,2048]{0,2,1:T(8,128)(2,1)} %all-to-all-done.4), kind=kLoop, calls=%fused_computation.2 | loop fusion | flops 2097152 | bytes 12582912 | tf_op jit(solution)/shard_map/convert_element_type | solution.py:14
  299.6 9.2 %copy.19 = f32[8,128,2048]{2,1,0:T(8,128)} copy(f32[8,128,2048]{1,2,0:T(8,128)} %convert_bitcast_fusion) | data formatting | bytes 16777216 | tf_op jit(solution)/shard_map/convert_element_type | solution.py:14
  311.8 4.8 fusion.4
  316.6 9.2 %multiply_reduce_fusion = (f32[]{:T(128)}, f32[]{:T(128)}, f32[2048,1024]{1,0:T(8,128)}) fusion(s32[1024]{0:T(1024)S(1)} %iota_add_fusion.1, s32[2048]{0:T(1024)S(1)} %iota_add_fusion, f32[2048,1024]{1,0:T(8,128)S(1)} %bitcast.87, bf16[1024,2048]{1,0:T(8,128)(2,1)S(1)} %fusion.4, bf16[1024,1024]{1,0:T(8,128)(2,1)S(1)} %get-tuple-element.9), kind=kOutput, calls=%fused_computation.16 | convolution fusion | flops 4313841664 | bytes 23080968 | tf_op jit(solution)/shard_map/dot_general | solution.py:30
  325.9 11.3 %fusion.14 = f32[1024,2048]{1,0:T(8,128)} fusion(bf16[1024,1024]{1,0:T(8,128)(2,1)S(1)} %bitcast.80, f32[2048,1024]{1,0:T(8,128)} %get-tuple-element.15, s32[1024]{0:T(1024)S(1)} %iota_add_fusion.1, s32[2048]{0:T(1024)S(1)} %iota_add_fusion), kind=kOutput, calls=%fused_computation.30 | convolution fusion | flops 4303355904 | bytes 18886656 | tf_op jit(solution)/shard_map/dot_general | solution.py:44
  343.3 40.5 %reduce-scatter.3.cloned.1.call-done = f32[64,2048]{1,0:T(8,128)} async-done(((f32[1024,2048]{1,0:T(8,128)}), f32[64,2048]{1,0:T(8,128)}) %reduce-scatter.3.cloned.1.call-update) | async-done | bytes 524304 | tf_op jit(solution)/shard_map/reduce_scatter | solution.py:43
  386.0 5.7 all-to-all-start.2
  391.7 94.6 %reduce-scatter.5.cloned.1.call-done = f32[64,2048]{1,0:T(8,128)} async-done(((f32[1024,2048]{1,0:T(8,128)}), f32[64,2048]{1,0:T(8,128)}) %reduce-scatter.5.cloned.1.call-update) | async-done | bytes 524304 | tf_op jit(solution)/shard_map/reduce_scatter | solution.py:43
  488.4 4.5 all-to-all-start.5
  496.9 8.7 %all-to-all-done.5 = f32[8,8,2048]{2,1,0:T(8,128)S(1)} async-done(((f32[8,8,2048]{2,1,0:T(8,128)}), f32[8,8,2048]{2,1,0:T(8,128)S(1)}, u32[]{:S(2)}, u32[]{:S(2)}) %all-to-all-start.5) | async-done | bytes 524320 | tf_op jit(solution)/shard_map/all_to_all | solution.py:90
  507.3 64.5 %all-reduce = (f32[]{:T(128)}, f32[]{:T(128)}, f32[]{:T(128)}) all-reduce(f32[]{:T(128)} %get-tuple-element.12, f32[]{:T(128)S(6)} %select_n.28, f32[]{:T(128)S(6)} %add.86), channel_id=1, replica_groups=mesh['row'=8,'col'=16] {'row','col'}, use_global_device_ids=true, to_apply=%region_9.10 | all-reduce | flops 3 | bytes 24 | tf_op jit(solution)/shard_map/psum | solution.py:95
  (60 shorter events, 40.9 us)
Async XLA Ops:
  7.2 45.0 %all-gather.7.cloned.1.call-start = ((), (), s32[]{:S(2)}) async-start(), calls=%async_computation.9 | async-start | bytes 4456448 | tf_op jit(solution)/shard_map/all_gather | solution.py:75
  7.9 143.0 %all-gather.5.cloned.1.call-start = ((), (), s32[]{:S(2)}) async-start(), calls=%async_computation.8 | async-start | bytes 2359296 | tf_op jit(solution)/shard_map/all_gather | solution.py:71
  21.8 172.5 %all-gather.11.cloned.1.call-start = ((), (), s32[]{:S(2)}) async-start(), calls=%async_computation.12 | async-start | bytes 4456448 | tf_op jit(solution)/shard_map/all_gather | solution.py:76
  22.5 36.0 %all-to-all-start.3 = ((bf16[8,16,1024]{2,0,1:T(8,128)(2,1)}), bf16[8,16,1024]{2,0,1:T(8,128)(2,1)S(1)}, u32[]{:S(2)}, u32[]{:S(2)}) async-start(bf16[8,16,1024]{2,0,1:T(8,128)(2,1)} %bitcast.78), calls=%async_computation.4 | async-start | bytes 524288 | tf_op jit(solution)/shard_map/all_to_all | solution.py:68
  58.6 0.7 copy-start.4
  59.3 97.5 %all-to-all-start.1 = ((bf16[128,8,2048]{0,2,1:T(8,128)(2,1)}), bf16[128,8,2048]{0,2,1:T(8,128)(2,1)}, u32[]{:S(2)}, u32[]{:S(2)}) async-start(bf16[128,8,2048]{0,2,1:T(8,128)(2,1)} %bitcast.74), calls=%async_computation.1 | async-start | bytes 8388608 | tf_op jit(solution)/shard_map/all_to_all | solution.py:79
  65.8 222.0 %all-gather.9.cloned.1.call-start = ((), (), s32[]{:S(2)}) async-start(), calls=%async_computation.11 | async-start | bytes 2359296 | tf_op jit(solution)/shard_map/all_gather | solution.py:72
  66.4 317.5 %reduce-scatter.3.cloned.1.call-start = ((), (), s32[]{:S(2)}) async-start(), calls=%async_computation.10 | async-start | bytes 8912896 | tf_op jit(solution)/shard_map/reduce_scatter | solution.py:43
  179.5 7.9 %copy-start.3 = (bf16[16,8,8,1024]{3,2,1,0:T(8,128)(2,1)S(1)}, bf16[16,8,8,1024]{3,2,1,0:T(8,128)(2,1)}, u32[]{:S(2)}) copy-start(bf16[16,8,8,1024]{3,2,1,0:T(8,128)(2,1)} %copy.13) | copy-start | bytes 6291460
  184.1 3.2 copy-start.5
  200.7 92.9 %all-to-all-start.4 = ((bf16[128,8,2048]{0,2,1:T(8,128)(2,1)}), bf16[128,8,2048]{0,2,1:T(8,128)(2,1)}, u32[]{:S(2)}, u32[]{:S(2)}) async-start(bf16[128,8,2048]{0,2,1:T(8,128)(2,1)} %bitcast.75), calls=%async_computation.5 | async-start | bytes 8388608 | tf_op jit(solution)/shard_map/all_to_all | solution.py:80
  205.3 281.0 %reduce-scatter.5.cloned.1.call-start = ((), (), s32[]{:S(2)}) async-start(), calls=%async_computation.13 | async-start | bytes 8912896 | tf_op jit(solution)/shard_map/reduce_scatter | solution.py:43
  308.7 7.8 %slice-start = ((s8[8388608]{0:T(1024)(128)(4,1)}), s8[4194304]{0:T(1024)(128)(4,1)S(1)}, s32[]{:S(2)}) async-start(s8[8388608]{0:T(1024)(128)(4,1)} %bitcast.86), calls=%async_computation.14 | async-start | bytes 8388608
  311.8 4.8 slice-start.1
  316.6 9.2 %copy-start.2 = (bf16[16,8,8,1024]{3,2,1,0:T(8,128)(2,1)S(1)}, bf16[16,8,8,1024]{3,2,1,0:T(8,128)(2,1)}, u32[]{:S(2)}) copy-start(bf16[16,8,8,1024]{3,2,1,0:T(8,128)(2,1)} %copy.17) | copy-start | bytes 6291460
  340.2 165.3 %copy-start = (bf16[8,16384]{1,0:T(8,128)(2,1)S(1)}, bf16[8,16384]{1,0:T(8,128)(2,1)}, u32[]{:S(2)}) copy-start(bf16[8,16384]{1,0:T(8,128)(2,1)} %param.3) | copy-start | bytes 786436
  340.2 165.3 %copy-start.1 = (bf16[8,16384]{1,0:T(8,128)(2,1)S(1)}, bf16[8,16384]{1,0:T(8,128)(2,1)}, u32[]{:S(2)}) copy-start(bf16[8,16384]{1,0:T(8,128)(2,1)} %param.2) | copy-start | bytes 786436
  386.0 102.4 %all-to-all-start.2 = ((f32[8,8,2048]{2,1,0:T(8,128)}), f32[8,8,2048]{2,1,0:T(8,128)S(1)}, u32[]{:S(2)}, u32[]{:S(2)}) async-start(f32[8,8,2048]{2,1,0:T(8,128)} %fusion.37), calls=%async_computation.3 | async-start | bytes 1048576 | tf_op jit(solution)/shard_map/all_to_all | solution.py:89
  488.4 17.1 %all-to-all-start.5 = ((f32[8,8,2048]{2,1,0:T(8,128)}), f32[8,8,2048]{2,1,0:T(8,128)S(1)}, u32[]{:S(2)}, u32[]{:S(2)}) async-start(f32[8,8,2048]{2,1,0:T(8,128)} %fusion.31), calls=%async_computation.7 | async-start | bytes 1048576 | tf_op jit(solution)/shard_map/all_to_all | solution.py:90
Sparse Core Ops, SparseCore 0:
  9.7 42.4 all-gather.6
  54.5 96.3 all-gather.4
  152.6 36.0 all-gather.10
  191.5 96.2 all-gather.8
  290.0 93.7 reduce-scatter.2
  386.1 100.1 reduce-scatter.4
where the time goes:
time: 584 us; the launch traced here: 582 us
  waiting for transfers between devices  339 us (58%)
  blocking collectives  78.3 us (13%)
  other arithmetic  49.1 us (8%)
  local copies, waits for them, and re-layouts  38.2 us (7%)
  matrix products  32.1 us (5%)
  starting transfers between devices  25.2 us (4%)
  between operations  20 us (3%)
    reduce_scatter x2, waiting for transfers between devices, feature_part(): lax.psum_scatter(lax.dot_general(permuted, tile_round, (((1,), (1,)), (()...  135 us
    all_gather x1, waiting for transfers between devices, body(): lax.all_gather(col_split_data[0], 'row', axis=0, tiled=True)  84.5 us
    all_gather x1, waiting for transfers between devices, body(): lax.all_gather(col_split_data[1], 'row', axis=0, tiled=True)  82.3 us
    psum x1, blocking collectives, body(): lax.psum((inv_local, hinge_local, cov_first + cov_second), ('row', 'col'))  64.5 us
    all_gather x1, waiting for transfers between devices, body(): lax.all_gather(view_one, 'col', axis=0, tiled=True)  26.1 us
    convert_element_type x2, local copies, waits for them, and re-layouts, center(): values = raw_block.astype(jnp.float32)  18.4 us
    dot_general x2, matrix products, feature_part(): lax.dot_general(permuted, tile_round, (((1,), (1,)), ((), ())), preferred...  18.2 us
    dot_general x2, matrix products, feature_part(): lax.dot_general(x_round, y_round, (((0,), (0,)), ((), ())), preferred_ele...  13.9 us
  transfers between devices with their start and end apart: 11, of which 6 were waited for; matrix products, arithmetic and copies ran while one was open for 20% of the time, Pallas kernels for 0%

commit v1 on v0

v1 whole, which is shorter than its diff:
```python
import jax
import jax.numpy as jnp
import numpy as np
from jax import lax
from jax.sharding import Mesh
from jax.sharding import PartitionSpec as P

epsilon = 0.0001
inv_weight = 25.0
var_weight = 25.0
cov_weight = 1.0
out_scale = 25.0

FINE = ("zh", "x", "y", "zl", "core")
SIZES = (2, 4, 4, 2, 2)
ROW_GROUP = ("x", "core")
FEATURE_GROUP = ("zh", "y", "zl")
SWAP = ((0, 1), (1, 0))
NEAR = ((0, 1), (1, 0), (2, 3), (3, 2))
FAR = ((0, 2), (2, 0), (1, 3), (3, 1))


def to_bf16(values):
    return lax.reduce_precision(values, 8, 7)


def gram_part(halves, first_row, group_rows, batch_rows):
    product = 0.0
    stats = []
    for raw in halves:
        values = raw.astype(jnp.float32)
        centered = values - jnp.sum(values, axis=0) / batch_rows
        spread = jnp.sqrt(jnp.sum(centered * centered, axis=0) / (batch_rows - 1) + epsilon)
        wide = to_bf16(centered)
        rounded = wide.astype(jnp.bfloat16)
        energy = jnp.sum(wide * wide, axis=0)
        mine = lax.dynamic_slice_in_dim(rounded, first_row, group_rows, 0)
        product = product + lax.dot_general(
            mine, rounded, (((1,), (1,)), ((), ())), preferred_element_type=jnp.float32
        )
        hinge = jnp.where(
            spread < 1.0,
            lax.dynamic_slice_in_dim(centered, first_row, group_rows, 0) / spread,
            0.0,
        )
        stats.append((rounded, mine, energy, spread, hinge))
    return product, stats


def body(view_one, view_two):
    shard_rows, feature_count = view_one.shape
    x_size, core_size = lax.axis_size("x"), lax.axis_size("core")
    feature_parts = lax.axis_size("zh") * lax.axis_size("y") * lax.axis_size("zl")
    row_parts = x_size * core_size
    device_count = row_parts * feature_parts
    batch_rows = shard_rows * device_count
    group_rows = batch_rows // row_parts
    half_width = feature_count // feature_parts // core_size
    core = lax.axis_index("core")
    first_row = (lax.axis_index("x") * core_size + core) * group_rows
    views = jnp.stack([view_one, view_two])

    blocks = views.reshape(2, shard_rows, feature_parts, core_size, half_width)
    blocks = blocks.transpose(3, 2, 0, 1, 4)
    blocks = jnp.broadcast_to(blocks[None], (x_size,) + blocks.shape)
    blocks = blocks.reshape(device_count, 2, shard_rows, half_width)
    own = lax.all_to_all(blocks, ROW_GROUP + FEATURE_GROUP, 0, 0, tiled=True)
    other = lax.ppermute(own, "core", SWAP)

    parts, stats, scalar = [], [], 0.0
    for v in range(2):
        halves = [a[:, v].reshape(batch_rows, half_width) for a in (own, other)]
        product, stat = gram_part(halves, first_row, group_rows, batch_rows)
        parts.append(product.astype(jnp.bfloat16).reshape(feature_parts, shard_rows, batch_rows))
        stats.append(stat)
        scalar += var_weight / feature_count * sum(
            jnp.sum(jnp.maximum(1.0 - s[3], 0.0)) for s in stat
        ) / row_parts
        scalar -= cov_weight / feature_count / (batch_rows - 1) ** 2 * sum(
            jnp.sum(s[2] * s[2]) for s in stat
        ) / row_parts

    pieces = lax.all_to_all(jnp.stack(parts, 1), FEATURE_GROUP, 0, 0, tiled=True)
    pieces = jnp.sum(pieces.astype(jnp.float32), axis=0)
    scalar += cov_weight / feature_count / (batch_rows - 1) ** 2 * jnp.sum(pieces * pieces)
    view_diff = view_one.astype(jnp.float32) - view_two.astype(jnp.float32)
    scalar += inv_weight / (batch_rows * feature_count) * jnp.sum(view_diff * view_diff)

    ids = lax.broadcasted_iota(jnp.int32, (shard_rows, batch_rows), 1)
    row_ids = lax.broadcasted_iota(jnp.int32, (shard_rows, batch_rows), 0)
    feature_idx = lax.axis_index(FEATURE_GROUP)
    on_diagonal = ids == first_row + feature_idx * shard_rows + row_ids
    sent = to_bf16(pieces)
    lost = jnp.sum(jnp.where(on_diagonal, pieces - sent, 0.0), axis=2, keepdims=True)
    high = to_bf16(scalar)
    middle = to_bf16(scalar - high)
    low = scalar - high - middle
    lanes = lax.broadcasted_iota(jnp.int32, (2, shard_rows, 128), 2)
    extra = jnp.where(lanes == 0, lost, 0.0)
    for lane, value in ((1, high), (2, middle), (3, low)):
        extra = jnp.where(lanes == lane, value, extra)
    sent = jnp.concatenate([sent, extra], axis=2).astype(jnp.bfloat16)
    gram = jnp.broadcast_to(sent[None], (feature_parts,) + sent.shape)
    gram = lax.all_to_all(gram, FEATURE_GROUP, 0, 0, tiled=True)
    total_loss = jnp.sum(gram[:, 0, 0, batch_rows + 1 : batch_rows + 4].astype(jnp.float32))
    for axis, pairs in (("core", SWAP), ("x", NEAR), ("x", FAR)):
        total_loss = total_loss + lax.ppermute(total_loss, axis, pairs)

    factor_cov = 4.0 * cov_weight * batch_rows / (batch_rows - 1)
    factor_var = var_weight * batch_rows / (batch_rows - 1)
    grads = []
    for v in range(2):
        rows = gram[:, v, :, :batch_rows].reshape(group_rows, batch_rows)
        lost = gram[:, v, :, batch_rows].reshape(group_rows, 1).astype(jnp.float32)
        for rounded, mine, energy, spread, hinge in stats[v]:
            product = lax.dot_general(
                rows, rounded, (((1,), (0,)), ((), ())), preferred_element_type=jnp.float32
            )
            product = (product - mine.astype(jnp.float32) * (energy - lost)) / (batch_rows - 1)
            grad = (factor_cov * product - factor_var * hinge) / out_scale
            grads.append(grad.astype(jnp.bfloat16).reshape(feature_parts, shard_rows, half_width))
    grads = jnp.stack(grads, 1)
    grads = lax.all_to_all(grads, FEATURE_GROUP, 0, 0, tiled=True)
    grads = grads.reshape(feature_parts, 2, core_size, shard_rows, half_width).astype(jnp.float32)
    grads = jnp.where(core == 0, grads, grads[:, :, ::-1])
    grads = grads.transpose(1, 3, 0, 2, 4).reshape(2, shard_rows, feature_count)
    push = 2.0 * inv_weight / out_scale * view_diff
    return grads[0] + push, grads[1] - push, total_loss


def solution(mesh):
    fine = Mesh(np.asarray(mesh.devices).reshape(SIZES), FINE)
    rows = P(FINE, None)
    return jax.shard_map(
        body, mesh=fine, in_specs=(rows, rows), out_specs=(rows, rows, P()), check_vma=False
    )
```

time: 584 us -> 126 us (0.22)
  waiting for transfers between devices: 339 us -> 47.4 us
  blocking collectives: 78.3 us -> 0 us
  local copies, waits for them, and re-layouts: 38.2 us -> 4.24 us
  other arithmetic: 49.1 us -> 22.4 us
  matrix products: 32.1 us -> 8.05 us
  between operations: 20 us -> 13.4 us
    all_gather x4 -> x0, waiting for transfers between devices: 193 us -> none  [the longest x1 84.5 us: body(): lax.all_gather(col_split_data[0], 'row', axis=0, tiled=True)]
    reduce_scatter x2 -> x0, waiting for transfers between devices: 135 us -> none  [feature_part(): lax.psum_scatter(lax.dot_general(permuted, tile_round, (((1,), (1,)), (()...]
    psum x1 -> x0, blocking collectives: 64.5 us -> none  [body(): lax.psum((inv_local, hinge_local, cov_first + cov_second), ('row', 'col'))]
    all_to_all x5 -> x4, waiting for transfers between devices: 8.68 us -> 43.3 us  [the longest x1 27.8 us: body(): own = lax.all_to_all(blocks, ROW_GROUP + FEATURE_GROUP, 0, 0, tiled=True)]
    dot_general x4 -> x8, matrix products: 32.1 us -> 8.05 us  [the longest x4 6.17 us: body(): lax.dot_general(rows, rounded, (((1,), (0,)), ((), ())), preferred_elemen...]
    convert_element_type x4 -> x2, other arithmetic: 21.3 us -> 1 us  [the longest x1 0.88 us: body(): lost = gram[:, v, :, batch_rows].reshape(group_rows, 1).astype(jnp.float32)]
    convert_element_type x2, local copies, waits for them, and re-layouts: 18.4 us -> 0.17 us  [body(): lost = gram[:, v, :, batch_rows].reshape(group_rows, 1).astype(jnp.float32)]
    reduce_sum x11 -> x10, other arithmetic: 23.5 us -> 7.86 us  [the longest x4 3.5 us: gram_part(): energy = jnp.sum(wide * wide, axis=0)]
  transfers between devices with their start and end apart: 11 -> 8, of which waited for: 6 -> 6; matrix products, arithmetic and copies ran while one was open for 20% -> 9% of each run, Pallas kernels for 0% -> 0%
where the time goes in v1:
time: 126 us; the launch traced here: 125 us
  waiting for transfers between devices  47.4 us (38%)
  starting transfers between devices  29.6 us (23%)
  other arithmetic  22.4 us (18%)
  between operations  13.4 us (11%)
  matrix products  8.05 us (6%)
  local copies, waits for them, and re-layouts  4.24 us (3%)
    all_to_all x1, waiting for transfers between devices, body(): own = lax.all_to_all(blocks, ROW_GROUP + FEATURE_GROUP, 0, 0, tiled=True)  27.8 us
    all_to_all x1, waiting for transfers between devices, body(): gram = lax.all_to_all(gram, FEATURE_GROUP, 0, 0, tiled=True)  11.5 us
    all_to_all x1, starting transfers between devices, body(): own = lax.all_to_all(blocks, ROW_GROUP + FEATURE_GROUP, 0, 0, tiled=True)  11.1 us
    dot_general x4, matrix products, body(): lax.dot_general(rows, rounded, (((1,), (0,)), ((), ())), preferred_elemen...  6.17 us
    ppermute x3, starting transfers between devices, body(): total_loss = total_loss + lax.ppermute(total_loss, axis, pairs)  5.81 us
    sub x2, other arithmetic, gram_part(): centered = values - jnp.sum(values, axis=0) / batch_rows  5.42 us
    all_to_all x1, starting transfers between devices, body(): gram = lax.all_to_all(gram, FEATURE_GROUP, 0, 0, tiled=True)  4.25 us
    all_to_all x1, starting transfers between devices, body(): lax.all_to_all(jnp.stack(parts, 1), FEATURE_GROUP, 0, 0, tiled=True)  4.24 us
  transfers between devices with their start and end apart: 8, of which 6 were waited for; matrix products, arithmetic and copies ran while one was open for 9% of the time, Pallas kernels for 0%

profile of v1, /device:TPU:0, one launch (start us, length us, event | category | flops | bytes accessed | tf_op | source)
XLA Modules:
  0.0 125.0 jit_solution(14362957125862981063)
XLA Ops:
  0.6 1.1 maximum_bitcast_fusion
  1.8 1.6 %broadcast_in_dim.75 = bf16[4,2,16,2,8,512]{5,4,3,2,1,0:T(8,128)(2,1)} broadcast(bf16[2,16,2,8,512]{4,3,2,1,0:T(8,128)(2,1)S(1)} %copy.11), dimensions={1,2,3,4,5} | broadcast | bytes 2621440 | tf_op jit(solution)/shard_map/broadcast_in_dim | solution.py:65
  3.4 11.1 %all-to-all-start = ((bf16[128,2,8,512]{3,2,1,0:T(8,128)(2,1)}), bf16[128,2,8,512]{3,2,1,0:T(8,128)(2,1)S(1)}, u32[]{:S(2)}, u32[]{:S(2)}) async-start(bf16[128,2,8,512]{3,2,1,0:T(8,128)(2,1)} %bitcast.87), calls=%async_computation | async-start | bytes 4194304 | tf_op jit(solution)/shard_map/all_to_all | solution.py:67
  16.1 27.8 %all-to-all-done = bf16[128,2,8,512]{3,2,1,0:T(8,128)(2,1)S(1)} async-done(((bf16[128,2,8,512]{3,2,1,0:T(8,128)(2,1)}), bf16[128,2,8,512]{3,2,1,0:T(8,128)(2,1)S(1)}, u32[]{:S(2)}, u32[]{:S(2)}) %all-to-all-start) | async-done | bytes 2097184 | tf_op jit(solution)/shard_map/all_to_all | solution.py:67
  47.2 2.7 %fusion.24 = (f32[1024,512]{1,0:T(8,128)}, bf16[1024,512]{1,0:T(8,128)(2,1)S(1)}, bf16[1024,512]{1,0:T(8,128)(2,1)S(1)}, f32[1024,512]{1,0:T(8,128)}) fusion(f32[512]{0:T(512)S(1)} %broadcast_multiply_fusion.3, bf16[128,2,8,512]{3,2,1,0:T(8,128)(2,1)S(1)} %all-to-all-done, f32[512]{0:T(512)S(1)} %broadcast_multiply_fusion.1), kind=kLoop, calls=%fused_computation.36 | loop fusion | flops 4194304 | bytes 8392704 | tf_op jit(solution)/shard_map/sub | solution.py:32
  51.8 2.7 %fusion.25 = (f32[1024,512]{1,0:T(8,128)}, bf16[1024,512]{1,0:T(8,128)(2,1)S(1)}, f32[1024,512]{1,0:T(8,128)}, bf16[1024,512]{1,0:T(8,128)(2,1)S(1)}) fusion(f32[512]{0:T(512)S(1)} %broadcast_multiply_fusion.2, bf16[128,2,8,512]{3,2,1,0:T(8,128)(2,1)S(1)} %collective-permute-done, f32[512]{0:T(512)S(1)} %broadcast_multiply_fusion), kind=kLoop, calls=%fused_computation.37 | loop fusion | flops 4194304 | bytes 8392704 | tf_op jit(solution)/shard_map/sub | solution.py:32
  56.8 4.2 %all-to-all-start.1 = ((bf16[16,2,8,1024]{3,2,1,0:T(8,128)(2,1)}), bf16[16,2,8,1024]{3,2,1,0:T(8,128)(2,1)}, u32[]{:S(2)}, u32[]{:S(2)}) async-start(bf16[16,2,8,1024]{3,2,1,0:T(8,128)(2,1)} %pad_maximum_fusion), calls=%async_computation.1 | async-start | bytes 1048576 | tf_op jit(solution)/shard_map/all_to_all | solution.py:83
  62.9 1.7 %fusion.17 = (f32[512]{0:T(512)S(1)}, f32[512]{0:T(512)S(1)}) fusion(f32[512]{0:T(512)S(1)} %broadcast_multiply_fusion.2, bf16[128,2,8,512]{3,2,1,0:T(8,128)(2,1)} %copy-done), kind=kLoop, calls=%fused_computation.29 | loop fusion | flops 3668992 | bytes 1054720 | tf_op jit(solution)/shard_map/reduce_sum | solution.py:36
  69.1 3.9 %all-to-all-done.1 = bf16[16,2,8,1024]{3,2,1,0:T(8,128)(2,1)} async-done(((bf16[16,2,8,1024]{3,2,1,0:T(8,128)(2,1)}), bf16[16,2,8,1024]{3,2,1,0:T(8,128)(2,1)}, u32[]{:S(2)}, u32[]{:S(2)}) %all-to-all-start.1) | async-done | bytes 524320 | tf_op jit(solution)/shard_map/all_to_all | solution.py:83
  73.0 1.1 convert_reduce_fusion.4
  77.7 1.4 %select_convert_fusion = bf16[2,8,128]{2,1,0:T(8,128)(2,1)S(1)} fusion(bf16[2,8]{1,0:T(2,128)(2,1)S(1)} %get-tuple-element.16, f32[]{:T(128)} %reduce_precision.48, f32[]{:T(128)} %reduce_precision.49, bf16[]{:T(256)S(6)} %sub.190, pred[128]{0:T(512)(128)(4,1)S(1)} %get-tuple-element.46, pred[128]{0:T(512)(128)(4,1)S(1)} %get-tuple-element.47, ...), kind=kLoop, calls=%fused_computation.116 | loop fusion | flops 8192 | bytes 4650 | tf_op jit(solution)/shard_map/convert.8
  79.9 4.2 %all-to-all-start.2 = ((bf16[16,2,8,1152]{3,2,1,0:T(8,128)(2,1)}), bf16[16,2,8,1152]{3,2,1,0:T(8,128)(2,1)}, u32[]{:S(2)}, u32[]{:S(2)}) async-start(bf16[16,2,8,1152]{3,2,1,0:T(8,128)(2,1)} %broadcast_in_dim.83), calls=%async_computation.2 | async-start | bytes 1179648 | tf_op jit(solution)/shard_map/all_to_all | solution.py:104
  84.2 11.5 %all-to-all-done.2 = bf16[16,2,8,1152]{3,2,1,0:T(8,128)(2,1)} async-done(((bf16[16,2,8,1152]{3,2,1,0:T(8,128)(2,1)}), bf16[16,2,8,1152]{3,2,1,0:T(8,128)(2,1)}, u32[]{:S(2)}, u32[]{:S(2)}) %all-to-all-start.2) | async-done | bytes 589856 | tf_op jit(solution)/shard_map/all_to_all | solution.py:104
  96.8 1.8 %fusion.50 = bf16[16,1,8,512]{3,2,1,0:T(8,128)(2,1)S(1)} fusion(f32[512]{0:T(512)S(1)} %broadcast_multiply_fusion.2, bf16[128,2,8,512]{3,2,1,0:T(8,128)(2,1)} %copy-done, f32[1024,512]{1,0:T(8,128)} %get-tuple-element.19, s32[]{:T(128)S(6)} %select_n.58, bf16[16,2,8,1152]{3,2,1,0:T(8,128)(2,1)} %all-to-all-done.2, f32[512]{0:T(512)S(1)} %get-tuple-element.36, ...), kind=kOutput, calls=%fused_computation.73 | convolution fusion | flops 137035776 | bytes 1842180 | tf_op jit(solution)/shard_map/dot_general | solution.py:116
  98.6 1.6 %fusion.51 = bf16[16,1,8,512]{3,2,1,0:T(8,128)(2,1)S(1)} fusion(f32[512]{0:T(512)S(1)} %broadcast_multiply_fusion.3, bf16[128,2,8,512]{3,2,1,0:T(8,128)(2,1)S(1)} %all-to-all-done, f32[1024,512]{1,0:T(8,128)} %get-tuple-element.17, s32[]{:T(128)S(6)} %select_n.58, bf16[16,2,8,1152]{3,2,1,0:T(8,128)(2,1)} %all-to-all-done.2, f32[512]{0:T(512)S(1)} %get-tuple-element.34, ...), kind=kOutput, calls=%fused_computation.74 | convolution fusion | flops 137035776 | bytes 1842180 | tf_op jit(solution)/shard_map/dot_general | solution.py:116
  100.4 1.4 %fusion.48 = bf16[16,1,8,512]{3,2,1,0:T(8,128)(2,1)S(1)} fusion(f32[512]{0:T(512)S(1)} %broadcast_multiply_fusion, bf16[128,2,8,512]{3,2,1,0:T(8,128)(2,1)S(1)} %copy-done.1, f32[1024,512]{1,0:T(8,128)} %get-tuple-element.27, s32[]{:T(128)S(6)} %select_n.58, bf16[16,2,8,1152]{3,2,1,0:T(8,128)(2,1)} %all-to-all-done.2, f32[512]{0:T(512)S(1)} %get-tuple-element.40, ...), kind=kOutput, calls=%fused_computation.71 | convolution fusion | flops 137035776 | bytes 1842180 | tf_op jit(solution)/shard_map/dot_general | solution.py:116
  101.8 1.4 %fusion.49 = bf16[16,1,8,512]{3,2,1,0:T(8,128)(2,1)S(1)} fusion(f32[512]{0:T(512)S(1)} %broadcast_multiply_fusion.1, bf16[128,2,8,512]{3,2,1,0:T(8,128)(2,1)S(1)} %all-to-all-done, f32[1024,512]{1,0:T(8,128)} %get-tuple-element.26, s32[]{:T(128)S(6)} %select_n.58, bf16[16,2,8,1152]{3,2,1,0:T(8,128)(2,1)} %all-to-all-done.2, f32[512]{0:T(512)S(1)} %get-tuple-element.38, ...), kind=kOutput, calls=%fused_computation.72 | convolution fusion | flops 137035776 | bytes 1842180 | tf_op jit(solution)/shard_map/dot_general | solution.py:116
  104.1 3.6 %all-to-all-start.3 = ((bf16[16,4,8,512]{3,2,1,0:T(8,128)(2,1)}), bf16[16,4,8,512]{3,2,1,0:T(8,128)(2,1)S(1)}, u32[]{:S(2)}, u32[]{:S(2)}) async-start(bf16[16,4,8,512]{3,2,1,0:T(8,128)(2,1)} %pad_maximum_fusion.1), calls=%async_computation.3 | async-start | bytes 1048576 | tf_op jit(solution)/shard_map/all_to_all | solution.py:123
  107.7 1.5 %fusion.80 = f32[]{:T(128)} fusion(bf16[16,2,8,1152]{3,2,1,0:T(8,128)(2,1)} %all-to-all-done.2), kind=kLoop, calls=%fused_computation.115 | loop fusion | flops 95 | bytes 100 | tf_op jit(solution)/shard_map/reduce_sum | solution.py:105
  109.1 1.2 collective-permute-done.1
  111.7 2.3 %collective-permute-start.2 = (f32[]{:T(128)}, f32[]{:T(128)}, u32[]{:S(2)}, u32[]{:S(2)}) collective-permute-start(f32[]{:T(128)} %add.117), channel_id=1, source_target_pairs={{0,16},{16,0},{32,48},{48,32},{1,17},{17,1},{33,49},{49,33},{2,18}... | collective-permute-start | bytes 20 | tf_op jit(solution)/shard_map/ppermute | solution.py:107
  114.0 1.2 collective-permute-done.2
  116.0 3.5 %collective-permute-start.3 = (f32[]{:T(128)}, f32[]{:T(128)}, u32[]{:S(2)}, u32[]{:S(2)}) collective-permute-start(f32[]{:T(128)} %add.118), channel_id=1, source_target_pairs={{0,32},{32,0},{16,48},{48,16},{1,33},{33,1},{17,49},{49,17},{2,34}... | collective-permute-start | bytes 20 | tf_op jit(solution)/shard_map/ppermute | solution.py:107
  119.4 1.6 %collective-permute-done.3 = f32[]{:T(128)} collective-permute-done((f32[]{:T(128)}, f32[]{:T(128)}, u32[]{:S(2)}, u32[]{:S(2)}) %collective-permute-start.3) | collective-permute-done | bytes 36 | tf_op jit(solution)/shard_map/ppermute | solution.py:107
  (59 shorter events, 15.3 us)
Async XLA Ops:
  3.4 11.2 %copy-start.5 = (bf16[8,16384]{1,0:T(8,128)(2,1)S(1)}, bf16[8,16384]{1,0:T(8,128)(2,1)}, u32[]{:S(2)}) copy-start(bf16[8,16384]{1,0:T(8,128)(2,1)} %param.3) | copy-start | bytes 786436
  3.4 11.2 %copy-start.6 = (bf16[8,16384]{1,0:T(8,128)(2,1)S(1)}, bf16[8,16384]{1,0:T(8,128)(2,1)}, u32[]{:S(2)}) copy-start(bf16[8,16384]{1,0:T(8,128)(2,1)} %param.2) | copy-start | bytes 786436
  3.4 40.5 %all-to-all-start = ((bf16[128,2,8,512]{3,2,1,0:T(8,128)(2,1)}), bf16[128,2,8,512]{3,2,1,0:T(8,128)(2,1)S(1)}, u32[]{:S(2)}, u32[]{:S(2)}) async-start(bf16[128,2,8,512]{3,2,1,0:T(8,128)(2,1)} %bitcast.87), calls=%async_computation | async-start | bytes 4194304 | tf_op jit(solution)/shard_map/all_to_all | solution.py:67
  44.2 6.7 %collective-permute-start = (bf16[128,2,8,512]{3,2,1,0:T(8,128)(2,1)S(1)}, bf16[128,2,8,512]{3,2,1,0:T(8,128)(2,1)S(1)}, u32[]{:S(2)}, u32[]{:S(2)}) collective-permute-start(bf16[128,2,8,512]{3,2,1,0:T(8,128)(2,1)S(1)} %all-to-all-done), channel_id=1, source_target_pairs={{0,1},{1,0},{2,3},{3,2},{4,5},{5,4},{6,7},{7,6},{8,9},{9,8},{10,11... | collective-permute-start | bytes 6291464 | tf_op jit(solution)/shard_map/ppermute | solution.py:68
  49.9 1.2 copy-start.2
  50.9 3.6 %copy-start = (bf16[128,2,8,512]{3,2,1,0:T(8,128)(2,1)}, bf16[128,2,8,512]{3,2,1,0:T(8,128)(2,1)S(1)}, u32[]{:S(2)}) copy-start(bf16[128,2,8,512]{3,2,1,0:T(8,128)(2,1)S(1)} %collective-permute-done) | copy-start | bytes 6291460
  54.5 1.0 copy-start.3
  54.5 1.4 %copy-start.4 = (bf16[1024,512]{1,0:T(8,128)(2,1)}, bf16[1024,512]{1,0:T(8,128)(2,1)S(1)}, u32[]{:S(2)}) copy-start(bf16[1024,512]{1,0:T(8,128)(2,1)S(1)} %get-tuple-element.20) | copy-start | bytes 3145732
  56.8 16.2 %all-to-all-start.1 = ((bf16[16,2,8,1024]{3,2,1,0:T(8,128)(2,1)}), bf16[16,2,8,1024]{3,2,1,0:T(8,128)(2,1)}, u32[]{:S(2)}, u32[]{:S(2)}) async-start(bf16[16,2,8,1024]{3,2,1,0:T(8,128)(2,1)} %pad_maximum_fusion), calls=%async_computation.1 | async-start | bytes 1048576 | tf_op jit(solution)/shard_map/all_to_all | solution.py:83
  79.9 15.8 %all-to-all-start.2 = ((bf16[16,2,8,1152]{3,2,1,0:T(8,128)(2,1)}), bf16[16,2,8,1152]{3,2,1,0:T(8,128)(2,1)}, u32[]{:S(2)}, u32[]{:S(2)}) async-start(bf16[16,2,8,1152]{3,2,1,0:T(8,128)(2,1)} %broadcast_in_dim.83), calls=%async_computation.2 | async-start | bytes 1179648 | tf_op jit(solution)/shard_map/all_to_all | solution.py:104
  98.6 1.8 %copy-start.1 = (bf16[128,2,8,512]{3,2,1,0:T(8,128)(2,1)S(1)}, bf16[128,2,8,512]{3,2,1,0:T(8,128)(2,1)}, u32[]{:S(2)}) copy-start(bf16[128,2,8,512]{3,2,1,0:T(8,128)(2,1)} %copy-done) | copy-start | bytes 6291460
  104.1 17.7 %all-to-all-start.3 = ((bf16[16,4,8,512]{3,2,1,0:T(8,128)(2,1)}), bf16[16,4,8,512]{3,2,1,0:T(8,128)(2,1)S(1)}, u32[]{:S(2)}, u32[]{:S(2)}) async-start(bf16[16,4,8,512]{3,2,1,0:T(8,128)(2,1)} %pad_maximum_fusion.1), calls=%async_computation.3 | async-start | bytes 1048576 | tf_op jit(solution)/shard_map/all_to_all | solution.py:123
  109.1 1.2 collective-permute-start.1
  111.7 3.6 %collective-permute-start.2 = (f32[]{:T(128)}, f32[]{:T(128)}, u32[]{:S(2)}, u32[]{:S(2)}) collective-permute-start(f32[]{:T(128)} %add.117), channel_id=1, source_target_pairs={{0,16},{16,0},{32,48},{48,32},{1,17},{17,1},{33,49},{49,33},{2,18}... | collective-permute-start | bytes 20 | tf_op jit(solution)/shard_map/ppermute | solution.py:107
  116.0 5.1 %collective-permute-start.3 = (f32[]{:T(128)}, f32[]{:T(128)}, u32[]{:S(2)}, u32[]{:S(2)}) collective-permute-start(f32[]{:T(128)} %add.118), channel_id=1, source_target_pairs={{0,32},{32,0},{16,48},{48,16},{1,33},{33,1},{17,49},{49,17},{2,34}... | collective-permute-start | bytes 20 | tf_op jit(solution)/shard_map/ppermute | solution.py:107
  121.9 1.0 copy-start.7

commit v2 on v1

v2 whole, which is shorter than its diff:
```python
import functools

import jax
import jax.numpy as jnp
import numpy as np
from jax import lax
from jax.experimental import pallas as pl
from jax.experimental.pallas import tpu as pltpu
from jax.sharding import Mesh
from jax.sharding import PartitionSpec as P

epsilon = 0.0001
inv_weight = 25.0
var_weight = 25.0
cov_weight = 1.0
out_scale = 25.0

FINE = ("zh", "x", "y", "zl", "core")
SIZES = (2, 4, 4, 2, 2)
FEATURE_GROUP = ("zh", "y", "zl")
CHIPS = ("x",) + FEATURE_GROUP
SWAP = ((0, 1), (1, 0))
NEAR = ((0, 1), (1, 0), (2, 3), (3, 2))
FAR = ((0, 2), (2, 0), (1, 3), (3, 1))
LANES = 128
VMEM_BYTES = 48 * 1024 * 1024
CONTRACT_LAST = (((1,), (1,)), ((), ()))
CONTRACT_FIRST = (((1,), (0,)), ((), ()))


def of_view(block, v):
    devices, rows, width = block.shape
    half = rows // 2
    return block[:, v * half : (v + 1) * half].reshape(devices * half, width)


def both_views(first, second, devices):
    shape = (devices, first.shape[0] // devices, first.shape[1])
    return jnp.concatenate([first.reshape(shape), second.reshape(shape)], axis=1)


def gram_kernel(sizes, place, own, other, rounded, part, rest, share, total):
    batch_rows, feature_count, feature_parts, row_parts = sizes
    group_rows = batch_rows // row_parts
    step = pl.program_id(0)
    first_row = pl.multiple_of(place[0] * group_rows, group_rows)
    first_device = place[0] * feature_parts
    factor_cov = 4.0 * cov_weight * batch_rows / (batch_rows - 1) ** 2 / out_scale
    factor_var = var_weight * batch_rows / (batch_rows - 1) / out_scale
    half = batch_rows // 2
    shares = 0.0
    products = []
    for v in range(2):
        a = of_view(own[...].astype(jnp.float32), v)
        b = of_view(other[...].astype(jnp.float32), v)
        mean = (jnp.sum(a, axis=0, keepdims=True) + jnp.sum(b, axis=0, keepdims=True)) / batch_rows
        a = a - mean
        b = b - mean
        square = jnp.sum(a * a, axis=0, keepdims=True) + jnp.sum(b * b, axis=0, keepdims=True)
        spread = jnp.sqrt(square / (batch_rows - 1) + epsilon)
        a = a.astype(jnp.bfloat16)
        b = b.astype(jnp.bfloat16)
        rounded[v, :half] = a
        rounded[v, half:] = b
        a = a.astype(jnp.float32)
        b = b.astype(jnp.float32)
        energy = jnp.sum(a * a, axis=0, keepdims=True) + jnp.sum(b * b, axis=0, keepdims=True)
        mine = rounded[v, pl.ds(first_row, group_rows)]
        products.append(
            lax.dot_general(mine, rounded[v], CONTRACT_LAST, preferred_element_type=jnp.float32)
        )
        centered = of_view(own[pl.ds(first_device, feature_parts)].astype(jnp.float32), v) - mean
        hinge = jnp.where(spread < 1.0, centered / spread, 0.0)
        rest[v] = -factor_var * hinge - factor_cov * (mine.astype(jnp.float32) * energy)
        shares += var_weight / feature_count / row_parts * jnp.maximum(1.0 - spread, 0.0)
        shares -= cov_weight / feature_count / row_parts * (energy / (batch_rows - 1)) ** 2
    share[...] = shares

    @pl.when(step == 0)
    def _():
        for v in range(2):
            total[v] = products[v]

    @pl.when(step > 0)
    def _():
        for v in range(2):
            total[v] += products[v]

    @pl.when(step == pl.num_programs(0) - 1)
    def _():
        part[...] = both_views(total[0], total[1], feature_parts).astype(jnp.bfloat16)


def sum_kernel(sizes, place, inv, pieces, share, sent, scalar):
    batch_rows, feature_count, feature_parts, row_parts = sizes
    rows = pieces.shape[1] // 2
    summed = jnp.sum(pieces[...].astype(jnp.float32), axis=0)
    shape = summed.shape
    lane = lax.broadcasted_iota(jnp.int32, shape, 1)
    row = lax.broadcasted_iota(jnp.int32, shape, 0)
    diagonal = (place[0] * feature_parts + place[1]) * rows + row % rows
    short = summed.astype(jnp.bfloat16).astype(jnp.float32)
    lost = jnp.sum(jnp.where(lane == diagonal, summed - short, 0.0), axis=1, keepdims=True)
    extra = jnp.broadcast_to(lost, (shape[0], LANES))
    out = jnp.concatenate([short, extra], axis=1).astype(jnp.bfloat16)
    sent[...] = jnp.broadcast_to(out[None], sent.shape)
    factor = cov_weight / feature_count / (batch_rows - 1) ** 2
    value = factor * jnp.sum(summed * summed) + jnp.sum(share[...]) + inv[0]
    scalar[...] = jnp.full(scalar.shape, value, jnp.float32)


def grad_kernel(sizes, place, scalar, gram, rounded, rest, sent, whole):
    batch_rows, feature_count, feature_parts, row_parts = sizes
    group_rows = batch_rows // row_parts
    step = pl.program_id(0)
    width = rounded.shape[2]
    factor_cov = 4.0 * cov_weight * batch_rows / (batch_rows - 1) ** 2 / out_scale
    first_row = pl.multiple_of(place[0] * group_rows, group_rows)
    wide = gram[...].astype(jnp.float32)
    grads = []
    for v in range(2):
        rows = of_view(wide, v)
        lost = rows[:, batch_rows : batch_rows + 1]
        rows = rows[:, :batch_rows].astype(jnp.bfloat16)
        product = lax.dot_general(
            rows, rounded[v], CONTRACT_FIRST, preferred_element_type=jnp.float32
        )
        mine = rounded[v, pl.ds(first_row, group_rows)].astype(jnp.float32)
        grads.append(factor_cov * (product + lost * mine) + rest[v])
    place_out = pl.multiple_of(step * width, width)
    block = both_views(grads[0], grads[1], feature_parts).astype(jnp.bfloat16)
    sent[:, :, pl.ds(place_out, width)] = block

    @pl.when(step == 0)
    def _():
        shape = (whole.shape[1], LANES)
        value = jnp.full(shape, scalar[0], jnp.float32)
        high = value.astype(jnp.bfloat16).astype(jnp.float32)
        middle = (value - high).astype(jnp.bfloat16).astype(jnp.float32)
        low = value - high - middle
        lane = lax.broadcasted_iota(jnp.int32, shape, 1)
        parts = jnp.where(lane == 0, high, jnp.where(lane == 1, middle, low)).astype(jnp.bfloat16)
        whole[...] = jnp.broadcast_to(parts[None], whole.shape)


def body(view_one, view_two):
    shard_rows, feature_count = view_one.shape
    x_size, core_size = lax.axis_size("x"), lax.axis_size("core")
    feature_parts = lax.axis_size("zh") * lax.axis_size("y") * lax.axis_size("zl")
    row_parts = x_size * core_size
    chips = x_size * feature_parts
    batch_rows = shard_rows * row_parts * feature_parts
    group_rows = batch_rows // row_parts
    width = feature_count // feature_parts
    steps = 4
    chunk = width // steps
    sizes = (batch_rows, feature_count, feature_parts, row_parts)
    place = jnp.stack([lax.axis_index("x"), lax.axis_index(FEATURE_GROUP)]).astype(jnp.int32)
    params = pltpu.CompilerParams(vmem_limit_bytes=VMEM_BYTES)
    both = 2 * shard_rows

    blocks = jnp.concatenate([view_one, view_two]).reshape(both, feature_parts, width)
    blocks = blocks.transpose(1, 0, 2)
    blocks = jnp.broadcast_to(blocks[None], (x_size,) + blocks.shape).reshape(chips, both, width)
    own = lax.all_to_all(blocks, CHIPS, 0, 0, tiled=True)
    other = lax.ppermute(own, "core", SWAP)
    view_diff = view_one.astype(jnp.float32) - view_two.astype(jnp.float32)
    inv = inv_weight / (batch_rows * feature_count) * jnp.sum(view_diff * view_diff)

    rounded, part, rest, share = pl.pallas_call(
        functools.partial(gram_kernel, sizes),
        grid_spec=pltpu.PrefetchScalarGridSpec(
            num_scalar_prefetch=1,
            grid=(steps,),
            in_specs=[
                pl.BlockSpec((chips, both, chunk), lambda f, place: (0, 0, f)),
                pl.BlockSpec((chips, both, chunk), lambda f, place: (0, 0, f)),
            ],
            out_specs=[
                pl.BlockSpec((2, batch_rows, chunk), lambda f, place: (0, 0, f)),
                pl.BlockSpec((feature_parts, both, batch_rows), lambda f, place: (0, 0, 0)),
                pl.BlockSpec((2, group_rows, chunk), lambda f, place: (0, 0, f)),
                pl.BlockSpec((1, chunk), lambda f, place: (0, f)),
            ],
            scratch_shapes=[pltpu.VMEM((2, group_rows, batch_rows), jnp.float32)],
        ),
        out_shape=[
            jax.ShapeDtypeStruct((2, batch_rows, width), jnp.bfloat16),
            jax.ShapeDtypeStruct((feature_parts, both, batch_rows), jnp.bfloat16),
            jax.ShapeDtypeStruct((2, group_rows, width), jnp.float32),
            jax.ShapeDtypeStruct((1, width), jnp.float32),
        ],
        compiler_params=params,
        name="gram_part",
    )(place, own, other)

    pieces = lax.all_to_all(part, FEATURE_GROUP, 0, 0, tiled=True)
    smem = pl.BlockSpec(memory_space=pltpu.SMEM)
    vmem = pl.BlockSpec(memory_space=pltpu.VMEM)
    sent, scalar = pl.pallas_call(
        functools.partial(sum_kernel, sizes),
        in_specs=[smem, smem, vmem, vmem],
        out_specs=[vmem, vmem],
        out_shape=[
            jax.ShapeDtypeStruct((feature_parts, both, batch_rows + LANES), jnp.bfloat16),
            jax.ShapeDtypeStruct((8, LANES), jnp.float32),
        ],
        compiler_params=params,
        name="gram_sum",
    )(place, inv.reshape(1), pieces, share)

    gram = lax.all_to_all(sent, FEATURE_GROUP, 0, 0, tiled=True)
    for axis, pairs in (("core", SWAP), ("x", NEAR), ("x", FAR)):
        scalar = scalar + lax.ppermute(scalar, axis, pairs)

    grads, whole = pl.pallas_call(
        functools.partial(grad_kernel, sizes),
        grid_spec=pltpu.PrefetchScalarGridSpec(
            num_scalar_prefetch=2,
            grid=(steps,),
            in_specs=[
                pl.BlockSpec(sent.shape, lambda f, place, scalar: (0, 0, 0)),
                pl.BlockSpec((2, batch_rows, chunk), lambda f, place, scalar: (0, 0, f)),
                pl.BlockSpec((2, group_rows, chunk), lambda f, place, scalar: (0, 0, f)),
            ],
            out_specs=[
                pl.BlockSpec((feature_parts, both, width), lambda f, place, scalar: (0, 0, 0)),
                pl.BlockSpec((feature_parts, both, LANES), lambda f, place, scalar: (0, 0, 0)),
            ],
        ),
        out_shape=[
            jax.ShapeDtypeStruct((feature_parts, both, width), jnp.bfloat16),
            jax.ShapeDtypeStruct((feature_parts, both, LANES), jnp.bfloat16),
        ],
        compiler_params=params,
        name="grad_rows",
    )(place, scalar[0, :1], gram, rounded, rest)

    grads = jnp.concatenate([grads, whole], axis=2)
    grads = lax.all_to_all(grads, FEATURE_GROUP, 0, 0, tiled=True)
    total_loss = jnp.sum(grads[:, 0, width : width + 3].astype(jnp.float32))
    grads = grads[:, :, :width].reshape(feature_parts, 2, shard_rows, width).astype(jnp.float32)
    grads = grads.transpose(1, 2, 0, 3).reshape(2, shard_rows, feature_count)
    push = 2.0 * inv_weight / out_scale * view_diff
    return grads[0] + push, grads[1] - push, total_loss


def solution(mesh):
    fine = Mesh(np.asarray(mesh.devices).reshape(SIZES), FINE)
    rows = P(FINE, None)
    return jax.shard_map(
        body, mesh=fine, in_specs=(rows, rows), out_specs=(rows, rows, P()), check_vma=False
    )
```

time: 126 us -> 114 us (0.905)
  blocking collectives: 0 us -> 57.4 us
  waiting for transfers between devices: 47.4 us -> 23.4 us
  starting transfers between devices: 29.6 us -> 8.81 us
  other arithmetic: 22.4 us -> 4.69 us
  Pallas kernels: 0 us -> 14.6 us
  between operations: 13.4 us -> 1.38 us
  matrix products: 8.05 us -> 0 us
  local copies, waits for them, and re-layouts: 4.24 us -> 2.98 us
    all_to_all x0 -> x2, blocking collectives: none -> 57.4 us  [the longest x1 41.2 us: body(): own = lax.all_to_all(blocks, CHIPS, 0, 0, tiled=True)]
    all_to_all x4 -> x2, waiting for transfers between devices: 43.3 us -> 10.9 us  [the longest x1 9.74 us: body(): pieces = lax.all_to_all(part, FEATURE_GROUP, 0, 0, tiled=True)]
    all_to_all x4 -> x2, starting transfers between devices: 23.2 us -> 7.16 us  [the longest x1 3.58 us: body(): gram = lax.all_to_all(sent, FEATURE_GROUP, 0, 0, tiled=True)]
    pallas_call x0 -> x3, Pallas kernels: none -> 14.6 us  [the longest x1 8.26 us: body(): pl.pallas_call(functools.partial(gram_kernel, sizes), grid_spec=pltpu.Pre...]
    dot_general x8 -> x0, matrix products: 8.05 us -> none  [the longest x4 6.17 us: body(): lax.dot_general(rows, rounded, (((1,), (0,)), ((), ())), preferred_elemen...]
    reduce_sum x9 -> x1, other arithmetic: 7.12 us -> 0.62 us  [body(): total_loss = jnp.sum(grads[:, 0, width:width + 3].astype(jnp.float32))]
    sub x2 -> x0, other arithmetic: 5.42 us -> none  [gram_part(): centered = values - jnp.sum(values, axis=0) / batch_rows]
    ppermute x3, waiting for transfers between devices: 4.08 us -> 8.3 us  [body(): scalar = scalar + lax.ppermute(scalar, axis, pairs)]
  transfers between devices with their start and end apart: 8 -> 6, of which waited for: 6 -> 6; matrix products, arithmetic and copies ran while one was open for 9% -> 2% of each run, Pallas kernels for 0% -> 0%
where the time goes in v2:
time: 114 us; the launch traced here: 113 us
  blocking collectives  57.4 us (50%)
  waiting for transfers between devices  23.4 us (21%)
  Pallas kernels  14.6 us (13%)
  starting transfers between devices  8.81 us (8%)
  other arithmetic  4.69 us (4%)
  local copies, waits for them, and re-layouts  2.98 us (3%)
  between operations  1.38 us (1%)
    all_to_all x1, blocking collectives, body(): own = lax.all_to_all(blocks, CHIPS, 0, 0, tiled=True)  41.2 us
    all_to_all x1, blocking collectives, body(): grads = lax.all_to_all(grads, FEATURE_GROUP, 0, 0, tiled=True)  16.3 us
    all_to_all x1, waiting for transfers between devices, body(): pieces = lax.all_to_all(part, FEATURE_GROUP, 0, 0, tiled=True)  9.74 us
    ppermute x3, waiting for transfers between devices, body(): scalar = scalar + lax.ppermute(scalar, axis, pairs)  8.3 us
    pallas_call x1, Pallas kernels, body(): pl.pallas_call(functools.partial(gram_kernel, sizes), grid_spec=pltpu.Pre...  8.26 us
    pallas_call x1, Pallas kernels, body(): pl.pallas_call(functools.partial(grad_kernel, sizes), grid_spec=pltpu.Pre...  4.76 us
    ppermute x1, waiting for transfers between devices, body(): other = lax.ppermute(own, 'core', SWAP)  4.21 us
    all_to_all x1, starting transfers between devices, body(): gram = lax.all_to_all(sent, FEATURE_GROUP, 0, 0, tiled=True)  3.58 us
  transfers between devices with their start and end apart: 6, of which 6 were waited for; matrix products, arithmetic and copies ran while one was open for 2% of the time, Pallas kernels for 0%

profile of v2, /device:TPU:0, one launch (start us, length us, event | category | flops | bytes accessed | tf_op | source)
XLA Modules:
  0.0 113.2 jit_solution(7887227931971549883)
XLA Ops:
  0.6 1.1 pad_maximum_fusion.1
  1.7 0.3 copy.6
  2.0 0.3 copy.5
  2.6 41.2 %all_to_all.20.own = bf16[64,16,1024]{2,1,0:T(8,128)(2,1)S(1)} all-to-all(bf16[64,16,1024]{2,1,0:T(8,128)(2,1)S(1)} %bitcast.18), channel_id=1, replica_groups=mesh['zh'=2,'x'=4,'y'=4,'zl'=2,'core'=2] {'x','zh','y','zl'}, dimensions={0} | all-to-all | bytes 4194304 | tf_op jit(solution)/shard_map/all_to_all | solution.py:165
  43.8 4.2 %collective-permute-done.other = bf16[64,16,1024]{2,1,0:T(8,128)(2,1)} collective-permute-done((bf16[64,16,1024]{2,1,0:T(8,128)(2,1)S(1)}, bf16[64,16,1024]{2,1,0:T(8,128)(2,1)}, u32[]{:S(2)}, u32[]{:S(2)}) %collective-permute-start) | collective-permute-done | bytes 2097184 | tf_op jit(solution)/shard_map/ppermute | solution.py:166
  48.0 8.3 %gram_part.1 = (bf16[2,1024,1024]{2,1,0:T(8,128)(2,1)}, bf16[16,16,1024]{2,1,0:T(8,128)(2,1)S(1)}, f32[2,128,1024]{2,1,0:T(8,128)S(1)}, f32[1,1024]{1,0:T(1,128)S(1)}) custom-call(s32[2]{0:T(128)S(1)} %pad_add_fusion.place, bf16[64,16,1024]{2,1,0:T(8,128)(2,1)S(1)} %all_to_all.20.own, bf16[64,16,1024]{2,1,0:T(8,128)(2,1)} %collective-permute-done.other), custom_call_target="tpu_custom_call" | custom-call | tf_op jit(solution)/shard_map/gram_part/pallas_call | solution.py:170
  56.3 0.8 copy-done
  57.1 3.6 %all-to-all-start.1 = ((bf16[16,16,1024]{2,1,0:T(8,128)(2,1)}), bf16[16,16,1024]{2,1,0:T(8,128)(2,1)S(1)}, u32[]{:S(2)}, u32[]{:S(2)}) async-start(bf16[16,16,1024]{2,1,0:T(8,128)(2,1)} %copy-done), calls=%async_computation.1 | async-start | bytes 1048576 | tf_op jit(solution)/shard_map/all_to_all | solution.py:197
  60.7 1.7 %multiply_reduce_fusion = f32[]{:T(128)} fusion(bf16[8,16384]{1,0:T(8,128)(2,1)S(1)} %copy-done.1, bf16[8,16384]{1,0:T(8,128)(2,1)} %param.2), kind=kLoop, calls=%fused_computation.4 | loop fusion | flops 655359 | bytes 524292 | tf_op jit(solution)/shard_map/reduce_sum | solution.py:168
  63.0 9.7 %all-to-all-done.1.pieces = bf16[16,16,1024]{2,1,0:T(8,128)(2,1)S(1)} async-done(((bf16[16,16,1024]{2,1,0:T(8,128)(2,1)}), bf16[16,16,1024]{2,1,0:T(8,128)(2,1)S(1)}, u32[]{:S(2)}, u32[]{:S(2)}) %all-to-all-start.1) | async-done | bytes 524320 | tf_op jit(solution)/shard_map/all_to_all | solution.py:197
  72.7 1.6 %gram_sum.1 = (bf16[16,16,1152]{2,1,0:T(8,128)(2,1)}, f32[8,128]{1,0:T(8,128)S(1)}) custom-call(s32[2]{0:T(128)S(1)} %pad_add_fusion.place, f32[1]{0:T(128)} %bitcast.2.inv, bf16[16,16,1024]{2,1,0:T(8,128)(2,1)S(1)} %all-to-all-done.1.pieces, f32[1,1024]{1,0:T(1,128)S(1)} %get-tuple-element.12.share), custom_call_target="tpu_custom_call" | custom-call | tf_op jit(solution)/shard_map/gram_sum/pallas_call | solution.py:200
  74.3 3.6 %all-to-all-start.2 = ((bf16[16,16,1152]{2,1,0:T(8,128)(2,1)}), bf16[16,16,1152]{2,1,0:T(8,128)(2,1)S(1)}, u32[]{:S(2)}, u32[]{:S(2)}) async-start(bf16[16,16,1152]{2,1,0:T(8,128)(2,1)} %get-tuple-element.14), calls=%async_computation.2 | async-start | bytes 1179648 | tf_op jit(solution)/shard_map/all_to_all | solution.py:212
  78.0 1.2 %collective-permute-done.1 = f32[8,128]{1,0:T(8,128)S(1)} collective-permute-done((f32[8,128]{1,0:T(8,128)S(1)}, f32[8,128]{1,0:T(8,128)S(1)}, u32[]{:S(2)}, u32[]{:S(2)}) %collective-permute-start.1) | collective-permute-done | bytes 4128 | tf_op jit(solution)/shard_map/ppermute | solution.py:214
  79.1 0.7 collective-permute-start.2
  79.8 2.9 %collective-permute-done.2 = f32[8,128]{1,0:T(8,128)S(1)} collective-permute-done((f32[8,128]{1,0:T(8,128)S(1)}, f32[8,128]{1,0:T(8,128)S(1)}, u32[]{:S(2)}, u32[]{:S(2)}) %collective-permute-start.2) | collective-permute-done | bytes 4128 | tf_op jit(solution)/shard_map/ppermute | solution.py:214
  82.8 0.9 collective-permute-start.3
  83.7 4.2 %collective-permute-done.3 = f32[8,128]{1,0:T(8,128)S(1)} collective-permute-done((f32[8,128]{1,0:T(8,128)S(1)}, f32[8,128]{1,0:T(8,128)S(1)}, u32[]{:S(2)}, u32[]{:S(2)}) %collective-permute-start.3) | collective-permute-done | bytes 4128 | tf_op jit(solution)/shard_map/ppermute | solution.py:214
  87.9 0.5 slice.17
  88.4 1.1 all-to-all-done.2.gram
  89.5 4.8 %grad_rows.1 = (bf16[16,16,1024]{2,1,0:T(8,128)(2,1)S(1)}, bf16[16,16,128]{2,1,0:T(8,128)(2,1)S(1)}) custom-call(s32[2]{0:T(128)S(1)} %pad_add_fusion.place, f32[1]{0:T(128)} %bitcast.5.scalar, bf16[16,16,1152]{2,1,0:T(8,128)(2,1)S(1)} %all-to-all-done.2.gram, bf16[2,1024,1024]{2,1,0:T(8,128)(2,1)} %get-tuple-element.15.rounded, ...), custom_call_target="tpu_custom_call" | custom-call | tf_op jit(solution)/shard_map/grad_rows/pallas_call | solution.py:216
  94.3 16.3 %all_to_all.21 = bf16[16,16,1152]{2,1,0:T(8,128)(2,1)S(1)} all-to-all(bf16[16,16,1152]{2,1,0:T(8,128)(2,1)S(1)} %pad_maximum_fusion), channel_id=1, replica_groups=mesh['zh'=2,'x'=4,'y'=4,'zl'=2,'core'=2] {'zh','y','zl'}, dimensions={0} | all-to-all | bytes 1179648 | tf_op jit(solution)/shard_map/all_to_all | solution.py:240
  110.8 0.8 copy-done.2
  111.6 1.1 fusion.1
  112.6 0.6 fusion.3
  (14 shorter events, 0.7 us)
Async XLA Ops:
  43.7 4.3 %collective-permute-start = (bf16[64,16,1024]{2,1,0:T(8,128)(2,1)S(1)}, bf16[64,16,1024]{2,1,0:T(8,128)(2,1)}, u32[]{:S(2)}, u32[]{:S(2)}) collective-permute-start(bf16[64,16,1024]{2,1,0:T(8,128)(2,1)S(1)} %all_to_all.20.own), channel_id=1, source_target_pairs={{0,1},{1,0},{2,3},{3,2},{4,5},{5,4},{6,7},{7,6},{8,9},{9,8},{10,11... | collective-permute-start | bytes 6291464 | tf_op jit(solution)/shard_map/ppermute | solution.py:166
  43.8 16.9 %copy-start.1 = (bf16[8,16384]{1,0:T(8,128)(2,1)S(1)}, bf16[8,16384]{1,0:T(8,128)(2,1)}, u32[]{:S(2)}) copy-start(bf16[8,16384]{1,0:T(8,128)(2,1)} %param.3) | copy-start | bytes 786436
  56.3 0.8 copy-start
  57.1 15.7 %all-to-all-start.1 = ((bf16[16,16,1024]{2,1,0:T(8,128)(2,1)}), bf16[16,16,1024]{2,1,0:T(8,128)(2,1)S(1)}, u32[]{:S(2)}, u32[]{:S(2)}) async-start(bf16[16,16,1024]{2,1,0:T(8,128)(2,1)} %copy-done), calls=%async_computation.1 | async-start | bytes 1048576 | tf_op jit(solution)/shard_map/all_to_all | solution.py:197
  74.3 15.2 %all-to-all-start.2 = ((bf16[16,16,1152]{2,1,0:T(8,128)(2,1)}), bf16[16,16,1152]{2,1,0:T(8,128)(2,1)S(1)}, u32[]{:S(2)}, u32[]{:S(2)}) async-start(bf16[16,16,1152]{2,1,0:T(8,128)(2,1)} %get-tuple-element.14), calls=%async_computation.2 | async-start | bytes 1179648 | tf_op jit(solution)/shard_map/all_to_all | solution.py:212
  77.9 1.2 %collective-permute-start.1 = (f32[8,128]{1,0:T(8,128)S(1)}, f32[8,128]{1,0:T(8,128)S(1)}, u32[]{:S(2)}, u32[]{:S(2)}) collective-permute-start(f32[8,128]{1,0:T(8,128)S(1)} %get-tuple-element.13), channel_id=1, source_target_pairs={{0,1},{1,0},{2,3},{3,2},{4,5},{5,4},{6,7},{7,6},{8,9},{9,8},{10,11... | collective-permute-start | bytes 12296 | tf_op jit(solution)/shard_map/ppermute | solution.py:214
  79.1 3.6 %collective-permute-start.2 = (f32[8,128]{1,0:T(8,128)S(1)}, f32[8,128]{1,0:T(8,128)S(1)}, u32[]{:S(2)}, u32[]{:S(2)}) collective-permute-start(f32[8,128]{1,0:T(8,128)S(1)} %add.20), channel_id=1, source_target_pairs={{0,16},{16,0},{32,48},{48,32},{1,17},{17,1},{33,49},{49,33},{2,18}... | collective-permute-start | bytes 12296 | tf_op jit(solution)/shard_map/ppermute | solution.py:214
  82.8 5.1 %collective-permute-start.3 = (f32[8,128]{1,0:T(8,128)S(1)}, f32[8,128]{1,0:T(8,128)S(1)}, u32[]{:S(2)}, u32[]{:S(2)}) collective-permute-start(f32[8,128]{1,0:T(8,128)S(1)} %add.21), channel_id=1, source_target_pairs={{0,32},{32,0},{16,48},{48,16},{1,33},{33,1},{17,49},{49,17},{2,34}... | collective-permute-start | bytes 12296 | tf_op jit(solution)/shard_map/ppermute | solution.py:214
  110.6 1.0 copy-start.2

commit v3 on v2

v3 whole, which is shorter than its diff:
```python
import functools

import jax
import jax.numpy as jnp
import numpy as np
from jax import lax
from jax.experimental import pallas as pl
from jax.experimental.pallas import tpu as pltpu
from jax.sharding import Mesh
from jax.sharding import PartitionSpec as P

epsilon = 0.0001
inv_weight = 25.0
var_weight = 25.0
cov_weight = 1.0
out_scale = 25.0

FINE = ("zh", "x", "y", "zl", "core")
SIZES = (2, 4, 4, 2, 2)
LANES = 128
VMEM_BYTES = 48 * 1024 * 1024
CONTRACT_LAST = (((1,), (1,)), ((), ()))
CONTRACT_FIRST = (((1,), (0,)), ((), ()))

IDS = np.arange(128).reshape(SIZES)
BY_RING = np.stack(
    [
        IDS[..., 0].transpose(1, 0, 2, 3).reshape(4, 16),
        IDS[..., 1].transpose(2, 0, 1, 3).reshape(4, 16),
    ]
)
GROUPS = [[int(i) for i in g] for core in BY_RING for g in core]
SWAP = [(int(i), int(i) ^ 1) for i in IDS.reshape(-1)]


def along_ring(source):
    return [
        (int(BY_RING[k, source[i], c]), int(BY_RING[k, i, c]))
        for k in range(2)
        for i in range(4)
        for c in range(16)
    ]


UP = along_ring((3, 0, 1, 2))
DOWN = along_ring((1, 2, 3, 0))
NEAR = along_ring((1, 0, 3, 2))
FAR = along_ring((2, 3, 0, 1))


def exchange(blocks):
    return lax.all_to_all(blocks, FINE, 0, 0, tiled=True, axis_index_groups=GROUPS)


def move(block, pairs):
    return lax.ppermute(block, FINE, pairs)


def pick(core, first, second):
    return jnp.where(core == 0, first, second)


def pack_kernel(core, view_one, view_two, got, packed):
    parts, rows, width = packed.shape
    for c in range(parts):
        cut = pl.ds(c * width, width)
        keep = pick(
            core[0], view_one[:, cut].astype(jnp.float32), view_two[:, cut].astype(jnp.float32)
        )
        both = jnp.concatenate([keep, got[:, cut].astype(jnp.float32)], axis=0)
        packed[c] = both.astype(jnp.bfloat16)


def gram_kernel(sizes, own, up, down, far_up, far_down, rounded, part, rest, share, total):
    batch_rows, feature_count, row_parts = sizes
    group_rows = batch_rows // row_parts
    step = pl.program_id(0)
    width = own.shape[2]
    factor_cov = 4.0 * cov_weight * batch_rows / (batch_rows - 1) ** 2 / out_scale
    factor_var = var_weight * batch_rows / (batch_rows - 1) / out_scale
    values = [
        ref[...].reshape(-1, width).astype(jnp.float32)
        for ref in (own, up, down, far_up, far_down)
    ]
    mean = sum(jnp.sum(a, axis=0, keepdims=True) for a in values) / batch_rows
    values = [a - mean for a in values]
    square = sum(jnp.sum(a * a, axis=0, keepdims=True) for a in values)
    spread = jnp.sqrt(square / (batch_rows - 1) + epsilon)
    energy = 0.0
    row = 0
    for a in values:
        a = a.astype(jnp.bfloat16)
        rounded[pl.ds(row, a.shape[0])] = a
        row += a.shape[0]
        a = a.astype(jnp.float32)
        energy += jnp.sum(a * a, axis=0, keepdims=True)
    mine = rounded[pl.ds(0, group_rows)]
    product = lax.dot_general(
        mine, rounded[...], CONTRACT_LAST, preferred_element_type=jnp.float32
    )
    hinge = values[0] * jnp.where(spread < 1.0, 1.0 / spread, 0.0)
    rest[...] = -factor_var * hinge - mine.astype(jnp.float32) * (factor_cov * energy)
    shares = var_weight / feature_count / row_parts * jnp.maximum(1.0 - spread, 0.0)
    share[...] = shares - cov_weight / feature_count / row_parts * (energy / (batch_rows - 1)) ** 2

    @pl.when(step == 0)
    def _():
        total[...] = product

    @pl.when(step > 0)
    def _():
        total[...] += product

    @pl.when(step == pl.num_programs(0) - 1)
    def _():
        part[...] = total[...].astype(jnp.bfloat16).reshape(part.shape)


def sum_kernel(sizes, place, inv, pieces, share, sent, scalar):
    batch_rows, feature_count, row_parts = sizes
    rows = pieces.shape[1]
    summed = jnp.sum(pieces[...].astype(jnp.float32), axis=0)
    shape = summed.shape
    lane = lax.broadcasted_iota(jnp.int32, shape, 1)
    row = lax.broadcasted_iota(jnp.int32, shape, 0)
    short = summed.astype(jnp.bfloat16).astype(jnp.float32)
    on_diagonal = lane == place[0] * rows + row
    lost = jnp.sum(jnp.where(on_diagonal, summed - short, 0.0), axis=1, keepdims=True)
    extra = jnp.broadcast_to(lost, (rows, LANES))
    out = jnp.concatenate([short, extra], axis=1).astype(jnp.bfloat16)
    sent[...] = jnp.broadcast_to(out[None], sent.shape)
    factor = cov_weight / feature_count / (batch_rows - 1) ** 2
    value = factor * jnp.sum(summed * summed) + jnp.sum(share[...]) + inv[0]
    scalar[...] = jnp.full(scalar.shape, value, jnp.float32)


def grad_kernel(sizes, scalar, gram, rounded, rest, sent, matrix, lost):
    batch_rows, feature_count, row_parts = sizes
    parts, rows, _ = gram.shape
    group_rows = parts * rows
    step = pl.program_id(0)
    width = rounded.shape[1]
    factor_cov = 4.0 * cov_weight * batch_rows / (batch_rows - 1) ** 2 / out_scale

    @pl.when(step == 0)
    def _():
        matrix[...] = gram[:, :, pl.ds(0, batch_rows)].reshape(group_rows, batch_rows)
        extra = gram[:, :, pl.ds(batch_rows, LANES)].reshape(group_rows, LANES)
        lost[...] = extra.astype(jnp.float32)
        value = jnp.broadcast_to(scalar[0:1], (rows, LANES))
        high = value.astype(jnp.bfloat16).astype(jnp.float32)
        middle = (value - high).astype(jnp.bfloat16).astype(jnp.float32)
        low = value - high - middle
        lane = lax.broadcasted_iota(jnp.int32, value.shape, 1)
        three = jnp.where(lane == 0, high, jnp.where(lane == 1, middle, low)).astype(jnp.bfloat16)
        whole = sent.shape[2] - LANES
        sent[:, :, pl.ds(whole, LANES)] = jnp.broadcast_to(three[None], (parts, rows, LANES))

    product = lax.dot_general(
        matrix[...], rounded[...], CONTRACT_FIRST, preferred_element_type=jnp.float32
    )
    mine = rounded[pl.ds(0, group_rows)].astype(jnp.float32)
    grad = factor_cov * (product + lost[:, 0:1] * mine) + rest[...]
    cut = pl.ds(pl.multiple_of(step * width, width), width)
    sent[:, :, cut] = grad.astype(jnp.bfloat16).reshape(parts, rows, width)


def final_kernel(core, recv, got, view_one, view_two, grad_one, grad_two, loss):
    parts, rows, width = got.shape
    width -= LANES
    push = 2.0 * inv_weight / out_scale
    sums = 0.0
    for c in range(parts):
        mine = recv[c].astype(jnp.float32)[:rows]
        other = got[c].astype(jnp.float32)
        cut = pl.ds(c * width, width)
        diff = push * (view_one[:, cut].astype(jnp.float32) - view_two[:, cut].astype(jnp.float32))
        grad_one[:, cut] = pick(core[0], mine[:, :width], other[:, :width]) + diff
        grad_two[:, cut] = pick(core[0], other[:, :width], mine[:, :width]) - diff
        sums += mine[:, width:] + other[:, width:]
    lane = lax.broadcasted_iota(jnp.int32, sums.shape, 1)
    row = lax.broadcasted_iota(jnp.int32, sums.shape, 0)
    loss[0] = jnp.sum(jnp.where((lane < 3) & (row == 0), sums, 0.0))


def body(view_one, view_two):
    shard_rows, feature_count = view_one.shape
    row_parts, feature_parts = BY_RING.shape[1:]
    batch_rows = shard_rows * 2 * row_parts * feature_parts
    group_rows = batch_rows // row_parts
    width = feature_count // feature_parts
    rows = 2 * shard_rows
    steps = 4
    chunk = width // steps
    sizes = (batch_rows, feature_count, row_parts)
    core = lax.axis_index("core")
    across = pick(core, lax.axis_index("y"), lax.axis_index("x"))
    place = (lax.axis_index("zh") * 4 + across) * 2 + lax.axis_index("zl")
    core = core.astype(jnp.int32).reshape(1)
    place = place.astype(jnp.int32).reshape(1)
    params = pltpu.CompilerParams(vmem_limit_bytes=VMEM_BYTES)
    smem = pl.BlockSpec(memory_space=pltpu.SMEM)
    vmem = pl.BlockSpec(memory_space=pltpu.VMEM)

    swapped = move(pick(core[0], view_two, view_one), SWAP)
    blocks = pl.pallas_call(
        pack_kernel,
        in_specs=[smem, vmem, vmem, vmem],
        out_specs=vmem,
        out_shape=jax.ShapeDtypeStruct((feature_parts, rows, width), jnp.bfloat16),
        compiler_params=params,
        name="pack_rows",
    )(core, view_one, view_two, swapped)
    own = exchange(blocks)
    up, down = move(own, UP), move(own, DOWN)
    half = feature_parts // 2
    far_up, far_down = move(up[:half], UP), move(down[half:], DOWN)
    view_diff = view_one.astype(jnp.float32) - view_two.astype(jnp.float32)
    inv = inv_weight / (batch_rows * feature_count) * jnp.sum(view_diff * view_diff)

    full_block = pl.BlockSpec((feature_parts, rows, chunk), lambda f: (0, 0, f))
    half_block = pl.BlockSpec((half, rows, chunk), lambda f: (0, 0, f))
    rounded, part, rest, share = pl.pallas_call(
        functools.partial(gram_kernel, sizes),
        grid=(steps,),
        in_specs=[full_block, full_block, full_block, half_block, half_block],
        out_specs=[
            pl.BlockSpec((batch_rows, chunk), lambda f: (0, f)),
            pl.BlockSpec((feature_parts, rows, batch_rows), lambda f: (0, 0, 0)),
            pl.BlockSpec((group_rows, chunk), lambda f: (0, f)),
            pl.BlockSpec((1, chunk), lambda f: (0, f)),
        ],
        scratch_shapes=[pltpu.VMEM((group_rows, batch_rows), jnp.float32)],
        out_shape=[
            jax.ShapeDtypeStruct((batch_rows, width), jnp.bfloat16),
            jax.ShapeDtypeStruct((feature_parts, rows, batch_rows), jnp.bfloat16),
            jax.ShapeDtypeStruct((group_rows, width), jnp.float32),
            jax.ShapeDtypeStruct((1, width), jnp.float32),
        ],
        compiler_params=params,
        name="gram_part",
    )(own, up, down, far_up, far_down)

    pieces = exchange(part)
    sent, scalar = pl.pallas_call(
        functools.partial(sum_kernel, sizes),
        in_specs=[smem, smem, vmem, vmem],
        out_specs=[vmem, vmem],
        out_shape=[
            jax.ShapeDtypeStruct((feature_parts, rows, batch_rows + LANES), jnp.bfloat16),
            jax.ShapeDtypeStruct((8, LANES), jnp.float32),
        ],
        compiler_params=params,
        name="gram_sum",
    )(place, inv.reshape(1), pieces, share)

    gram = exchange(sent)
    scalar = scalar + move(scalar, NEAR)
    scalar = scalar + move(scalar, FAR)

    grads = pl.pallas_call(
        functools.partial(grad_kernel, sizes),
        grid=(steps,),
        in_specs=[
            vmem,
            pl.BlockSpec(sent.shape, lambda f: (0, 0, 0)),
            pl.BlockSpec((batch_rows, chunk), lambda f: (0, f)),
            pl.BlockSpec((group_rows, chunk), lambda f: (0, f)),
        ],
        out_specs=pl.BlockSpec((feature_parts, rows, width + LANES), lambda f: (0, 0, 0)),
        out_shape=jax.ShapeDtypeStruct((feature_parts, rows, width + LANES), jnp.bfloat16),
        scratch_shapes=[
            pltpu.VMEM((group_rows, batch_rows), jnp.bfloat16),
            pltpu.VMEM((group_rows, LANES), jnp.float32),
        ],
        compiler_params=params,
        name="grad_rows",
    )(scalar, gram, rounded, rest)

    grads = exchange(grads)
    others = move(grads[:, shard_rows:], SWAP)
    grad_one, grad_two, loss = pl.pallas_call(
        final_kernel,
        in_specs=[smem, vmem, vmem, vmem, vmem],
        out_specs=[vmem, vmem, smem],
        out_shape=[
            jax.ShapeDtypeStruct(view_one.shape, jnp.float32),
            jax.ShapeDtypeStruct(view_one.shape, jnp.float32),
            jax.ShapeDtypeStruct((1,), jnp.float32),
        ],
        compiler_params=params,
        name="add_pull",
    )(core, grads, others, view_one, view_two)
    return grad_one, grad_two, loss.reshape(())


def solution(mesh):
    fine = Mesh(np.asarray(mesh.devices).reshape(SIZES), FINE)
    rows = P(FINE, None)
    return jax.shard_map(
        body, mesh=fine, in_specs=(rows, rows), out_specs=(rows, rows, P()), check_vma=False
    )
```

time: 114 us -> 103 us (0.904)
  blocking collectives: 57.4 us -> 34.1 us
  waiting for transfers between devices: 23.4 us -> 36.4 us
  Pallas kernels: 14.6 us -> 7.3 us
  starting transfers between devices: 8.81 us -> 14.6 us
  other arithmetic: 4.69 us -> 1.73 us
  local copies, waits for them, and re-layouts: 2.98 us -> 5.78 us
    all_to_all x2, blocking collectives: 57.4 us -> 34.1 us  [exchange(): lax.all_to_all(blocks, FINE, 0, 0, tiled=True, axis_index_groups=GROUPS)]
    ppermute x4 -> x8, waiting for transfers between devices: 12.5 us -> 26.1 us  [move(): return lax.ppermute(block, FINE, pairs)]
    pallas_call x2 -> x4, Pallas kernels: 13 us -> 7.08 us  [the longest x1 4.12 us: body(): pl.pallas_call(functools.partial(gram_kernel, sizes), grid=(steps,), in_s...]
    ppermute x4 -> x8, starting transfers between devices: 1.66 us -> 6.51 us  [move(): return lax.ppermute(block, FINE, pairs)]
    unnamed x7 -> x16, local copies, waits for them, and re-layouts: 1.84 us -> 5.72 us
    pallas_call x1, Pallas kernels: 1.56 us -> 0.22 us  [body(): pl.pallas_call(functools.partial(sum_kernel, sizes), in_specs=[smem, smem...]
  transfers between devices with their start and end apart: 6 -> 10, of which waited for: 6 -> 9; matrix products, arithmetic and copies ran while one was open for 2% -> 1% of each run, Pallas kernels for 0% -> 0%
where the time goes in v3:
time: 103 us; the launch traced here: 101 us
  waiting for transfers between devices  36.4 us (35%)
  blocking collectives  34.1 us (33%)
  starting transfers between devices  14.6 us (14%)
  Pallas kernels  7.3 us (7%)
  local copies, waits for them, and re-layouts  5.78 us (6%)
  other arithmetic  1.73 us (2%)
  between operations  1.44 us (1%)
    all_to_all x2, blocking collectives, exchange(): lax.all_to_all(blocks, FINE, 0, 0, tiled=True, axis_index_groups=GROUPS)  34.1 us
    ppermute x8, waiting for transfers between devices, move(): return lax.ppermute(block, FINE, pairs)  26.1 us
    all_to_all x2, waiting for transfers between devices, exchange(): lax.all_to_all(blocks, FINE, 0, 0, tiled=True, axis_index_groups=GROUPS)  10.3 us
    all_to_all x2, starting transfers between devices, exchange(): lax.all_to_all(blocks, FINE, 0, 0, tiled=True, axis_index_groups=GROUPS)  8.09 us
    ppermute x8, starting transfers between devices, move(): return lax.ppermute(block, FINE, pairs)  6.51 us
    unnamed x16, local copies, waits for them, and re-layouts  5.72 us
    pallas_call x1, Pallas kernels, body(): pl.pallas_call(functools.partial(gram_kernel, sizes), grid=(steps,), in_s...  4.12 us
  transfers between devices with their start and end apart: 10, of which 9 were waited for; matrix products, arithmetic and copies ran while one was open for 1% of the time, Pallas kernels for 0%

profile of v3, /device:TPU:0, one launch (start us, length us, event | category | flops | bytes accessed | tf_op | source)
XLA Modules:
  0.0 101.3 jit_solution(7188762579978162093)
XLA Ops:
  0.6 1.0 broadcast_select_fusion
  1.7 1.5 %collective-permute-done.got = bf16[8,16384]{1,0:T(8,128)(2,1)S(1)} collective-permute-done((bf16[8,16384]{1,0:T(8,128)(2,1)S(1)}, bf16[8,16384]{1,0:T(8,128)(2,1)S(1)}, u32[]{:S(2)}, u32[]{:S(2)}) %collective-permute-start) | collective-permute-done | bytes 262176 | tf_op jit(solution)/shard_map/ppermute | solution.py:56
  3.2 0.9 copy-done
  4.2 0.9 copy-done.2
  5.2 18.3 %all_to_all.20.own = bf16[16,16,1024]{2,1,0:T(8,128)(2,1)S(1)} all-to-all(bf16[16,16,1024]{2,1,0:T(8,128)(2,1)S(1)} %pack_rows.1), channel_id=1, replica_groups={{0,2,4,6,8,10,12,14,64,66,68,70,72,74,76,78},{16,18,20,22,24,26,28,30,8..., dimensions={0} | all-to-all | bytes 1048576 | tf_op jit(solution)/shard_map/all_to_all | solution.py:52
  23.6 2.4 %collective-permute-start.2 = (bf16[16,16,1024]{2,1,0:T(8,128)(2,1)S(1)}, bf16[16,16,1024]{2,1,0:T(8,128)(2,1)S(1)}, u32[]{:S(2)}, u32[]{:S(2)}) collective-permute-start(bf16[16,16,1024]{2,1,0:T(8,128)(2,1)S(1)} %all_to_all.20.own), channel_id=1, source_target_pairs={{16,0},{18,2},{20,4},{22,6},{24,8},{26,10},{28,12},{30,14},{80,64}... | collective-permute-start | bytes 1572872 | tf_op jit(solution)/shard_map/ppermute | solution.py:56
  26.0 6.7 %collective-permute-done.2.down = bf16[16,16,1024]{2,1,0:T(8,128)(2,1)S(1)} collective-permute-done((bf16[16,16,1024]{2,1,0:T(8,128)(2,1)S(1)}, bf16[16,16,1024]{2,1,0:T(8,128)(2,1)S(1)}, u32[]{:S(2)}, u32[]{:S(2)}) %collective-permute-start.2) | collective-permute-done | bytes 524320 | tf_op jit(solution)/shard_map/ppermute | solution.py:56
  32.8 3.7 %collective-permute-start.4 = (bf16[8,16,1024]{2,1,0:T(8,128)(2,1)S(1)}, bf16[8,16,1024]{2,1,0:T(8,128)(2,1)S(1)}, u32[]{:S(2)}, u32[]{:S(2)}) collective-permute-start(bf16[8,16,1024]{2,1,0:T(8,128)(2,1)S(1)} %slice.13), channel_id=1, source_target_pairs={{16,0},{18,2},{20,4},{22,6},{24,8},{26,10},{28,12},{30,14},{80,64}... | collective-permute-start | bytes 786440 | tf_op jit(solution)/shard_map/ppermute | solution.py:56
  36.6 3.8 %collective-permute-done.4.far_down = bf16[8,16,1024]{2,1,0:T(8,128)(2,1)S(1)} collective-permute-done((bf16[8,16,1024]{2,1,0:T(8,128)(2,1)S(1)}, bf16[8,16,1024]{2,1,0:T(8,128)(2,1)S(1)}, u32[]{:S(2)}, u32[]{:S(2)}) %collective-permute-start.4) | collective-permute-done | bytes 262176 | tf_op jit(solution)/shard_map/ppermute | solution.py:56
  40.4 3.8 %collective-permute-done.3.far_up = bf16[8,16,1024]{2,1,0:T(8,128)(2,1)S(1)} collective-permute-done((bf16[8,16,1024]{2,1,0:T(8,128)(2,1)S(1)}, bf16[8,16,1024]{2,1,0:T(8,128)(2,1)S(1)}, u32[]{:S(2)}, u32[]{:S(2)}) %collective-permute-start.3) | collective-permute-done | bytes 262176 | tf_op jit(solution)/shard_map/ppermute | solution.py:56
  44.2 4.1 %gram_part.1 = (bf16[1024,1024]{1,0:T(8,128)(2,1)S(1)}, bf16[16,16,1024]{2,1,0:T(8,128)(2,1)S(1)}, f32[256,1024]{1,0:T(8,128)S(1)}, f32[1,1024]{1,0:T(1,128)S(1)}) custom-call(bf16[16,16,1024]{2,1,0:T(8,128)(2,1)S(1)} %all_to_all.20.own, bf16[16,16,1024]{2,1,0:T(8,128)(2,1)S(1)} %collective-permute-done.1.up, ...), custom_call_target="tpu_custom_call" | custom-call | tf_op jit(solution)/shard_map/gram_part/pallas_call | solution.py:223
  48.3 1.0 copy-done.4
  50.1 4.5 %all-to-all-start.1 = ((bf16[16,16,1024]{2,1,0:T(8,128)(2,1)}), bf16[16,16,1024]{2,1,0:T(8,128)(2,1)S(1)}, u32[]{:S(2)}, u32[]{:S(2)}) async-start(bf16[16,16,1024]{2,1,0:T(8,128)(2,1)} %copy-done.7), calls=%async_computation.1 | async-start | bytes 1048576 | tf_op jit(solution)/shard_map/all_to_all | solution.py:52
  56.0 8.7 %all-to-all-done.1.pieces = bf16[16,16,1024]{2,1,0:T(8,128)(2,1)S(1)} async-done(((bf16[16,16,1024]{2,1,0:T(8,128)(2,1)}), bf16[16,16,1024]{2,1,0:T(8,128)(2,1)S(1)}, u32[]{:S(2)}, u32[]{:S(2)}) %all-to-all-start.1) | async-done | bytes 524320 | tf_op jit(solution)/shard_map/all_to_all | solution.py:52
  65.0 0.8 copy-done.6
  65.8 3.6 %all-to-all-start.2 = ((bf16[16,16,1152]{2,1,0:T(8,128)(2,1)}), bf16[16,16,1152]{2,1,0:T(8,128)(2,1)S(1)}, u32[]{:S(2)}, u32[]{:S(2)}) async-start(bf16[16,16,1152]{2,1,0:T(8,128)(2,1)} %copy-done.6), calls=%async_computation.2 | async-start | bytes 1179648 | tf_op jit(solution)/shard_map/all_to_all | solution.py:52
  69.4 3.6 %collective-permute-done.5 = f32[8,128]{1,0:T(8,128)S(1)} collective-permute-done((f32[8,128]{1,0:T(8,128)S(1)}, f32[8,128]{1,0:T(8,128)S(1)}, u32[]{:S(2)}, u32[]{:S(2)}) %collective-permute-start.5) | collective-permute-done | bytes 4128 | tf_op jit(solution)/shard_map/ppermute | solution.py:56
  73.0 5.1 %collective-permute-done.6 = f32[8,128]{1,0:T(8,128)S(1)} collective-permute-done((f32[8,128]{1,0:T(8,128)S(1)}, f32[8,128]{1,0:T(8,128)S(1)}, u32[]{:S(2)}, u32[]{:S(2)}) %collective-permute-start.6) | collective-permute-done | bytes 4128 | tf_op jit(solution)/shard_map/ppermute | solution.py:56
  78.2 1.6 %all-to-all-done.2.gram = bf16[16,16,1152]{2,1,0:T(8,128)(2,1)S(1)} async-done(((bf16[16,16,1152]{2,1,0:T(8,128)(2,1)}), bf16[16,16,1152]{2,1,0:T(8,128)(2,1)S(1)}, u32[]{:S(2)}, u32[]{:S(2)}) %all-to-all-start.2) | async-done | bytes 589856 | tf_op jit(solution)/shard_map/all_to_all | solution.py:52
  79.8 1.2 %copy-done.5 = f32[256,1024]{1,0:T(8,128)S(1)} copy-done((f32[256,1024]{1,0:T(8,128)S(1)}, f32[256,1024]{1,0:T(8,128)}, u32[]{:S(2)}) %copy-start.5) | copy-done | bytes 1048600
  81.0 1.7 %grad_rows.1 = bf16[16,16,1152]{2,1,0:T(8,128)(2,1)S(1)} custom-call(f32[8,128]{1,0:T(8,128)S(1)} %add.15.scalar, bf16[16,16,1152]{2,1,0:T(8,128)(2,1)S(1)} %all-to-all-done.2.gram, bf16[1024,1024]{1,0:T(8,128)(2,1)S(1)} %get-tuple-element.16.rounded, f32[256,1024]{1,0:T(8,128)S(1)} %copy-done.5), custom_call_target="tpu_custom_call" | custom-call | tf_op jit(solution)/shard_map/grad_rows/pallas_call | solution.py:261
  82.7 15.7 %all_to_all.21.recv = bf16[16,16,1152]{2,1,0:T(8,128)(2,1)S(1)} all-to-all(bf16[16,16,1152]{2,1,0:T(8,128)(2,1)S(1)} %grad_rows.1), channel_id=1, replica_groups={{0,2,4,6,8,10,12,14,64,66,68,70,72,74,76,78},{16,18,20,22,24,26,28,30,8..., dimensions={0} | all-to-all | bytes 1179648 | tf_op jit(solution)/shard_map/all_to_all | solution.py:52
  98.6 1.6 %collective-permute-done.7.got = bf16[16,8,1152]{2,1,0:T(8,128)(2,1)S(1)} collective-permute-done((bf16[16,8,1152]{2,1,0:T(8,128)(2,1)S(1)}, bf16[16,8,1152]{2,1,0:T(8,128)(2,1)S(1)}, u32[]{:S(2)}, u32[]{:S(2)}) %collective-permute-start.7) | collective-permute-done | bytes 294944 | tf_op jit(solution)/shard_map/ppermute | solution.py:56
  100.1 1.2 %add_pull.1 = (f32[8,16384]{1,0:T(8,128)}, f32[8,16384]{1,0:T(8,128)}, f32[1]{0:T(128)}) custom-call(s32[1]{0:T(128)} %bitcast.core, bf16[16,16,1152]{2,1,0:T(8,128)(2,1)S(1)} %all_to_all.21.recv, bf16[16,8,1152]{2,1,0:T(8,128)(2,1)S(1)} %collective-permute-done.7.got, bf16[8,16384]{1,0:T(8,128)(2,1)S(1)} %copy-done.3, bf16[8,16384]{1,0:T(8,128)(2,1)S(1)} %copy-done.1), custom_call_target="tpu_custom_call" | custom-call | tf_op jit(solution)/shard_map/add_pull/pallas_call | solution.py:282
  (26 shorter events, 2.2 us)
Async XLA Ops:
  1.6 1.6 %collective-permute-start = (bf16[8,16384]{1,0:T(8,128)(2,1)S(1)}, bf16[8,16384]{1,0:T(8,128)(2,1)S(1)}, u32[]{:S(2)}, u32[]{:S(2)}) collective-permute-start(bf16[8,16384]{1,0:T(8,128)(2,1)S(1)} %broadcast_select_fusion), channel_id=1, source_target_pairs={{0,1},{1,0},{2,3},{3,2},{4,5},{5,4},{6,7},{7,6},{8,9},{9,8},{10,11... | collective-permute-start | bytes 786440 | tf_op jit(solution)/shard_map/ppermute | solution.py:56
  3.2 1.0 copy-start
  4.2 0.9 copy-start.2
  23.6 31.1 %copy-start.1 = (bf16[8,16384]{1,0:T(8,128)(2,1)S(1)}, bf16[8,16384]{1,0:T(8,128)(2,1)}, u32[]{:S(2)}) copy-start(bf16[8,16384]{1,0:T(8,128)(2,1)} %view_two.3) | copy-start | bytes 786436
  23.6 31.1 %copy-start.3 = (bf16[8,16384]{1,0:T(8,128)(2,1)S(1)}, bf16[8,16384]{1,0:T(8,128)(2,1)}, u32[]{:S(2)}) copy-start(bf16[8,16384]{1,0:T(8,128)(2,1)} %view_one.3) | copy-start | bytes 786436
  23.6 9.2 %collective-permute-start.2 = (bf16[16,16,1024]{2,1,0:T(8,128)(2,1)S(1)}, bf16[16,16,1024]{2,1,0:T(8,128)(2,1)S(1)}, u32[]{:S(2)}, u32[]{:S(2)}) collective-permute-start(bf16[16,16,1024]{2,1,0:T(8,128)(2,1)S(1)} %all_to_all.20.own), channel_id=1, source_target_pairs={{16,0},{18,2},{20,4},{22,6},{24,8},{26,10},{28,12},{30,14},{80,64}... | collective-permute-start | bytes 1572872 | tf_op jit(solution)/shard_map/ppermute | solution.py:56
  26.0 10.5 %collective-permute-start.1 = (bf16[16,16,1024]{2,1,0:T(8,128)(2,1)S(1)}, bf16[16,16,1024]{2,1,0:T(8,128)(2,1)S(1)}, u32[]{:S(2)}, u32[]{:S(2)}) collective-permute-start(bf16[16,16,1024]{2,1,0:T(8,128)(2,1)S(1)} %all_to_all.20.own), channel_id=1, source_target_pairs={{48,0},{50,2},{52,4},{54,6},{56,8},{58,10},{60,12},{62,14},{112,64... | collective-permute-start | bytes 1572872 | tf_op jit(solution)/shard_map/ppermute | solution.py:56
  32.8 7.6 %collective-permute-start.4 = (bf16[8,16,1024]{2,1,0:T(8,128)(2,1)S(1)}, bf16[8,16,1024]{2,1,0:T(8,128)(2,1)S(1)}, u32[]{:S(2)}, u32[]{:S(2)}) collective-permute-start(bf16[8,16,1024]{2,1,0:T(8,128)(2,1)S(1)} %slice.13), channel_id=1, source_target_pairs={{16,0},{18,2},{20,4},{22,6},{24,8},{26,10},{28,12},{30,14},{80,64}... | collective-permute-start | bytes 786440 | tf_op jit(solution)/shard_map/ppermute | solution.py:56
  36.5 7.7 %collective-permute-start.3 = (bf16[8,16,1024]{2,1,0:T(8,128)(2,1)S(1)}, bf16[8,16,1024]{2,1,0:T(8,128)(2,1)S(1)}, u32[]{:S(2)}, u32[]{:S(2)}) collective-permute-start(bf16[8,16,1024]{2,1,0:T(8,128)(2,1)S(1)} %slice.12), channel_id=1, source_target_pairs={{48,0},{50,2},{52,4},{54,6},{56,8},{58,10},{60,12},{62,14},{112,64... | collective-permute-start | bytes 786440 | tf_op jit(solution)/shard_map/ppermute | solution.py:56
  48.3 1.0 copy-start.4
  49.3 0.8 copy-start.7
  50.1 14.6 %all-to-all-start.1 = ((bf16[16,16,1024]{2,1,0:T(8,128)(2,1)}), bf16[16,16,1024]{2,1,0:T(8,128)(2,1)S(1)}, u32[]{:S(2)}, u32[]{:S(2)}) async-start(bf16[16,16,1024]{2,1,0:T(8,128)(2,1)} %copy-done.7), calls=%async_computation.1 | async-start | bytes 1048576 | tf_op jit(solution)/shard_map/all_to_all | solution.py:52
  64.9 0.8 copy-start.6
  65.8 14.0 %all-to-all-start.2 = ((bf16[16,16,1152]{2,1,0:T(8,128)(2,1)}), bf16[16,16,1152]{2,1,0:T(8,128)(2,1)S(1)}, u32[]{:S(2)}, u32[]{:S(2)}) async-start(bf16[16,16,1152]{2,1,0:T(8,128)(2,1)} %copy-done.6), calls=%async_computation.2 | async-start | bytes 1179648 | tf_op jit(solution)/shard_map/all_to_all | solution.py:52
  69.4 3.7 %collective-permute-start.5 = (f32[8,128]{1,0:T(8,128)S(1)}, f32[8,128]{1,0:T(8,128)S(1)}, u32[]{:S(2)}, u32[]{:S(2)}) collective-permute-start(f32[8,128]{1,0:T(8,128)S(1)} %get-tuple-element.14), channel_id=1, source_target_pairs={{16,0},{18,2},{20,4},{22,6},{24,8},{26,10},{28,12},{30,14},{80,64}... | collective-permute-start | bytes 12296 | tf_op jit(solution)/shard_map/ppermute | solution.py:56
  73.0 5.1 %collective-permute-start.6 = (f32[8,128]{1,0:T(8,128)S(1)}, f32[8,128]{1,0:T(8,128)S(1)}, u32[]{:S(2)}, u32[]{:S(2)}) collective-permute-start(f32[8,128]{1,0:T(8,128)S(1)} %add.14), channel_id=1, source_target_pairs={{32,0},{34,2},{36,4},{38,6},{40,8},{42,10},{44,12},{46,14},{96,64}... | collective-permute-start | bytes 12296 | tf_op jit(solution)/shard_map/ppermute | solution.py:56
  79.8 1.2 %copy-start.5 = (f32[256,1024]{1,0:T(8,128)S(1)}, f32[256,1024]{1,0:T(8,128)}, u32[]{:S(2)}) copy-start(f32[256,1024]{1,0:T(8,128)} %copy-done.4) | copy-start | bytes 3145732
  98.5 1.7 %collective-permute-start.7 = (bf16[16,8,1152]{2,1,0:T(8,128)(2,1)S(1)}, bf16[16,8,1152]{2,1,0:T(8,128)(2,1)S(1)}, u32[]{:S(2)}, u32[]{:S(2)}) collective-permute-start(bf16[16,8,1152]{2,1,0:T(8,128)(2,1)S(1)} %slice.14), channel_id=1, source_target_pairs={{0,1},{1,0},{2,3},{3,2},{4,5},{5,4},{6,7},{7,6},{8,9},{9,8},{10,11... | collective-permute-start | bytes 884744 | tf_op jit(solution)/shard_map/ppermute | solution.py:56

commit v4 on v3

--- a/solution.py
+++ b/solution.py
@@ -18,7 +18,6 @@
 FINE = ("zh", "x", "y", "zl", "core")
 SIZES = (2, 4, 4, 2, 2)
 LANES = 128
-VMEM_BYTES = 48 * 1024 * 1024
 CONTRACT_LAST = (((1,), (1,)), ((), ()))
 CONTRACT_FIRST = (((1,), (0,)), ((), ()))
 
@@ -44,7 +43,6 @@
 
 UP = along_ring((3, 0, 1, 2))
 DOWN = along_ring((1, 2, 3, 0))
-NEAR = along_ring((1, 0, 3, 2))
 FAR = along_ring((2, 3, 0, 1))
 
 
@@ -56,32 +54,34 @@
     return lax.ppermute(block, FINE, pairs)
 
 
+def room(mebibytes):
+    return pltpu.CompilerParams(vmem_limit_bytes=mebibytes * 1024 * 1024)
+
+
 def pick(core, first, second):
     return jnp.where(core == 0, first, second)
 
 
-def pack_kernel(core, view_one, view_two, got, packed):
+def pack_kernel(factor, keep, give, got, packed, inv):
     parts, rows, width = packed.shape
+    squares = 0.0
     for c in range(parts):
         cut = pl.ds(c * width, width)
-        keep = pick(
-            core[0], view_one[:, cut].astype(jnp.float32), view_two[:, cut].astype(jnp.float32)
-        )
-        both = jnp.concatenate([keep, got[:, cut].astype(jnp.float32)], axis=0)
-        packed[c] = both.astype(jnp.bfloat16)
-
-
-def gram_kernel(sizes, own, up, down, far_up, far_down, rounded, part, rest, share, total):
+        mine, other, more = [ref[:, cut].astype(jnp.float32) for ref in (keep, give, got)]
+        packed[c] = jnp.concatenate([mine, more], axis=0).astype(jnp.bfloat16)
+        squares += (mine - other) ** 2
+    inv[0] = factor * jnp.sum(squares)
+
+
+def gram_kernel(sizes, inv, own, *refs):
+    copies, (rounded, part, rest, share, total) = refs[:-5], refs[-5:]
     batch_rows, feature_count, row_parts = sizes
     group_rows = batch_rows // row_parts
     step = pl.program_id(0)
     width = own.shape[2]
     factor_cov = 4.0 * cov_weight * batch_rows / (batch_rows - 1) ** 2 / out_scale
     factor_var = var_weight * batch_rows / (batch_rows - 1) / out_scale
-    values = [
-        ref[...].reshape(-1, width).astype(jnp.float32)
-        for ref in (own, up, down, far_up, far_down)
-    ]
+    values = [ref[...].reshape(-1, width).astype(jnp.float32) for ref in (own,) + copies]
     mean = sum(jnp.sum(a, axis=0, keepdims=True) for a in values) / batch_rows
     values = [a - mean for a in values]
     square = sum(jnp.sum(a * a, axis=0, keepdims=True) for a in values)
@@ -101,6 +101,7 @@
     hinge = values[0] * jnp.where(spread < 1.0, 1.0 / spread, 0.0)
     rest[...] = -factor_var * hinge - mine.astype(jnp.float32) * (factor_cov * energy)
     shares = var_weight / feature_count / row_parts * jnp.maximum(1.0 - spread, 0.0)
+    shares += inv[0] / (width * pl.num_programs(0))
     share[...] = shares - cov_weight / feature_count / row_parts * (energy / (batch_rows - 1)) ** 2
 
     @pl.when(step == 0)
@@ -116,7 +117,7 @@
         part[...] = total[...].astype(jnp.bfloat16).reshape(part.shape)
 
 
-def sum_kernel(sizes, place, inv, pieces, share, sent, scalar):
+def sum_kernel(sizes, place, pieces, share, sent, scalar):
     batch_rows, feature_count, row_parts = sizes
     rows = pieces.shape[1]
     summed = jnp.sum(pieces[...].astype(jnp.float32), axis=0)
@@ -130,11 +131,11 @@
     out = jnp.concatenate([short, extra], axis=1).astype(jnp.bfloat16)
     sent[...] = jnp.broadcast_to(out[None], sent.shape)
     factor = cov_weight / feature_count / (batch_rows - 1) ** 2
-    value = factor * jnp.sum(summed * summed) + jnp.sum(share[...]) + inv[0]
+    value = factor * jnp.sum(summed * summed) + jnp.sum(share[...])
     scalar[...] = jnp.full(scalar.shape, value, jnp.float32)
 
 
-def grad_kernel(sizes, scalar, gram, rounded, rest, sent, matrix, lost):
+def grad_kernel(sizes, here, far, before, after, gram, rounded, rest, sent, matrix, lost):
     batch_rows, feature_count, row_parts = sizes
     parts, rows, _ = gram.shape
     group_rows = parts * rows
@@ -147,7 +148,8 @@
         matrix[...] = gram[:, :, pl.ds(0, batch_rows)].reshape(group_rows, batch_rows)
         extra = gram[:, :, pl.ds(batch_rows, LANES)].reshape(group_rows, LANES)
         lost[...] = extra.astype(jnp.float32)
-        value = jnp.broadcast_to(scalar[0:1], (rows, LANES))
+        scalar = (here[0:1] + far[0:1]) + (before[0:1] + after[0:1])
+        value = jnp.broadcast_to(scalar, (rows, LANES))
         high = value.astype(jnp.bfloat16).astype(jnp.float32)
         middle = (value - high).astype(jnp.bfloat16).astype(jnp.float32)
         low = value - high - middle
@@ -198,32 +200,34 @@
     place = (lax.axis_index("zh") * 4 + across) * 2 + lax.axis_index("zl")
     core = core.astype(jnp.int32).reshape(1)
     place = place.astype(jnp.int32).reshape(1)
-    params = pltpu.CompilerParams(vmem_limit_bytes=VMEM_BYTES)
     smem = pl.BlockSpec(memory_space=pltpu.SMEM)
     vmem = pl.BlockSpec(memory_space=pltpu.VMEM)
 
-    swapped = move(pick(core[0], view_two, view_one), SWAP)
-    blocks = pl.pallas_call(
-        pack_kernel,
-        in_specs=[smem, vmem, vmem, vmem],
-        out_specs=vmem,
-        out_shape=jax.ShapeDtypeStruct((feature_parts, rows, width), jnp.bfloat16),
-        compiler_params=params,
+    keep, give = pick(core[0], view_one, view_two), pick(core[0], view_two, view_one)
+    blocks, inv = pl.pallas_call(
+        functools.partial(pack_kernel, inv_weight / (batch_rows * feature_count)),
+        in_specs=[vmem, vmem, vmem],
+        out_specs=[vmem, smem],
+        out_shape=[
+            jax.ShapeDtypeStruct((feature_parts, rows, width), jnp.bfloat16),
+            jax.ShapeDtypeStruct((1,), jnp.float32),
+        ],
+        compiler_params=room(4),
         name="pack_rows",
-    )(core, view_one, view_two, swapped)
+    )(keep, give, move(give, SWAP))
     own = exchange(blocks)
-    up, down = move(own, UP), move(own, DOWN)
     half = feature_parts // 2
-    far_up, far_down = move(up[:half], UP), move(down[half:], DOWN)
-    view_diff = view_one.astype(jnp.float32) - view_two.astype(jnp.float32)
-    inv = inv_weight / (batch_rows * feature_count) * jnp.sum(view_diff * view_diff)
-
+    first, second = own[:half], own[half:]
+    up_first, down_second = move(first, UP), move(second, DOWN)
+    up_second, down_first = move(second, UP), move(first, DOWN)
+    far_first, far_second = move(up_first, UP), move(down_second, DOWN)
+    copies = (up_first, up_second, down_first, down_second, far_first, far_second)
     full_block = pl.BlockSpec((feature_parts, rows, chunk), lambda f: (0, 0, f))
     half_block = pl.BlockSpec((half, rows, chunk), lambda f: (0, 0, f))
     rounded, part, rest, share = pl.pallas_call(
         functools.partial(gram_kernel, sizes),
         grid=(steps,),
-        in_specs=[full_block, full_block, full_block, half_block, half_block],
+        in_specs=[smem, full_block] + [half_block] * len(copies),
         out_specs=[
             pl.BlockSpec((batch_rows, chunk), lambda f: (0, f)),
             pl.BlockSpec((feature_parts, rows, batch_rows), lambda f: (0, 0, 0)),
@@ -232,37 +236,36 @@
         ],
         scratch_shapes=[pltpu.VMEM((group_rows, batch_rows), jnp.float32)],
         out_shape=[
-            jax.ShapeDtypeStruct((batch_rows, width), jnp.bfloat16),
-            jax.ShapeDtypeStruct((feature_parts, rows, batch_rows), jnp.bfloat16),
+            pltpu.HBM((batch_rows, width), jnp.bfloat16),
+            pltpu.HBM((feature_parts, rows, batch_rows), jnp.bfloat16),
             jax.ShapeDtypeStruct((group_rows, width), jnp.float32),
             jax.ShapeDtypeStruct((1, width), jnp.float32),
         ],
-        compiler_params=params,
+        compiler_params=room(10),
         name="gram_part",
-    )(own, up, down, far_up, far_down)
+    )(inv, own, *copies)
 
     pieces = exchange(part)
     sent, scalar = pl.pallas_call(
         functools.partial(sum_kernel, sizes),
-        in_specs=[smem, smem, vmem, vmem],
+        in_specs=[smem, vmem, vmem],
         out_specs=[vmem, vmem],
         out_shape=[
-            jax.ShapeDtypeStruct((feature_parts, rows, batch_rows + LANES), jnp.bfloat16),
+            pltpu.HBM((feature_parts, rows, batch_rows + LANES), jnp.bfloat16),
             jax.ShapeDtypeStruct((8, LANES), jnp.float32),
         ],
-        compiler_params=params,
+        compiler_params=room(4),
         name="gram_sum",
-    )(place, inv.reshape(1), pieces, share)
+    )(place, pieces, share)
 
     gram = exchange(sent)
-    scalar = scalar + move(scalar, NEAR)
-    scalar = scalar + move(scalar, FAR)
+    scalars = [scalar] + [move(scalar, pairs) for pairs in (FAR, UP, DOWN)]
 
     grads = pl.pallas_call(
         functools.partial(grad_kernel, sizes),
         grid=(steps,),
-        in_specs=[
-            vmem,
+        in_specs=[vmem] * 4
+        + [
             pl.BlockSpec(sent.shape, lambda f: (0, 0, 0)),
             pl.BlockSpec((batch_rows, chunk), lambda f: (0, f)),
             pl.BlockSpec((group_rows, chunk), lambda f: (0, f)),
@@ -273,9 +276,9 @@
             pltpu.VMEM((group_rows, batch_rows), jnp.bfloat16),
             pltpu.VMEM((group_rows, LANES), jnp.float32),
         ],
-        compiler_params=params,
+        compiler_params=room(8),
         name="grad_rows",
-    )(scalar, gram, rounded, rest)
+    )(*scalars, gram, pltpu.with_memory_space_constraint(rounded, pltpu.HBM), rest)
 
     grads = exchange(grads)
     others = move(grads[:, shard_rows:], SWAP)
@@ -288,7 +291,7 @@
             jax.ShapeDtypeStruct(view_one.shape, jnp.float32),
             jax.ShapeDtypeStruct((1,), jnp.float32),
         ],
-        compiler_params=params,
+        compiler_params=room(4),
         name="add_pull",
     )(core, grads, others, view_one, view_two)
     return grad_one, grad_two, loss.reshape(())

time: 103 us -> 97 us (0.942)
  waiting for transfers between devices: 36.4 us -> 29.7 us
  local copies, waits for them, and re-layouts: 5.78 us -> 0.07 us
  starting transfers between devices: 14.6 us -> 19.8 us
  Pallas kernels: 7.3 us -> 11.6 us
  blocking collectives: 34.1 us -> 32.5 us
    ppermute x8 -> x11, waiting for transfers between devices: 26.1 us -> 16.4 us  [move(): return lax.ppermute(block, FINE, pairs)]
    unnamed x16 -> x4, local copies, waits for them, and re-layouts: 5.72 us -> 0.01 us
    ppermute x8 -> x11, starting transfers between devices: 6.51 us -> 11.7 us  [move(): return lax.ppermute(block, FINE, pairs)]
    all_to_all x2, waiting for transfers between devices: 10.3 us -> 13.3 us  [exchange(): lax.all_to_all(blocks, FINE, 0, 0, tiled=True, axis_index_groups=GROUPS)]
    all_to_all x2, blocking collectives: 34.1 us -> 32.5 us  [exchange(): lax.all_to_all(blocks, FINE, 0, 0, tiled=True, axis_index_groups=GROUPS)]
    pallas_call x1, Pallas kernels: 1.73 us -> 3.24 us  [body(): pl.pallas_call(functools.partial(grad_kernel, sizes), grid=(steps,), in_s...]
    pallas_call x2, Pallas kernels: 0.3 us -> 1.75 us  [the longest x1 1.02 us: body(): pl.pallas_call(functools.partial(sum_kernel, sizes), in_specs=[smem, vmem...]
    pallas_call x1, Pallas kernels: 4.12 us -> 5.48 us  [body(): pl.pallas_call(functools.partial(gram_kernel, sizes), grid=(steps,), in_s...]
  transfers between devices with their start and end apart: 10 -> 13, of which waited for: 9 -> 11; matrix products, arithmetic and copies ran while one was open for 1% -> 0% of each run, Pallas kernels for 0% -> 0%
where the time goes in v4:
time: 97 us; the launch traced here: 95.5 us
  blocking collectives  32.5 us (34%)
  waiting for transfers between devices  29.7 us (31%)
  starting transfers between devices  19.8 us (20%)
  Pallas kernels  11.6 us (12%)
  other arithmetic  1.07 us (1%)
    all_to_all x2, blocking collectives, exchange(): lax.all_to_all(blocks, FINE, 0, 0, tiled=True, axis_index_groups=GROUPS)  32.5 us
    ppermute x11, waiting for transfers between devices, move(): return lax.ppermute(block, FINE, pairs)  16.4 us
    all_to_all x2, waiting for transfers between devices, exchange(): lax.all_to_all(blocks, FINE, 0, 0, tiled=True, axis_index_groups=GROUPS)  13.3 us
    ppermute x11, starting transfers between devices, move(): return lax.ppermute(block, FINE, pairs)  11.7 us
    all_to_all x2, starting transfers between devices, exchange(): lax.all_to_all(blocks, FINE, 0, 0, tiled=True, axis_index_groups=GROUPS)  8.09 us
    pallas_call x1, Pallas kernels, body(): pl.pallas_call(functools.partial(gram_kernel, sizes), grid=(steps,), in_s...  5.48 us
    pallas_call x1, Pallas kernels, body(): pl.pallas_call(functools.partial(grad_kernel, sizes), grid=(steps,), in_s...  3.24 us
  transfers between devices with their start and end apart: 13, of which 11 were waited for; matrix products, arithmetic and copies ran while one was open for 0% of the time, Pallas kernels for 0%

profile of v4, /device:TPU:0, one launch (start us, length us, event | category | flops | bytes accessed | tf_op | source)
XLA Modules:
  0.0 95.5 jit_solution(5134254994125171895)
XLA Ops:
  0.6 1.1 %broadcast_select_fusion = (bf16[8,16384]{1,0:T(8,128)(2,1)S(1)}, bf16[8,16384]{1,0:T(8,128)(2,1)S(1)}) fusion(bf16[8,16384]{1,0:T(8,128)(2,1)} %view_two.1, bf16[8,16384]{1,0:T(8,128)(2,1)} %view_one.1, pred[]{:T(512)S(6)} %eq.2), kind=kLoop, calls=%fused_computation | loop fusion | flops 262144 | bytes 1048577 | tf_op jit(solution)/shard_map/jit(_where)/select_n | solution.py:62
  1.8 1.5 %collective-permute-done.got = bf16[8,16384]{1,0:T(8,128)(2,1)S(1)} collective-permute-done((bf16[8,16384]{1,0:T(8,128)(2,1)S(1)}, bf16[8,16384]{1,0:T(8,128)(2,1)S(1)}, u32[]{:S(2)}, u32[]{:S(2)}) %collective-permute-start) | collective-permute-done | bytes 262176 | tf_op jit(solution)/shard_map/ppermute | solution.py:54
  4.1 18.3 %all_to_all.20.own = bf16[16,16,1024]{2,1,0:T(8,128)(2,1)S(1)} all-to-all(bf16[16,16,1024]{2,1,0:T(8,128)(2,1)S(1)} %get-tuple-element.15), channel_id=1, replica_groups={{0,2,4,6,8,10,12,14,64,66,68,70,72,74,76,78},{16,18,20,22,24,26,28,30,8..., dimensions={0} | all-to-all | bytes 1048576 | tf_op jit(solution)/shard_map/all_to_all | solution.py:50
  22.4 2.5 %collective-permute-start.4 = (bf16[8,16,1024]{2,1,0:T(8,128)(2,1)S(1)}, bf16[8,16,1024]{2,1,0:T(8,128)(2,1)S(1)}, u32[]{:S(2)}, u32[]{:S(2)}) collective-permute-start(bf16[8,16,1024]{2,1,0:T(8,128)(2,1)S(1)} %get-tuple-element.25), channel_id=1, source_target_pairs={{16,0},{18,2},{20,4},{22,6},{24,8},{26,10},{28,12},{30,14},{80,64}... | collective-permute-start | bytes 786440 | tf_op jit(solution)/shard_map/ppermute | solution.py:54
  25.0 0.8 collective-permute-start.2
  25.7 2.5 %collective-permute-start.3 = (bf16[8,16,1024]{2,1,0:T(8,128)(2,1)S(1)}, bf16[8,16,1024]{2,1,0:T(8,128)(2,1)S(1)}, u32[]{:S(2)}, u32[]{:S(2)}) collective-permute-start(bf16[8,16,1024]{2,1,0:T(8,128)(2,1)S(1)} %get-tuple-element.26), channel_id=1, source_target_pairs={{16,0},{18,2},{20,4},{22,6},{24,8},{26,10},{28,12},{30,14},{80,64}... | collective-permute-start | bytes 786440 | tf_op jit(solution)/shard_map/ppermute | solution.py:54
  28.9 3.7 %collective-permute-start.6 = (bf16[8,16,1024]{2,1,0:T(8,128)(2,1)S(1)}, bf16[8,16,1024]{2,1,0:T(8,128)(2,1)S(1)}, u32[]{:S(2)}, u32[]{:S(2)}) collective-permute-start(bf16[8,16,1024]{2,1,0:T(8,128)(2,1)S(1)} %collective-permute-done.4.refs_3_), channel_id=1, source_target_pairs={{16,0},{18,2},{20,4},{22,6},{24,8},{26,10},{28,12},{30,14},{80,64}... | collective-permute-start | bytes 786440 | tf_op jit(solution)/shard_map/ppermute | solution.py:54
  32.5 2.8 %collective-permute-done.2.refs_1_ = bf16[8,16,1024]{2,1,0:T(8,128)(2,1)S(1)} collective-permute-done((bf16[8,16,1024]{2,1,0:T(8,128)(2,1)S(1)}, bf16[8,16,1024]{2,1,0:T(8,128)(2,1)S(1)}, u32[]{:S(2)}, u32[]{:S(2)}) %collective-permute-start.2) | collective-permute-done | bytes 262176 | tf_op jit(solution)/shard_map/ppermute | solution.py:54
  35.4 1.1 %collective-permute-done.6.refs_5_ = bf16[8,16,1024]{2,1,0:T(8,128)(2,1)S(1)} collective-permute-done((bf16[8,16,1024]{2,1,0:T(8,128)(2,1)S(1)}, bf16[8,16,1024]{2,1,0:T(8,128)(2,1)S(1)}, u32[]{:S(2)}, u32[]{:S(2)}) %collective-permute-start.6) | collective-permute-done | bytes 262176 | tf_op jit(solution)/shard_map/ppermute | solution.py:54
  36.4 3.7 %collective-permute-done.5.refs_4_ = bf16[8,16,1024]{2,1,0:T(8,128)(2,1)S(1)} collective-permute-done((bf16[8,16,1024]{2,1,0:T(8,128)(2,1)S(1)}, bf16[8,16,1024]{2,1,0:T(8,128)(2,1)S(1)}, u32[]{:S(2)}, u32[]{:S(2)}) %collective-permute-start.5) | collective-permute-done | bytes 262176 | tf_op jit(solution)/shard_map/ppermute | solution.py:54
  40.1 5.5 %gram_part.1 = (bf16[1024,1024]{1,0:T(8,128)(2,1)}, bf16[16,16,1024]{2,1,0:T(8,128)(2,1)}, f32[256,1024]{1,0:T(8,128)S(1)}, f32[1,1024]{1,0:T(1,128)S(1)}) custom-call(f32[1]{0:T(128)} %get-tuple-element.14.inv, bf16[16,16,1024]{2,1,0:T(8,128)(2,1)S(1)} %all_to_all.20.own, bf16[8,16,1024]{2,1,0:T(8,128)(2,1)S(1)} %collective-permute-done.1.refs_0_, ...), custom_call_target="tpu_custom_call" | custom-call | tf_op jit(solution)/shard_map/gram_part/pallas_call | solution.py:227
  45.6 4.5 %all-to-all-start.1 = ((bf16[16,16,1024]{2,1,0:T(8,128)(2,1)}), bf16[16,16,1024]{2,1,0:T(8,128)(2,1)S(1)}, u32[]{:S(2)}, u32[]{:S(2)}) async-start(bf16[16,16,1024]{2,1,0:T(8,128)(2,1)} %get-tuple-element.16), calls=%async_computation.1 | async-start | bytes 1048576 | tf_op jit(solution)/shard_map/all_to_all | solution.py:50
  50.1 10.1 %all-to-all-done.1.pieces = bf16[16,16,1024]{2,1,0:T(8,128)(2,1)S(1)} async-done(((bf16[16,16,1024]{2,1,0:T(8,128)(2,1)}), bf16[16,16,1024]{2,1,0:T(8,128)(2,1)S(1)}, u32[]{:S(2)}, u32[]{:S(2)}) %all-to-all-start.1) | async-done | bytes 524320 | tf_op jit(solution)/shard_map/all_to_all | solution.py:50
  60.2 1.0 %gram_sum.1 = (bf16[16,16,1152]{2,1,0:T(8,128)(2,1)}, f32[8,128]{1,0:T(8,128)S(1)}) custom-call(s32[1]{0:T(128)} %bitcast.1.place, bf16[16,16,1024]{2,1,0:T(8,128)(2,1)S(1)} %all-to-all-done.1.pieces, f32[1,1024]{1,0:T(1,128)S(1)} %get-tuple-element.17.share), custom_call_target="tpu_custom_call" | custom-call | tf_op jit(solution)/shard_map/gram_sum/pallas_call | solution.py:249
  61.2 3.6 %all-to-all-start.2 = ((bf16[16,16,1152]{2,1,0:T(8,128)(2,1)}), bf16[16,16,1152]{2,1,0:T(8,128)(2,1)S(1)}, u32[]{:S(2)}, u32[]{:S(2)}) async-start(bf16[16,16,1152]{2,1,0:T(8,128)(2,1)} %get-tuple-element.19), calls=%async_computation.2 | async-start | bytes 1179648 | tf_op jit(solution)/shard_map/all_to_all | solution.py:50
  64.9 2.0 %collective-permute-start.8 = (f32[8,128]{1,0:T(8,128)S(1)}, f32[8,128]{1,0:T(8,128)S(1)}, u32[]{:S(2)}, u32[]{:S(2)}) collective-permute-start(f32[8,128]{1,0:T(8,128)S(1)} %get-tuple-element.18.here), channel_id=1, source_target_pairs={{48,0},{50,2},{52,4},{54,6},{56,8},{58,10},{60,12},{62,14},{112,64... | collective-permute-start | bytes 12296 | tf_op jit(solution)/shard_map/ppermute | solution.py:54
  66.9 1.6 %collective-permute-done.9.after = f32[8,128]{1,0:T(8,128)S(1)} collective-permute-done((f32[8,128]{1,0:T(8,128)S(1)}, f32[8,128]{1,0:T(8,128)S(1)}, u32[]{:S(2)}, u32[]{:S(2)}) %collective-permute-start.9) | collective-permute-done | bytes 4128 | tf_op jit(solution)/shard_map/ppermute | solution.py:54
  68.5 1.3 %collective-permute-done.8.before = f32[8,128]{1,0:T(8,128)S(1)} collective-permute-done((f32[8,128]{1,0:T(8,128)S(1)}, f32[8,128]{1,0:T(8,128)S(1)}, u32[]{:S(2)}, u32[]{:S(2)}) %collective-permute-start.8) | collective-permute-done | bytes 4128 | tf_op jit(solution)/shard_map/ppermute | solution.py:54
  69.8 2.2 %collective-permute-done.7.far = f32[8,128]{1,0:T(8,128)S(1)} collective-permute-done((f32[8,128]{1,0:T(8,128)S(1)}, f32[8,128]{1,0:T(8,128)S(1)}, u32[]{:S(2)}, u32[]{:S(2)}) %collective-permute-start.7) | collective-permute-done | bytes 4128 | tf_op jit(solution)/shard_map/ppermute | solution.py:54
  72.0 3.2 %all-to-all-done.2.gram = bf16[16,16,1152]{2,1,0:T(8,128)(2,1)S(1)} async-done(((bf16[16,16,1152]{2,1,0:T(8,128)(2,1)}), bf16[16,16,1152]{2,1,0:T(8,128)(2,1)S(1)}, u32[]{:S(2)}, u32[]{:S(2)}) %all-to-all-start.2) | async-done | bytes 589856 | tf_op jit(solution)/shard_map/all_to_all | solution.py:50
  75.3 3.2 %grad_rows.1 = bf16[16,16,1152]{2,1,0:T(8,128)(2,1)S(1)} custom-call(f32[8,128]{1,0:T(8,128)S(1)} %get-tuple-element.18.here, f32[8,128]{1,0:T(8,128)S(1)} %collective-permute-done.7.far, f32[8,128]{1,0:T(8,128)S(1)} %collective-permute-done.8.before, f32[8,128]{1,0:T(8,128)S(1)} %collective-permute-done.9.after, ...), custom_call_target="tpu_custom_call" | custom-call | tf_op jit(solution)/shard_map/grad_rows/pallas_call | solution.py:264
  78.5 14.1 %all_to_all.21.recv = bf16[16,16,1152]{2,1,0:T(8,128)(2,1)S(1)} all-to-all(bf16[16,16,1152]{2,1,0:T(8,128)(2,1)S(1)} %grad_rows.1), channel_id=1, replica_groups={{0,2,4,6,8,10,12,14,64,66,68,70,72,74,76,78},{16,18,20,22,24,26,28,30,8..., dimensions={0} | all-to-all | bytes 1179648 | tf_op jit(solution)/shard_map/all_to_all | solution.py:50
  92.8 1.6 %collective-permute-done.10.got = bf16[16,8,1152]{2,1,0:T(8,128)(2,1)S(1)} collective-permute-done((bf16[16,8,1152]{2,1,0:T(8,128)(2,1)S(1)}, bf16[16,8,1152]{2,1,0:T(8,128)(2,1)S(1)}, u32[]{:S(2)}, u32[]{:S(2)}) %collective-permute-start.10) | collective-permute-done | bytes 294944 | tf_op jit(solution)/shard_map/ppermute | solution.py:54
  94.3 1.2 %add_pull.1 = (f32[8,16384]{1,0:T(8,128)}, f32[8,16384]{1,0:T(8,128)}, f32[1]{0:T(128)}) custom-call(s32[1]{0:T(128)} %bitcast.core, bf16[16,16,1152]{2,1,0:T(8,128)(2,1)S(1)} %all_to_all.21.recv, bf16[16,8,1152]{2,1,0:T(8,128)(2,1)S(1)} %collective-permute-done.10.got, bf16[8,16384]{1,0:T(8,128)(2,1)S(1)} %copy-done.1, bf16[8,16384]{1,0:T(8,128)(2,1)S(1)} %copy-done), custom_call_target="tpu_custom_call" | custom-call | tf_op jit(solution)/shard_map/add_pull/pallas_call | solution.py:285
  (16 shorter events, 1.7 us)
Async XLA Ops:
  1.7 1.6 %collective-permute-start = (bf16[8,16384]{1,0:T(8,128)(2,1)S(1)}, bf16[8,16384]{1,0:T(8,128)(2,1)S(1)}, u32[]{:S(2)}, u32[]{:S(2)}) collective-permute-start(bf16[8,16384]{1,0:T(8,128)(2,1)S(1)} %get-tuple-element.27.give), channel_id=1, source_target_pairs={{0,1},{1,0},{2,3},{3,2},{4,5},{5,4},{6,7},{7,6},{8,9},{9,8},{10,11... | collective-permute-start | bytes 786440 | tf_op jit(solution)/shard_map/ppermute | solution.py:54
  22.4 6.4 %collective-permute-start.4 = (bf16[8,16,1024]{2,1,0:T(8,128)(2,1)S(1)}, bf16[8,16,1024]{2,1,0:T(8,128)(2,1)S(1)}, u32[]{:S(2)}, u32[]{:S(2)}) collective-permute-start(bf16[8,16,1024]{2,1,0:T(8,128)(2,1)S(1)} %get-tuple-element.25), channel_id=1, source_target_pairs={{16,0},{18,2},{20,4},{22,6},{24,8},{26,10},{28,12},{30,14},{80,64}... | collective-permute-start | bytes 786440 | tf_op jit(solution)/shard_map/ppermute | solution.py:54
  25.0 7.6 %collective-permute-start.1 = (bf16[8,16,1024]{2,1,0:T(8,128)(2,1)S(1)}, bf16[8,16,1024]{2,1,0:T(8,128)(2,1)S(1)}, u32[]{:S(2)}, u32[]{:S(2)}) collective-permute-start(bf16[8,16,1024]{2,1,0:T(8,128)(2,1)S(1)} %get-tuple-element.26), channel_id=1, source_target_pairs={{48,0},{50,2},{52,4},{54,6},{56,8},{58,10},{60,12},{62,14},{112,64... | collective-permute-start | bytes 786440 | tf_op jit(solution)/shard_map/ppermute | solution.py:54
  25.0 10.4 %collective-permute-start.2 = (bf16[8,16,1024]{2,1,0:T(8,128)(2,1)S(1)}, bf16[8,16,1024]{2,1,0:T(8,128)(2,1)S(1)}, u32[]{:S(2)}, u32[]{:S(2)}) collective-permute-start(bf16[8,16,1024]{2,1,0:T(8,128)(2,1)S(1)} %get-tuple-element.25), channel_id=1, source_target_pairs={{48,0},{50,2},{52,4},{54,6},{56,8},{58,10},{60,12},{62,14},{112,64... | collective-permute-start | bytes 786440 | tf_op jit(solution)/shard_map/ppermute | solution.py:54
  25.7 9.6 %collective-permute-start.3 = (bf16[8,16,1024]{2,1,0:T(8,128)(2,1)S(1)}, bf16[8,16,1024]{2,1,0:T(8,128)(2,1)S(1)}, u32[]{:S(2)}, u32[]{:S(2)}) collective-permute-start(bf16[8,16,1024]{2,1,0:T(8,128)(2,1)S(1)} %get-tuple-element.26), channel_id=1, source_target_pairs={{16,0},{18,2},{20,4},{22,6},{24,8},{26,10},{28,12},{30,14},{80,64}... | collective-permute-start | bytes 786440 | tf_op jit(solution)/shard_map/ppermute | solution.py:54
  28.9 7.5 %collective-permute-start.6 = (bf16[8,16,1024]{2,1,0:T(8,128)(2,1)S(1)}, bf16[8,16,1024]{2,1,0:T(8,128)(2,1)S(1)}, u32[]{:S(2)}, u32[]{:S(2)}) collective-permute-start(bf16[8,16,1024]{2,1,0:T(8,128)(2,1)S(1)} %collective-permute-done.4.refs_3_), channel_id=1, source_target_pairs={{16,0},{18,2},{20,4},{22,6},{24,8},{26,10},{28,12},{30,14},{80,64}... | collective-permute-start | bytes 786440 | tf_op jit(solution)/shard_map/ppermute | solution.py:54
  32.5 7.6 %collective-permute-start.5 = (bf16[8,16,1024]{2,1,0:T(8,128)(2,1)S(1)}, bf16[8,16,1024]{2,1,0:T(8,128)(2,1)S(1)}, u32[]{:S(2)}, u32[]{:S(2)}) collective-permute-start(bf16[8,16,1024]{2,1,0:T(8,128)(2,1)S(1)} %collective-permute-done.1.refs_0_), channel_id=1, source_target_pairs={{48,0},{50,2},{52,4},{54,6},{56,8},{58,10},{60,12},{62,14},{112,64... | collective-permute-start | bytes 786440 | tf_op jit(solution)/shard_map/ppermute | solution.py:54
  45.6 14.6 %all-to-all-start.1 = ((bf16[16,16,1024]{2,1,0:T(8,128)(2,1)}), bf16[16,16,1024]{2,1,0:T(8,128)(2,1)S(1)}, u32[]{:S(2)}, u32[]{:S(2)}) async-start(bf16[16,16,1024]{2,1,0:T(8,128)(2,1)} %get-tuple-element.16), calls=%async_computation.1 | async-start | bytes 1048576 | tf_op jit(solution)/shard_map/all_to_all | solution.py:50
  61.2 14.0 %all-to-all-start.2 = ((bf16[16,16,1152]{2,1,0:T(8,128)(2,1)}), bf16[16,16,1152]{2,1,0:T(8,128)(2,1)S(1)}, u32[]{:S(2)}, u32[]{:S(2)}) async-start(bf16[16,16,1152]{2,1,0:T(8,128)(2,1)} %get-tuple-element.19), calls=%async_computation.2 | async-start | bytes 1179648 | tf_op jit(solution)/shard_map/all_to_all | solution.py:50
  64.8 3.7 %collective-permute-start.9 = (f32[8,128]{1,0:T(8,128)S(1)}, f32[8,128]{1,0:T(8,128)S(1)}, u32[]{:S(2)}, u32[]{:S(2)}) collective-permute-start(f32[8,128]{1,0:T(8,128)S(1)} %get-tuple-element.18.here), channel_id=1, source_target_pairs={{16,0},{18,2},{20,4},{22,6},{24,8},{26,10},{28,12},{30,14},{80,64}... | collective-permute-start | bytes 12296 | tf_op jit(solution)/shard_map/ppermute | solution.py:54
  64.9 4.9 %collective-permute-start.8 = (f32[8,128]{1,0:T(8,128)S(1)}, f32[8,128]{1,0:T(8,128)S(1)}, u32[]{:S(2)}, u32[]{:S(2)}) collective-permute-start(f32[8,128]{1,0:T(8,128)S(1)} %get-tuple-element.18.here), channel_id=1, source_target_pairs={{48,0},{50,2},{52,4},{54,6},{56,8},{58,10},{60,12},{62,14},{112,64... | collective-permute-start | bytes 12296 | tf_op jit(solution)/shard_map/ppermute | solution.py:54
  66.9 5.1 %collective-permute-start.7 = (f32[8,128]{1,0:T(8,128)S(1)}, f32[8,128]{1,0:T(8,128)S(1)}, u32[]{:S(2)}, u32[]{:S(2)}) collective-permute-start(f32[8,128]{1,0:T(8,128)S(1)} %get-tuple-element.18.here), channel_id=1, source_target_pairs={{32,0},{34,2},{36,4},{38,6},{40,8},{42,10},{44,12},{46,14},{96,64}... | collective-permute-start | bytes 12296 | tf_op jit(solution)/shard_map/ppermute | solution.py:54
  75.2 19.1 %copy-start = (bf16[8,16384]{1,0:T(8,128)(2,1)S(1)}, bf16[8,16384]{1,0:T(8,128)(2,1)}, u32[]{:S(2)}) copy-start(bf16[8,16384]{1,0:T(8,128)(2,1)} %view_two.1) | copy-start | bytes 786436
  75.2 19.1 %copy-start.1 = (bf16[8,16384]{1,0:T(8,128)(2,1)S(1)}, bf16[8,16384]{1,0:T(8,128)(2,1)}, u32[]{:S(2)}) copy-start(bf16[8,16384]{1,0:T(8,128)(2,1)} %view_one.1) | copy-start | bytes 786436
  92.7 1.7 %collective-permute-start.10 = (bf16[16,8,1152]{2,1,0:T(8,128)(2,1)S(1)}, bf16[16,8,1152]{2,1,0:T(8,128)(2,1)S(1)}, u32[]{:S(2)}, u32[]{:S(2)}) collective-permute-start(bf16[16,8,1152]{2,1,0:T(8,128)(2,1)S(1)} %slice.14), channel_id=1, source_target_pairs={{0,1},{1,0},{2,3},{3,2},{4,5},{5,4},{6,7},{7,6},{8,9},{9,8},{10,11... | collective-permute-start | bytes 884744 | tf_op jit(solution)/shard_map/ppermute | solution.py:54

commit v5 on v4

v5 whole, which is shorter than its diff:
```python
import functools

import jax
import jax.numpy as jnp
import numpy as np
from jax import lax
from jax.experimental import pallas as pl
from jax.experimental.pallas import tpu as pltpu
from jax.sharding import Mesh
from jax.sharding import PartitionSpec as P

epsilon = 0.0001
inv_weight = 25.0
var_weight = 25.0
cov_weight = 1.0
out_scale = 25.0

FINE = ("zh", "x", "y", "zl", "core")
SIZES = (2, 4, 4, 2, 2)
LANES = 128
CHUNK = 256
CONTRACT_LAST = (((1,), (1,)), ((), ()))
CONTRACT_FIRST = (((1,), (0,)), ((), ()))

IDS = np.arange(128).reshape(SIZES)
BY_RING = np.stack(
    [
        IDS[..., 0].transpose(1, 0, 2, 3).reshape(4, 16),
        IDS[..., 1].transpose(2, 0, 1, 3).reshape(4, 16),
    ]
)
GROUPS = [[int(i) for i in g] for core in BY_RING for g in core]
SWAP = [(int(i), int(i) ^ 1) for i in IDS.reshape(-1)]


def along_ring(source):
    return [
        (int(BY_RING[k, source[i], c]), int(BY_RING[k, i, c]))
        for k in range(2)
        for i in range(4)
        for c in range(16)
    ]


UP = along_ring((3, 0, 1, 2))
DOWN = along_ring((1, 2, 3, 0))
FAR = along_ring((2, 3, 0, 1))


def exchange(blocks):
    return lax.all_to_all(blocks, FINE, 0, 0, tiled=True, axis_index_groups=GROUPS)


def move(block, pairs):
    return lax.ppermute(block, FINE, pairs)


def room(mebibytes):
    return pltpu.CompilerParams(vmem_limit_bytes=mebibytes * 1024 * 1024)


def pick(core, first, second):
    return jnp.where(core == 0, first, second)


def pack_kernel(factor, place_in, keep, give, got, packed, inv, place):
    parts, rows, width = packed.shape
    place[0] = place_in[0]
    squares = 0.0
    for c in range(parts):
        cut = pl.ds(c * width, width)
        mine, other, more = [ref[:, cut].astype(jnp.float32) for ref in (keep, give, got)]
        packed[c] = jnp.concatenate([mine, more], axis=0).astype(jnp.bfloat16)
        squares += (mine - other) ** 2
    inv[0] = factor * jnp.sum(squares)


def gram_kernel(sizes, inv, own, *refs):
    copies, (rounded, part, stats) = refs[:-3], refs[-3:]
    batch_rows, feature_count, row_parts = sizes
    group_rows = batch_rows // row_parts
    width = own.shape[2]
    for start in range(0, width, CHUNK):
        cut = pl.ds(start, CHUNK)
        values = [ref[:, :, cut].reshape(-1, CHUNK).astype(jnp.float32) for ref in (own,) + copies]
        mean = sum(jnp.sum(a, axis=0, keepdims=True) for a in values) / batch_rows
        values = [a - mean for a in values]
        square = sum(jnp.sum(a * a, axis=0, keepdims=True) for a in values)
        spread = jnp.sqrt(square / (batch_rows - 1) + epsilon)
        energy = 0.0
        row = 0
        for a in values:
            a = a.astype(jnp.bfloat16)
            rounded[pl.ds(row, a.shape[0]), cut] = a
            row += a.shape[0]
            a = a.astype(jnp.float32)
            energy += jnp.sum(a * a, axis=0, keepdims=True)
        share = var_weight / feature_count / row_parts * jnp.maximum(1.0 - spread, 0.0)
        share -= cov_weight / feature_count / row_parts * (energy / (batch_rows - 1)) ** 2
        share += inv[0] / width
        stats[0:1, cut] = mean
        stats[1:2, cut] = energy
        stats[2:3, cut] = jnp.where(spread < 1.0, 1.0 / spread, 0.0)
        stats[3:4, cut] = share
    product = lax.dot_general(
        rounded[pl.ds(0, group_rows)], rounded[...], CONTRACT_LAST, preferred_element_type=jnp.float32
    )
    part[...] = product.astype(jnp.bfloat16).reshape(part.shape)


def sum_kernel(sizes, place, pieces, stats, sent, scalar):
    batch_rows, feature_count, row_parts = sizes
    rows = pieces.shape[1]
    summed = jnp.sum(pieces[...].astype(jnp.float32), axis=0)
    shape = summed.shape
    lane = lax.broadcasted_iota(jnp.int32, shape, 1)
    row = lax.broadcasted_iota(jnp.int32, shape, 0)
    short = summed.astype(jnp.bfloat16).astype(jnp.float32)
    on_diagonal = lane == place[0] * rows + row
    lost = jnp.sum(jnp.where(on_diagonal, summed - short, 0.0), axis=1, keepdims=True)
    extra = jnp.broadcast_to(lost, (rows, LANES))
    out = jnp.concatenate([short, extra], axis=1).astype(jnp.bfloat16)
    sent[...] = jnp.broadcast_to(out[None], sent.shape)
    factor = cov_weight / feature_count / (batch_rows - 1) ** 2
    value = factor * jnp.sum(summed * summed) + jnp.sum(stats[3:4])
    scalar[...] = jnp.full(scalar.shape, value, jnp.float32)


def grad_kernel(sizes, here, far, before, after, gram, rounded, own, stats, sent):
    batch_rows, feature_count, row_parts = sizes
    parts, rows, width = own.shape
    group_rows = parts * rows
    factor_cov = 4.0 * cov_weight * batch_rows / (batch_rows - 1) ** 2 / out_scale
    factor_var = var_weight * batch_rows / (batch_rows - 1) / out_scale
    scalar = (here[0:1] + far[0:1]) + (before[0:1] + after[0:1])
    value = jnp.broadcast_to(scalar, (rows, LANES))
    high = value.astype(jnp.bfloat16).astype(jnp.float32)
    middle = (value - high).astype(jnp.bfloat16).astype(jnp.float32)
    low = value - high - middle
    lane = lax.broadcasted_iota(jnp.int32, value.shape, 1)
    three = jnp.where(lane == 0, high, jnp.where(lane == 1, middle, low)).astype(jnp.bfloat16)
    sent[:, :, pl.ds(width, LANES)] = jnp.broadcast_to(three[None], (parts, rows, LANES))

    matrix = gram[:, :, pl.ds(0, batch_rows)].reshape(group_rows, batch_rows)
    lost = gram[:, :, pl.ds(batch_rows, LANES)].reshape(group_rows, LANES).astype(jnp.float32)[:, 0:1]
    for start in range(0, width, CHUNK):
        cut = pl.ds(start, CHUNK)
        product = lax.dot_general(
            matrix, rounded[:, cut], CONTRACT_FIRST, preferred_element_type=jnp.float32
        )
        mine = rounded[pl.ds(0, group_rows), cut].astype(jnp.float32)
        centered = own[:, :, cut].reshape(group_rows, CHUNK).astype(jnp.float32) - stats[0:1, cut]
        product = product + (lost - stats[1:2, cut]) * mine
        grad = factor_cov * product - factor_var * stats[2:3, cut] * centered
        sent[:, :, cut] = grad.astype(jnp.bfloat16).reshape(parts, rows, CHUNK)


def final_kernel(core, recv, got, view_one, view_two, grad_one, grad_two, loss):
    parts, rows, width = got.shape
    width -= LANES
    push = 2.0 * inv_weight / out_scale
    sums = 0.0
    for c in range(parts):
        mine = recv[c].astype(jnp.float32)[:rows]
        other = got[c].astype(jnp.float32)
        cut = pl.ds(c * width, width)
        diff = push * (view_one[:, cut].astype(jnp.float32) - view_two[:, cut].astype(jnp.float32))
        grad_one[:, cut] = pick(core[0], mine[:, :width], other[:, :width]) + diff
        grad_two[:, cut] = pick(core[0], other[:, :width], mine[:, :width]) - diff
        sums += mine[:, width:] + other[:, width:]
    lane = lax.broadcasted_iota(jnp.int32, sums.shape, 1)
    row = lax.broadcasted_iota(jnp.int32, sums.shape, 0)
    loss[0] = jnp.sum(jnp.where((lane < 3) & (row == 0), sums, 0.0))


def body(view_one, view_two):
    shard_rows, feature_count = view_one.shape
    row_parts, feature_parts = BY_RING.shape[1:]
    batch_rows = shard_rows * 2 * row_parts * feature_parts
    group_rows = batch_rows // row_parts
    width = feature_count // feature_parts
    rows = 2 * shard_rows
    sizes = (batch_rows, feature_count, row_parts)
    core = lax.axis_index("core")
    across = pick(core, lax.axis_index("y"), lax.axis_index("x"))
    place = (lax.axis_index("zh") * 4 + across) * 2 + lax.axis_index("zl")
    core = core.astype(jnp.int32).reshape(1)
    place = place.astype(jnp.int32).reshape(1)
    smem = pl.BlockSpec(memory_space=pltpu.SMEM)
    vmem = pl.BlockSpec(memory_space=pltpu.VMEM)

    keep, give = pick(core[0], view_one, view_two), pick(core[0], view_two, view_one)
    blocks, inv, place = pl.pallas_call(
        functools.partial(pack_kernel, inv_weight / (batch_rows * feature_count)),
        in_specs=[smem, vmem, vmem, vmem],
        out_specs=[vmem, smem, smem],
        out_shape=[
            jax.ShapeDtypeStruct((feature_parts, rows, width), jnp.bfloat16),
            jax.ShapeDtypeStruct((1,), jnp.float32),
            jax.ShapeDtypeStruct((1,), jnp.int32),
        ],
        compiler_params=room(4),
        name="pack_rows",
    )(place, keep, give, move(give, SWAP))
    own = exchange(blocks)
    half = feature_parts // 2
    first, second = own[:half], own[half:]
    up_first, down_second = move(first, UP), move(second, DOWN)
    up_second, down_first = move(second, UP), move(first, DOWN)
    far_first, far_second = move(up_first, UP), move(down_second, DOWN)
    copies = (up_first, up_second, down_first, down_second, far_first, far_second)
    rounded, part, stats = pl.pallas_call(
        functools.partial(gram_kernel, sizes),
        in_specs=[smem, vmem] + [vmem] * len(copies),
        out_specs=[vmem, vmem, vmem],
        out_shape=[
            jax.ShapeDtypeStruct((batch_rows, width), jnp.bfloat16),
            jax.ShapeDtypeStruct((feature_parts, rows, batch_rows), jnp.bfloat16),
            jax.ShapeDtypeStruct((4, width), jnp.float32),
        ],
        compiler_params=room(24),
        name="gram_part",
    )(inv, own, *copies)

    pieces = exchange(part)
    sent, scalar = pl.pallas_call(
        functools.partial(sum_kernel, sizes),
        in_specs=[smem, vmem, vmem],
        out_specs=[vmem, vmem],
        out_shape=[
            pltpu.HBM((feature_parts, rows, batch_rows + LANES), jnp.bfloat16),
            jax.ShapeDtypeStruct((8, LANES), jnp.float32),
        ],
        compiler_params=room(4),
        name="gram_sum",
    )(place, pieces, stats)

    gram = exchange(sent)
    scalars = [scalar] + [move(scalar, pairs) for pairs in (FAR, UP, DOWN)]

    grads = pl.pallas_call(
        functools.partial(grad_kernel, sizes),
        in_specs=[vmem] * 8,
        out_specs=vmem,
        out_shape=jax.ShapeDtypeStruct((feature_parts, rows, width + LANES), jnp.bfloat16),
        compiler_params=room(16),
        name="grad_rows",
    )(*scalars, gram, rounded, own, stats)

    grads = exchange(grads)
    others = move(grads[:, shard_rows:], SWAP)
    grad_one, grad_two, loss = pl.pallas_call(
        final_kernel,
        in_specs=[smem, vmem, vmem, vmem, vmem],
        out_specs=[vmem, vmem, smem],
        out_shape=[
            jax.ShapeDtypeStruct(view_one.shape, jnp.float32),
            jax.ShapeDtypeStruct(view_one.shape, jnp.float32),
            jax.ShapeDtypeStruct((1,), jnp.float32),
        ],
        compiler_params=room(4),
        name="add_pull",
    )(core, grads, others, view_one, view_two)
    return grad_one, grad_two, loss.reshape(())


def solution(mesh):
    fine = Mesh(np.asarray(mesh.devices).reshape(SIZES), FINE)
    rows = P(FINE, None)
    return jax.shard_map(
        body, mesh=fine, in_specs=(rows, rows), out_specs=(rows, rows, P()), check_vma=False
    )
```

time: 97 us -> 92.3 us (0.952)
  blocking collectives: 32.5 us -> 46.9 us
  waiting for transfers between devices: 29.7 us -> 19.6 us
  starting transfers between devices: 19.8 us -> 15.3 us
  Pallas kernels: 11.6 us -> 7.19 us
    all_to_all x2 -> x3, blocking collectives: 32.5 us -> 46.9 us  [exchange(): lax.all_to_all(blocks, FINE, 0, 0, tiled=True, axis_index_groups=GROUPS)]
    all_to_all x2 -> x1, waiting for transfers between devices: 13.3 us -> 3.2 us  [exchange(): lax.all_to_all(blocks, FINE, 0, 0, tiled=True, axis_index_groups=GROUPS)]
    pallas_call x2, Pallas kernels: 8.72 us -> 3.64 us  [the longest x1 2.81 us: body(): pl.pallas_call(functools.partial(gram_kernel, sizes), in_specs=[smem, vme...]
    all_to_all x2 -> x1, starting transfers between devices: 8.09 us -> 3.58 us  [exchange(): lax.all_to_all(blocks, FINE, 0, 0, tiled=True, axis_index_groups=GROUPS)]
  transfers between devices with their start and end apart: 13 -> 12, of which waited for: 11 -> 10; matrix products, arithmetic and copies ran while one was open for 0% -> 0% of each run, Pallas kernels for 0% -> 0%
where the time goes in v5:
time: 92.3 us; the launch traced here: 90.9 us
  blocking collectives  46.9 us (51%)
  waiting for transfers between devices  19.6 us (21%)
  starting transfers between devices  15.3 us (17%)
  Pallas kernels  7.19 us (8%)
  other arithmetic  1.07 us (1%)
    all_to_all x3, blocking collectives, exchange(): lax.all_to_all(blocks, FINE, 0, 0, tiled=True, axis_index_groups=GROUPS)  46.9 us
    ppermute x11, waiting for transfers between devices, move(): return lax.ppermute(block, FINE, pairs)  16.4 us
    ppermute x11, starting transfers between devices, move(): return lax.ppermute(block, FINE, pairs)  11.7 us
    all_to_all x1, starting transfers between devices, exchange(): lax.all_to_all(blocks, FINE, 0, 0, tiled=True, axis_index_groups=GROUPS)  3.58 us
    all_to_all x1, waiting for transfers between devices, exchange(): lax.all_to_all(blocks, FINE, 0, 0, tiled=True, axis_index_groups=GROUPS)  3.2 us
    pallas_call x1, Pallas kernels, body(): pl.pallas_call(functools.partial(gram_kernel, sizes), in_specs=[smem, vme...  2.81 us
  transfers between devices with their start and end apart: 12, of which 10 were waited for; matrix products, arithmetic and copies ran while one was open for 0% of the time, Pallas kernels for 0%

profile of v5, /device:TPU:0, one launch (start us, length us, event | category | flops | bytes accessed | tf_op | source)
XLA Modules:
  0.0 90.9 jit_solution(283826221987456570)
XLA Ops:
  0.6 1.1 %broadcast_select_fusion = (bf16[8,16384]{1,0:T(8,128)(2,1)S(1)}, bf16[8,16384]{1,0:T(8,128)(2,1)S(1)}) fusion(bf16[8,16384]{1,0:T(8,128)(2,1)} %view_two.1, bf16[8,16384]{1,0:T(8,128)(2,1)} %view_one.1, pred[]{:T(512)S(6)} %eq.2), kind=kLoop, calls=%fused_computation | loop fusion | flops 262144 | bytes 1048577 | tf_op jit(solution)/shard_map/jit(_where)/select_n | solution.py:63
  1.8 1.5 %collective-permute-done.got = bf16[8,16384]{1,0:T(8,128)(2,1)S(1)} collective-permute-done((bf16[8,16384]{1,0:T(8,128)(2,1)S(1)}, bf16[8,16384]{1,0:T(8,128)(2,1)S(1)}, u32[]{:S(2)}, u32[]{:S(2)}) %collective-permute-start) | collective-permute-done | bytes 262176 | tf_op jit(solution)/shard_map/ppermute | solution.py:55
  3.3 0.7 pack_rows.1
  4.1 18.3 %all_to_all.20.own = bf16[16,16,1024]{2,1,0:T(8,128)(2,1)S(1)} all-to-all(bf16[16,16,1024]{2,1,0:T(8,128)(2,1)S(1)} %get-tuple-element.16), channel_id=1, replica_groups={{0,2,4,6,8,10,12,14,64,66,68,70,72,74,76,78},{16,18,20,22,24,26,28,30,8..., dimensions={0} | all-to-all | bytes 1048576 | tf_op jit(solution)/shard_map/all_to_all | solution.py:51
  22.5 2.5 %collective-permute-start.4 = (bf16[8,16,1024]{2,1,0:T(8,128)(2,1)S(1)}, bf16[8,16,1024]{2,1,0:T(8,128)(2,1)S(1)}, u32[]{:S(2)}, u32[]{:S(2)}) collective-permute-start(bf16[8,16,1024]{2,1,0:T(8,128)(2,1)S(1)} %get-tuple-element.25), channel_id=1, source_target_pairs={{16,0},{18,2},{20,4},{22,6},{24,8},{26,10},{28,12},{30,14},{80,64}... | collective-permute-start | bytes 786440 | tf_op jit(solution)/shard_map/ppermute | solution.py:55
  25.0 0.8 collective-permute-start.2
  25.7 2.5 %collective-permute-start.3 = (bf16[8,16,1024]{2,1,0:T(8,128)(2,1)S(1)}, bf16[8,16,1024]{2,1,0:T(8,128)(2,1)S(1)}, u32[]{:S(2)}, u32[]{:S(2)}) collective-permute-start(bf16[8,16,1024]{2,1,0:T(8,128)(2,1)S(1)} %get-tuple-element.26), channel_id=1, source_target_pairs={{16,0},{18,2},{20,4},{22,6},{24,8},{26,10},{28,12},{30,14},{80,64}... | collective-permute-start | bytes 786440 | tf_op jit(solution)/shard_map/ppermute | solution.py:55
  28.9 3.7 %collective-permute-start.6 = (bf16[8,16,1024]{2,1,0:T(8,128)(2,1)S(1)}, bf16[8,16,1024]{2,1,0:T(8,128)(2,1)S(1)}, u32[]{:S(2)}, u32[]{:S(2)}) collective-permute-start(bf16[8,16,1024]{2,1,0:T(8,128)(2,1)S(1)} %collective-permute-done.4.refs_3_), channel_id=1, source_target_pairs={{16,0},{18,2},{20,4},{22,6},{24,8},{26,10},{28,12},{30,14},{80,64}... | collective-permute-start | bytes 786440 | tf_op jit(solution)/shard_map/ppermute | solution.py:55
  32.6 2.8 %collective-permute-done.2.refs_1_ = bf16[8,16,1024]{2,1,0:T(8,128)(2,1)S(1)} collective-permute-done((bf16[8,16,1024]{2,1,0:T(8,128)(2,1)S(1)}, bf16[8,16,1024]{2,1,0:T(8,128)(2,1)S(1)}, u32[]{:S(2)}, u32[]{:S(2)}) %collective-permute-start.2) | collective-permute-done | bytes 262176 | tf_op jit(solution)/shard_map/ppermute | solution.py:55
  35.4 1.1 %collective-permute-done.6.refs_5_ = bf16[8,16,1024]{2,1,0:T(8,128)(2,1)S(1)} collective-permute-done((bf16[8,16,1024]{2,1,0:T(8,128)(2,1)S(1)}, bf16[8,16,1024]{2,1,0:T(8,128)(2,1)S(1)}, u32[]{:S(2)}, u32[]{:S(2)}) %collective-permute-start.6) | collective-permute-done | bytes 262176 | tf_op jit(solution)/shard_map/ppermute | solution.py:55
  36.4 3.7 %collective-permute-done.5.refs_4_ = bf16[8,16,1024]{2,1,0:T(8,128)(2,1)S(1)} collective-permute-done((bf16[8,16,1024]{2,1,0:T(8,128)(2,1)S(1)}, bf16[8,16,1024]{2,1,0:T(8,128)(2,1)S(1)}, u32[]{:S(2)}, u32[]{:S(2)}) %collective-permute-start.5) | collective-permute-done | bytes 262176 | tf_op jit(solution)/shard_map/ppermute | solution.py:55
  40.1 2.8 %gram_part.1 = (bf16[1024,1024]{1,0:T(8,128)(2,1)S(1)}, bf16[16,16,1024]{2,1,0:T(8,128)(2,1)S(1)}, f32[4,1024]{1,0:T(4,128)S(1)}) custom-call(f32[1]{0:T(128)} %get-tuple-element.15.inv, bf16[16,16,1024]{2,1,0:T(8,128)(2,1)S(1)} %all_to_all.20.own, bf16[8,16,1024]{2,1,0:T(8,128)(2,1)S(1)} %collective-permute-done.1.refs_0_, ...), custom_call_target="tpu_custom_call" | custom-call | tf_op jit(solution)/shard_map/gram_part/pallas_call | solution.py:212
  43.0 14.4 %all_to_all.21.pieces = bf16[16,16,1024]{2,1,0:T(8,128)(2,1)S(1)} all-to-all(bf16[16,16,1024]{2,1,0:T(8,128)(2,1)S(1)} %get-tuple-element.17), channel_id=1, replica_groups={{0,2,4,6,8,10,12,14,64,66,68,70,72,74,76,78},{16,18,20,22,24,26,28,30,8..., dimensions={0} | all-to-all | bytes 1048576 | tf_op jit(solution)/shard_map/all_to_all | solution.py:51
  57.4 1.7 %gram_sum.1 = (bf16[16,16,1152]{2,1,0:T(8,128)(2,1)}, f32[8,128]{1,0:T(8,128)S(1)}) custom-call(s32[1]{0:T(128)} %get-tuple-element.14.place, bf16[16,16,1024]{2,1,0:T(8,128)(2,1)S(1)} %all_to_all.21.pieces, f32[4,1024]{1,0:T(4,128)S(1)} %get-tuple-element.18.stats), custom_call_target="tpu_custom_call" | custom-call | tf_op jit(solution)/shard_map/gram_sum/pallas_call | solution.py:226
  59.0 3.6 %all-to-all-start.2 = ((bf16[16,16,1152]{2,1,0:T(8,128)(2,1)}), bf16[16,16,1152]{2,1,0:T(8,128)(2,1)S(1)}, u32[]{:S(2)}, u32[]{:S(2)}) async-start(bf16[16,16,1152]{2,1,0:T(8,128)(2,1)} %get-tuple-element.20), calls=%async_computation.2 | async-start | bytes 1179648 | tf_op jit(solution)/shard_map/all_to_all | solution.py:51
  62.7 2.0 %collective-permute-start.8 = (f32[8,128]{1,0:T(8,128)S(1)}, f32[8,128]{1,0:T(8,128)S(1)}, u32[]{:S(2)}, u32[]{:S(2)}) collective-permute-start(f32[8,128]{1,0:T(8,128)S(1)} %get-tuple-element.19.here), channel_id=1, source_target_pairs={{48,0},{50,2},{52,4},{54,6},{56,8},{58,10},{60,12},{62,14},{112,64... | collective-permute-start | bytes 12296 | tf_op jit(solution)/shard_map/ppermute | solution.py:55
  64.7 1.6 %collective-permute-done.9.after = f32[8,128]{1,0:T(8,128)S(1)} collective-permute-done((f32[8,128]{1,0:T(8,128)S(1)}, f32[8,128]{1,0:T(8,128)S(1)}, u32[]{:S(2)}, u32[]{:S(2)}) %collective-permute-start.9) | collective-permute-done | bytes 4128 | tf_op jit(solution)/shard_map/ppermute | solution.py:55
  66.3 1.3 %collective-permute-done.8.before = f32[8,128]{1,0:T(8,128)S(1)} collective-permute-done((f32[8,128]{1,0:T(8,128)S(1)}, f32[8,128]{1,0:T(8,128)S(1)}, u32[]{:S(2)}, u32[]{:S(2)}) %collective-permute-start.8) | collective-permute-done | bytes 4128 | tf_op jit(solution)/shard_map/ppermute | solution.py:55
  67.6 2.2 %collective-permute-done.7.far = f32[8,128]{1,0:T(8,128)S(1)} collective-permute-done((f32[8,128]{1,0:T(8,128)S(1)}, f32[8,128]{1,0:T(8,128)S(1)}, u32[]{:S(2)}, u32[]{:S(2)}) %collective-permute-start.7) | collective-permute-done | bytes 4128 | tf_op jit(solution)/shard_map/ppermute | solution.py:55
  69.8 3.2 %all-to-all-done.2.gram = bf16[16,16,1152]{2,1,0:T(8,128)(2,1)S(1)} async-done(((bf16[16,16,1152]{2,1,0:T(8,128)(2,1)}), bf16[16,16,1152]{2,1,0:T(8,128)(2,1)S(1)}, u32[]{:S(2)}, u32[]{:S(2)}) %all-to-all-start.2) | async-done | bytes 589856 | tf_op jit(solution)/shard_map/all_to_all | solution.py:51
  73.0 0.8 grad_rows.1
  73.9 14.1 %all_to_all.22.recv = bf16[16,16,1152]{2,1,0:T(8,128)(2,1)S(1)} all-to-all(bf16[16,16,1152]{2,1,0:T(8,128)(2,1)S(1)} %grad_rows.1), channel_id=1, replica_groups={{0,2,4,6,8,10,12,14,64,66,68,70,72,74,76,78},{16,18,20,22,24,26,28,30,8..., dimensions={0} | all-to-all | bytes 1179648 | tf_op jit(solution)/shard_map/all_to_all | solution.py:51
  88.1 1.6 %collective-permute-done.10.got = bf16[16,8,1152]{2,1,0:T(8,128)(2,1)S(1)} collective-permute-done((bf16[16,8,1152]{2,1,0:T(8,128)(2,1)S(1)}, bf16[16,8,1152]{2,1,0:T(8,128)(2,1)S(1)}, u32[]{:S(2)}, u32[]{:S(2)}) %collective-permute-start.10) | collective-permute-done | bytes 294944 | tf_op jit(solution)/shard_map/ppermute | solution.py:55
  89.7 1.2 %add_pull.1 = (f32[8,16384]{1,0:T(8,128)}, f32[8,16384]{1,0:T(8,128)}, f32[1]{0:T(128)}) custom-call(s32[1]{0:T(128)} %bitcast.core, bf16[16,16,1152]{2,1,0:T(8,128)(2,1)S(1)} %all_to_all.22.recv, bf16[16,8,1152]{2,1,0:T(8,128)(2,1)S(1)} %collective-permute-done.10.got, bf16[8,16384]{1,0:T(8,128)(2,1)S(1)} %copy-done.1, bf16[8,16384]{1,0:T(8,128)(2,1)S(1)} %copy-done), custom_call_target="tpu_custom_call" | custom-call | tf_op jit(solution)/shard_map/add_pull/pallas_call | solution.py:252
  (15 shorter events, 1.0 us)
Async XLA Ops:
  1.7 1.6 %collective-permute-start = (bf16[8,16384]{1,0:T(8,128)(2,1)S(1)}, bf16[8,16384]{1,0:T(8,128)(2,1)S(1)}, u32[]{:S(2)}, u32[]{:S(2)}) collective-permute-start(bf16[8,16384]{1,0:T(8,128)(2,1)S(1)} %get-tuple-element.27.give), channel_id=1, source_target_pairs={{0,1},{1,0},{2,3},{3,2},{4,5},{5,4},{6,7},{7,6},{8,9},{9,8},{10,11... | collective-permute-start | bytes 786440 | tf_op jit(solution)/shard_map/ppermute | solution.py:55
  22.5 6.4 %collective-permute-start.4 = (bf16[8,16,1024]{2,1,0:T(8,128)(2,1)S(1)}, bf16[8,16,1024]{2,1,0:T(8,128)(2,1)S(1)}, u32[]{:S(2)}, u32[]{:S(2)}) collective-permute-start(bf16[8,16,1024]{2,1,0:T(8,128)(2,1)S(1)} %get-tuple-element.25), channel_id=1, source_target_pairs={{16,0},{18,2},{20,4},{22,6},{24,8},{26,10},{28,12},{30,14},{80,64}... | collective-permute-start | bytes 786440 | tf_op jit(solution)/shard_map/ppermute | solution.py:55
  25.0 7.6 %collective-permute-start.1 = (bf16[8,16,1024]{2,1,0:T(8,128)(2,1)S(1)}, bf16[8,16,1024]{2,1,0:T(8,128)(2,1)S(1)}, u32[]{:S(2)}, u32[]{:S(2)}) collective-permute-start(bf16[8,16,1024]{2,1,0:T(8,128)(2,1)S(1)} %get-tuple-element.26), channel_id=1, source_target_pairs={{48,0},{50,2},{52,4},{54,6},{56,8},{58,10},{60,12},{62,14},{112,64... | collective-permute-start | bytes 786440 | tf_op jit(solution)/shard_map/ppermute | solution.py:55
  25.0 10.4 %collective-permute-start.2 = (bf16[8,16,1024]{2,1,0:T(8,128)(2,1)S(1)}, bf16[8,16,1024]{2,1,0:T(8,128)(2,1)S(1)}, u32[]{:S(2)}, u32[]{:S(2)}) collective-permute-start(bf16[8,16,1024]{2,1,0:T(8,128)(2,1)S(1)} %get-tuple-element.25), channel_id=1, source_target_pairs={{48,0},{50,2},{52,4},{54,6},{56,8},{58,10},{60,12},{62,14},{112,64... | collective-permute-start | bytes 786440 | tf_op jit(solution)/shard_map/ppermute | solution.py:55
  25.7 9.6 %collective-permute-start.3 = (bf16[8,16,1024]{2,1,0:T(8,128)(2,1)S(1)}, bf16[8,16,1024]{2,1,0:T(8,128)(2,1)S(1)}, u32[]{:S(2)}, u32[]{:S(2)}) collective-permute-start(bf16[8,16,1024]{2,1,0:T(8,128)(2,1)S(1)} %get-tuple-element.26), channel_id=1, source_target_pairs={{16,0},{18,2},{20,4},{22,6},{24,8},{26,10},{28,12},{30,14},{80,64}... | collective-permute-start | bytes 786440 | tf_op jit(solution)/shard_map/ppermute | solution.py:55
  28.9 7.5 %collective-permute-start.6 = (bf16[8,16,1024]{2,1,0:T(8,128)(2,1)S(1)}, bf16[8,16,1024]{2,1,0:T(8,128)(2,1)S(1)}, u32[]{:S(2)}, u32[]{:S(2)}) collective-permute-start(bf16[8,16,1024]{2,1,0:T(8,128)(2,1)S(1)} %collective-permute-done.4.refs_3_), channel_id=1, source_target_pairs={{16,0},{18,2},{20,4},{22,6},{24,8},{26,10},{28,12},{30,14},{80,64}... | collective-permute-start | bytes 786440 | tf_op jit(solution)/shard_map/ppermute | solution.py:55
  32.6 7.6 %collective-permute-start.5 = (bf16[8,16,1024]{2,1,0:T(8,128)(2,1)S(1)}, bf16[8,16,1024]{2,1,0:T(8,128)(2,1)S(1)}, u32[]{:S(2)}, u32[]{:S(2)}) collective-permute-start(bf16[8,16,1024]{2,1,0:T(8,128)(2,1)S(1)} %collective-permute-done.1.refs_0_), channel_id=1, source_target_pairs={{48,0},{50,2},{52,4},{54,6},{56,8},{58,10},{60,12},{62,14},{112,64... | collective-permute-start | bytes 786440 | tf_op jit(solution)/shard_map/ppermute | solution.py:55
  59.0 14.0 %all-to-all-start.2 = ((bf16[16,16,1152]{2,1,0:T(8,128)(2,1)}), bf16[16,16,1152]{2,1,0:T(8,128)(2,1)S(1)}, u32[]{:S(2)}, u32[]{:S(2)}) async-start(bf16[16,16,1152]{2,1,0:T(8,128)(2,1)} %get-tuple-element.20), calls=%async_computation.2 | async-start | bytes 1179648 | tf_op jit(solution)/shard_map/all_to_all | solution.py:51
  62.6 3.7 %collective-permute-start.9 = (f32[8,128]{1,0:T(8,128)S(1)}, f32[8,128]{1,0:T(8,128)S(1)}, u32[]{:S(2)}, u32[]{:S(2)}) collective-permute-start(f32[8,128]{1,0:T(8,128)S(1)} %get-tuple-element.19.here), channel_id=1, source_target_pairs={{16,0},{18,2},{20,4},{22,6},{24,8},{26,10},{28,12},{30,14},{80,64}... | collective-permute-start | bytes 12296 | tf_op jit(solution)/shard_map/ppermute | solution.py:55
  62.7 4.9 %collective-permute-start.8 = (f32[8,128]{1,0:T(8,128)S(1)}, f32[8,128]{1,0:T(8,128)S(1)}, u32[]{:S(2)}, u32[]{:S(2)}) collective-permute-start(f32[8,128]{1,0:T(8,128)S(1)} %get-tuple-element.19.here), channel_id=1, source_target_pairs={{48,0},{50,2},{52,4},{54,6},{56,8},{58,10},{60,12},{62,14},{112,64... | collective-permute-start | bytes 12296 | tf_op jit(solution)/shard_map/ppermute | solution.py:55
  64.7 5.1 %collective-permute-start.7 = (f32[8,128]{1,0:T(8,128)S(1)}, f32[8,128]{1,0:T(8,128)S(1)}, u32[]{:S(2)}, u32[]{:S(2)}) collective-permute-start(f32[8,128]{1,0:T(8,128)S(1)} %get-tuple-element.19.here), channel_id=1, source_target_pairs={{32,0},{34,2},{36,4},{38,6},{40,8},{42,10},{44,12},{46,14},{96,64}... | collective-permute-start | bytes 12296 | tf_op jit(solution)/shard_map/ppermute | solution.py:55
  73.0 16.7 %copy-start = (bf16[8,16384]{1,0:T(8,128)(2,1)S(1)}, bf16[8,16384]{1,0:T(8,128)(2,1)}, u32[]{:S(2)}) copy-start(bf16[8,16384]{1,0:T(8,128)(2,1)} %view_two.1) | copy-start | bytes 786436
  73.0 16.7 %copy-start.1 = (bf16[8,16384]{1,0:T(8,128)(2,1)S(1)}, bf16[8,16384]{1,0:T(8,128)(2,1)}, u32[]{:S(2)}) copy-start(bf16[8,16384]{1,0:T(8,128)(2,1)} %view_one.1) | copy-start | bytes 786436
  88.0 1.7 %collective-permute-start.10 = (bf16[16,8,1152]{2,1,0:T(8,128)(2,1)S(1)}, bf16[16,8,1152]{2,1,0:T(8,128)(2,1)S(1)}, u32[]{:S(2)}, u32[]{:S(2)}) collective-permute-start(bf16[16,8,1152]{2,1,0:T(8,128)(2,1)S(1)} %slice.14), channel_id=1, source_target_pairs={{0,1},{1,0},{2,3},{3,2},{4,5},{5,4},{6,7},{7,6},{8,9},{9,8},{10,11... | collective-permute-start | bytes 884744 | tf_op jit(solution)/shard_map/ppermute | solution.py:55

commit v6 on v5

--- a/solution.py
+++ b/solution.py
@@ -63,19 +63,19 @@
     return jnp.where(core == 0, first, second)
 
 
-def pack_kernel(factor, place_in, keep, give, got, packed, inv, place):
+def pack_kernel(factor, place_in, keep, give, got, packed, squares, place):
     parts, rows, width = packed.shape
     place[0] = place_in[0]
-    squares = 0.0
+    total = 0.0
     for c in range(parts):
         cut = pl.ds(c * width, width)
         mine, other, more = [ref[:, cut].astype(jnp.float32) for ref in (keep, give, got)]
         packed[c] = jnp.concatenate([mine, more], axis=0).astype(jnp.bfloat16)
-        squares += (mine - other) ** 2
-    inv[0] = factor * jnp.sum(squares)
-
-
-def gram_kernel(sizes, inv, own, *refs):
+        total += (mine - other) ** 2
+    squares[...] = factor * total
+
+
+def gram_kernel(sizes, pull, own, *refs):
     copies, (rounded, part, stats) = refs[:-3], refs[-3:]
     batch_rows, feature_count, row_parts = sizes
     group_rows = batch_rows // row_parts
@@ -97,7 +97,7 @@
             energy += jnp.sum(a * a, axis=0, keepdims=True)
         share = var_weight / feature_count / row_parts * jnp.maximum(1.0 - spread, 0.0)
         share -= cov_weight / feature_count / row_parts * (energy / (batch_rows - 1)) ** 2
-        share += inv[0] / width
+        share += jnp.sum(pull[:, cut], axis=0, keepdims=True)
         stats[0:1, cut] = mean
         stats[1:2, cut] = energy
         stats[2:3, cut] = jnp.where(spread < 1.0, 1.0 / spread, 0.0)
@@ -108,45 +108,76 @@
     part[...] = product.astype(jnp.bfloat16).reshape(part.shape)
 
 
-def sum_kernel(sizes, place, pieces, stats, sent, scalar):
+def slots(shape, rows, first, shift):
+    row = lax.broadcasted_iota(jnp.int32, shape, 0)
+    lane = lax.broadcasted_iota(jnp.int32, shape, 1)
+    inside = row % rows
+    return lane == first + row - inside + (inside + shift) % rows
+
+
+def three_parts(value, shape):
+    value = jnp.full(shape, value, jnp.float32)
+    high = value.astype(jnp.bfloat16).astype(jnp.float32)
+    middle = (value - high).astype(jnp.bfloat16).astype(jnp.float32)
+    row = lax.broadcasted_iota(jnp.int32, shape, 0)
+    low = jnp.where(row == 2, value - high - middle, 0.0)
+    return jnp.where(row == 0, high, jnp.where(row == 1, middle, low))
+
+
+def sum_kernel(sizes, place, pieces, stats, sent):
     batch_rows, feature_count, row_parts = sizes
     rows = pieces.shape[1]
     summed = jnp.sum(pieces[...].astype(jnp.float32), axis=0)
     shape = summed.shape
-    lane = lax.broadcasted_iota(jnp.int32, shape, 1)
-    row = lax.broadcasted_iota(jnp.int32, shape, 0)
+    first = place[0] * rows
     short = summed.astype(jnp.bfloat16).astype(jnp.float32)
-    on_diagonal = lane == place[0] * rows + row
-    lost = jnp.sum(jnp.where(on_diagonal, summed - short, 0.0), axis=1, keepdims=True)
-    extra = jnp.broadcast_to(lost, (rows, LANES))
-    out = jnp.concatenate([short, extra], axis=1).astype(jnp.bfloat16)
-    sent[...] = jnp.broadcast_to(out[None], sent.shape)
+    diagonal = slots(shape, rows, first, 0)
+    lost = jnp.sum(jnp.where(diagonal, summed - short, 0.0), axis=1, keepdims=True)
     factor = cov_weight / feature_count / (batch_rows - 1) ** 2
-    value = factor * jnp.sum(summed * summed) + jnp.sum(stats[3:4])
-    scalar[...] = jnp.full(scalar.shape, value, jnp.float32)
-
-
-def grad_kernel(sizes, here, far, before, after, gram, rounded, own, stats, sent):
+    value = jnp.sum(factor * jnp.sum(summed * summed, axis=0, keepdims=True) + stats[3:4])
+    out = jnp.where(slots(shape, rows, first, rows - 1), lost, short)
+    out = jnp.where(slots(shape, rows, first, rows - 2), three_parts(value, (rows, 1)), out)
+    sent[...] = jnp.broadcast_to(out.astype(jnp.bfloat16)[None], sent.shape)
+
+
+def grad_kernel(sizes, gram, rounded, own, stats, sent, scalar):
     batch_rows, feature_count, row_parts = sizes
     parts, rows, width = own.shape
     group_rows = parts * rows
     factor_cov = 4.0 * cov_weight * batch_rows / (batch_rows - 1) ** 2 / out_scale
     factor_var = var_weight * batch_rows / (batch_rows - 1) / out_scale
-    scalar = (here[0:1] + far[0:1]) + (before[0:1] + after[0:1])
-    value = jnp.broadcast_to(scalar, (rows, LANES))
-    high = value.astype(jnp.bfloat16).astype(jnp.float32)
-    middle = (value - high).astype(jnp.bfloat16).astype(jnp.float32)
-    low = value - high - middle
-    lane = lax.broadcasted_iota(jnp.int32, value.shape, 1)
-    three = jnp.where(lane == 0, high, jnp.where(lane == 1, middle, low)).astype(jnp.bfloat16)
-    sent[:, :, pl.ds(width, LANES)] = jnp.broadcast_to(three[None], (parts, rows, LANES))
-
-    matrix = gram[:, :, pl.ds(0, batch_rows)].reshape(group_rows, batch_rows)
-    lost = gram[:, :, pl.ds(batch_rows, LANES)].reshape(group_rows, LANES).astype(jnp.float32)[:, 0:1]
+
+    square = gram[:, :, pl.ds(0, group_rows)].reshape(group_rows, group_rows).astype(jnp.float32)
+    shape = square.shape
+    lane = lax.broadcasted_iota(jnp.int32, (1, group_rows), 1) % rows
+    restored = square
+    for shift in (1, 2):
+        mirror = jnp.sum(
+            jnp.where(slots(shape, rows, 0, shift), square, 0.0), axis=0, keepdims=True
+        )
+        ahead = pltpu.roll(mirror, group_rows - shift, 1)
+        around = pltpu.roll(mirror, rows - shift, 1)
+        mirror = jnp.where(lane < rows - shift, ahead, around)
+        here = slots(shape, rows, 0, rows - shift)
+        restored = jnp.where(here, mirror, restored)
+        taken = jnp.sum(jnp.where(here, square, 0.0), axis=1, keepdims=True)
+        if shift == 1:
+            lost = taken
+        else:
+            scalar[...] = jnp.full(scalar.shape, jnp.sum(taken), jnp.float32)
+    left = restored.astype(jnp.bfloat16)
+    right = gram[:, :, pl.ds(group_rows, batch_rows - group_rows)]
+    right = right.reshape(group_rows, batch_rows - group_rows)
     for start in range(0, width, CHUNK):
         cut = pl.ds(start, CHUNK)
         product = lax.dot_general(
-            matrix, rounded[:, cut], CONTRACT_FIRST, preferred_element_type=jnp.float32
+            left, rounded[pl.ds(0, group_rows), cut], CONTRACT_FIRST, preferred_element_type=jnp.float32
+        )
+        product += lax.dot_general(
+            right,
+            rounded[pl.ds(group_rows, batch_rows - group_rows), cut],
+            CONTRACT_FIRST,
+            preferred_element_type=jnp.float32,
         )
         mine = rounded[pl.ds(0, group_rows), cut].astype(jnp.float32)
         centered = own[:, :, cut].reshape(group_rows, CHUNK).astype(jnp.float32) - stats[0:1, cut]
@@ -155,22 +186,17 @@
         sent[:, :, cut] = grad.astype(jnp.bfloat16).reshape(parts, rows, CHUNK)
 
 
-def final_kernel(core, recv, got, view_one, view_two, grad_one, grad_two, loss):
+def final_kernel(core, recv, got, mine, other, view_one, view_two, grad_one, grad_two, loss):
     parts, rows, width = got.shape
-    width -= LANES
     push = 2.0 * inv_weight / out_scale
-    sums = 0.0
     for c in range(parts):
-        mine = recv[c].astype(jnp.float32)[:rows]
-        other = got[c].astype(jnp.float32)
+        own_rows = recv[c].astype(jnp.float32)[:rows]
+        more = got[c].astype(jnp.float32)
         cut = pl.ds(c * width, width)
         diff = push * (view_one[:, cut].astype(jnp.float32) - view_two[:, cut].astype(jnp.float32))
-        grad_one[:, cut] = pick(core[0], mine[:, :width], other[:, :width]) + diff
-        grad_two[:, cut] = pick(core[0], other[:, :width], mine[:, :width]) - diff
-        sums += mine[:, width:] + other[:, width:]
-    lane = lax.broadcasted_iota(jnp.int32, sums.shape, 1)
-    row = lax.broadcasted_iota(jnp.int32, sums.shape, 0)
-    loss[0] = jnp.sum(jnp.where((lane < 3) & (row == 0), sums, 0.0))
+        grad_one[:, cut] = pick(core[0], own_rows, more) + diff
+        grad_two[:, cut] = pick(core[0], more, own_rows) - diff
+    loss[0] = jnp.max(mine[...] + other[...])
 
 
 def body(view_one, view_two):
@@ -190,13 +216,13 @@
     vmem = pl.BlockSpec(memory_space=pltpu.VMEM)
 
     keep, give = pick(core[0], view_one, view_two), pick(core[0], view_two, view_one)
-    blocks, inv, place = pl.pallas_call(
+    blocks, pull, place = pl.pallas_call(
         functools.partial(pack_kernel, inv_weight / (batch_rows * feature_count)),
         in_specs=[smem, vmem, vmem, vmem],
-        out_specs=[vmem, smem, smem],
+        out_specs=[vmem, vmem, smem],
         out_shape=[
             jax.ShapeDtypeStruct((feature_parts, rows, width), jnp.bfloat16),
-            jax.ShapeDtypeStruct((1,), jnp.float32),
+            jax.ShapeDtypeStruct((shard_rows, width), jnp.float32),
             jax.ShapeDtypeStruct((1,), jnp.int32),
         ],
         compiler_params=room(4),
@@ -211,7 +237,7 @@
     copies = (up_first, up_second, down_first, down_second, far_first, far_second)
     rounded, part, stats = pl.pallas_call(
         functools.partial(gram_kernel, sizes),
-        in_specs=[smem, vmem] + [vmem] * len(copies),
+        in_specs=[vmem] * (2 + len(copies)),
         out_specs=[vmem, vmem, vmem],
         out_shape=[
             jax.ShapeDtypeStruct((batch_rows, width), jnp.bfloat16),
@@ -220,38 +246,39 @@
         ],
         compiler_params=room(24),
         name="gram_part",
-    )(inv, own, *copies)
+    )(pull, own, *copies)
 
     pieces = exchange(part)
-    sent, scalar = pl.pallas_call(
+    sent = pl.pallas_call(
         functools.partial(sum_kernel, sizes),
         in_specs=[smem, vmem, vmem],
-        out_specs=[vmem, vmem],
-        out_shape=[
-            pltpu.HBM((feature_parts, rows, batch_rows + LANES), jnp.bfloat16),
-            jax.ShapeDtypeStruct((8, LANES), jnp.float32),
-        ],
+        out_specs=vmem,
+        out_shape=jax.ShapeDtypeStruct((feature_parts, rows, batch_rows), jnp.bfloat16),
         compiler_params=room(4),
         name="gram_sum",
     )(place, pieces, stats)
 
     gram = exchange(sent)
-    scalars = [scalar] + [move(scalar, pairs) for pairs in (FAR, UP, DOWN)]
-
-    grads = pl.pallas_call(
+    grads, scalar = pl.pallas_call(
         functools.partial(grad_kernel, sizes),
-        in_specs=[vmem] * 8,
-        out_specs=vmem,
-        out_shape=jax.ShapeDtypeStruct((feature_parts, rows, width + LANES), jnp.bfloat16),
+        in_specs=[vmem] * 4,
+        out_specs=[vmem] * 2,
+        out_shape=[
+            pltpu.HBM((feature_parts, rows, width), jnp.bfloat16),
+            jax.ShapeDtypeStruct((8, LANES), jnp.float32),
+        ],
         compiler_params=room(16),
         name="grad_rows",
-    )(*scalars, gram, rounded, own, stats)
+    )(gram, rounded, own, stats)
 
     grads = exchange(grads)
-    others = move(grads[:, shard_rows:], SWAP)
+    far, before, after = [move(scalar, pairs) for pairs in (FAR, UP, DOWN)]
+    scalar = (scalar + far) + (before + after)
+    cut, scalar = lax.optimization_barrier((grads[:, shard_rows:], scalar))
+    others, other_scalar = move(cut, SWAP), move(scalar, SWAP)
     grad_one, grad_two, loss = pl.pallas_call(
         final_kernel,
-        in_specs=[smem, vmem, vmem, vmem, vmem],
+        in_specs=[smem] + [vmem] * 6,
         out_specs=[vmem, vmem, smem],
         out_shape=[
             jax.ShapeDtypeStruct(view_one.shape, jnp.float32),
@@ -260,7 +287,7 @@
         ],
         compiler_params=room(4),
         name="add_pull",
-    )(core, grads, others, view_one, view_two)
+    )(core, grads, others, scalar, other_scalar, view_one, view_two)
     return grad_one, grad_two, loss.reshape(())
 
 

time: 92.3 us -> 90.5 us (0.980)
    ppermute x11 -> x12, waiting for transfers between devices: 16.4 us -> 15.9 us  [move(): return lax.ppermute(block, FINE, pairs)]
    ppermute x11 -> x12, starting transfers between devices: 11.7 us -> 12.2 us  [move(): return lax.ppermute(block, FINE, pairs)]
  transfers between devices with their start and end apart: 12 -> 13, of which waited for: 10 -> 10; matrix products, arithmetic and copies ran while one was open for 0% -> 0% of each run, Pallas kernels for 0% -> 0%
where the time goes in v6:
time: 90.5 us; the launch traced here: 89.1 us
  blocking collectives  46.1 us (51%)
  waiting for transfers between devices  18.7 us (21%)
  starting transfers between devices  15.8 us (17%)
  Pallas kernels  6.6 us (7%)
  other arithmetic  1.08 us (1%)
    all_to_all x3, blocking collectives, exchange(): lax.all_to_all(blocks, FINE, 0, 0, tiled=True, axis_index_groups=GROUPS)  46.1 us
    ppermute x12, waiting for transfers between devices, move(): return lax.ppermute(block, FINE, pairs)  15.9 us
    ppermute x12, starting transfers between devices, move(): return lax.ppermute(block, FINE, pairs)  12.2 us
    all_to_all x1, starting transfers between devices, exchange(): lax.all_to_all(blocks, FINE, 0, 0, tiled=True, axis_index_groups=GROUPS)  3.57 us
    all_to_all x1, waiting for transfers between devices, exchange(): lax.all_to_all(blocks, FINE, 0, 0, tiled=True, axis_index_groups=GROUPS)  2.85 us
    pallas_call x1, Pallas kernels, body(): pl.pallas_call(functools.partial(gram_kernel, sizes), in_specs=[vmem] * (...  2.16 us
    pallas_call x1, Pallas kernels, body(): pl.pallas_call(functools.partial(grad_kernel, sizes), in_specs=[vmem] * 4...  1.84 us
  transfers between devices with their start and end apart: 13, of which 10 were waited for; matrix products, arithmetic and copies ran while one was open for 0% of the time, Pallas kernels for 0%

profile of v6, /device:TPU:0, one launch (start us, length us, event | category | flops | bytes accessed | tf_op | source)
XLA Modules:
  0.0 89.1 jit_solution(13789472025723808186)
XLA Ops:
  0.6 1.1 %broadcast_select_fusion = (bf16[8,16384]{1,0:T(8,128)(2,1)S(1)}, bf16[8,16384]{1,0:T(8,128)(2,1)S(1)}) fusion(bf16[8,16384]{1,0:T(8,128)(2,1)} %view_two.1, bf16[8,16384]{1,0:T(8,128)(2,1)} %view_one.1, pred[]{:T(512)S(6)} %eq.2), kind=kLoop, calls=%fused_computation | loop fusion | flops 262144 | bytes 1048577 | tf_op jit(solution)/shard_map/jit(_where)/select_n | solution.py:63
  1.8 1.5 %collective-permute-done.got = bf16[8,16384]{1,0:T(8,128)(2,1)S(1)} collective-permute-done((bf16[8,16384]{1,0:T(8,128)(2,1)S(1)}, bf16[8,16384]{1,0:T(8,128)(2,1)S(1)}, u32[]{:S(2)}, u32[]{:S(2)}) %collective-permute-start) | collective-permute-done | bytes 262176 | tf_op jit(solution)/shard_map/ppermute | solution.py:55
  3.9 18.3 %all_to_all.20.own = bf16[16,16,1024]{2,1,0:T(8,128)(2,1)S(1)} all-to-all(bf16[16,16,1024]{2,1,0:T(8,128)(2,1)S(1)} %get-tuple-element.18), channel_id=1, replica_groups={{0,2,4,6,8,10,12,14,64,66,68,70,72,74,76,78},{16,18,20,22,24,26,28,30,8..., dimensions={0} | all-to-all | bytes 1048576 | tf_op jit(solution)/shard_map/all_to_all | solution.py:51
  22.3 2.5 %collective-permute-start.4 = (bf16[8,16,1024]{2,1,0:T(8,128)(2,1)S(1)}, bf16[8,16,1024]{2,1,0:T(8,128)(2,1)S(1)}, u32[]{:S(2)}, u32[]{:S(2)}) collective-permute-start(bf16[8,16,1024]{2,1,0:T(8,128)(2,1)S(1)} %get-tuple-element.29), channel_id=1, source_target_pairs={{16,0},{18,2},{20,4},{22,6},{24,8},{26,10},{28,12},{30,14},{80,64}... | collective-permute-start | bytes 786440 | tf_op jit(solution)/shard_map/ppermute | solution.py:55
  24.8 0.8 collective-permute-start.2
  25.6 2.5 %collective-permute-start.3 = (bf16[8,16,1024]{2,1,0:T(8,128)(2,1)S(1)}, bf16[8,16,1024]{2,1,0:T(8,128)(2,1)S(1)}, u32[]{:S(2)}, u32[]{:S(2)}) collective-permute-start(bf16[8,16,1024]{2,1,0:T(8,128)(2,1)S(1)} %get-tuple-element.30), channel_id=1, source_target_pairs={{16,0},{18,2},{20,4},{22,6},{24,8},{26,10},{28,12},{30,14},{80,64}... | collective-permute-start | bytes 786440 | tf_op jit(solution)/shard_map/ppermute | solution.py:55
  28.1 0.7 collective-permute-done.4.refs_3_
  28.7 3.7 %collective-permute-start.6 = (bf16[8,16,1024]{2,1,0:T(8,128)(2,1)S(1)}, bf16[8,16,1024]{2,1,0:T(8,128)(2,1)S(1)}, u32[]{:S(2)}, u32[]{:S(2)}) collective-permute-start(bf16[8,16,1024]{2,1,0:T(8,128)(2,1)S(1)} %collective-permute-done.4.refs_3_), channel_id=1, source_target_pairs={{16,0},{18,2},{20,4},{22,6},{24,8},{26,10},{28,12},{30,14},{80,64}... | collective-permute-start | bytes 786440 | tf_op jit(solution)/shard_map/ppermute | solution.py:55
  32.4 2.8 %collective-permute-done.2.refs_1_ = bf16[8,16,1024]{2,1,0:T(8,128)(2,1)S(1)} collective-permute-done((bf16[8,16,1024]{2,1,0:T(8,128)(2,1)S(1)}, bf16[8,16,1024]{2,1,0:T(8,128)(2,1)S(1)}, u32[]{:S(2)}, u32[]{:S(2)}) %collective-permute-start.2) | collective-permute-done | bytes 262176 | tf_op jit(solution)/shard_map/ppermute | solution.py:55
  35.2 1.1 %collective-permute-done.6.refs_5_ = bf16[8,16,1024]{2,1,0:T(8,128)(2,1)S(1)} collective-permute-done((bf16[8,16,1024]{2,1,0:T(8,128)(2,1)S(1)}, bf16[8,16,1024]{2,1,0:T(8,128)(2,1)S(1)}, u32[]{:S(2)}, u32[]{:S(2)}) %collective-permute-start.6) | collective-permute-done | bytes 262176 | tf_op jit(solution)/shard_map/ppermute | solution.py:55
  36.3 3.7 %collective-permute-done.5.refs_4_ = bf16[8,16,1024]{2,1,0:T(8,128)(2,1)S(1)} collective-permute-done((bf16[8,16,1024]{2,1,0:T(8,128)(2,1)S(1)}, bf16[8,16,1024]{2,1,0:T(8,128)(2,1)S(1)}, u32[]{:S(2)}, u32[]{:S(2)}) %collective-permute-start.5) | collective-permute-done | bytes 262176 | tf_op jit(solution)/shard_map/ppermute | solution.py:55
  40.0 2.2 %gram_part.1 = (bf16[1024,1024]{1,0:T(8,128)(2,1)S(1)}, bf16[16,16,1024]{2,1,0:T(8,128)(2,1)S(1)}, f32[4,1024]{1,0:T(4,128)S(1)}) custom-call(f32[8,1024]{1,0:T(8,128)S(1)} %get-tuple-element.17.pull, bf16[16,16,1024]{2,1,0:T(8,128)(2,1)S(1)} %all_to_all.20.own, bf16[8,16,1024]{2,1,0:T(8,128)(2,1)S(1)} %collective-permute-done.1.refs_0_, ...), custom_call_target="tpu_custom_call" | custom-call | tf_op jit(solution)/shard_map/gram_part/pallas_call | solution.py:238
  42.1 14.4 %all_to_all.21.pieces = bf16[16,16,1024]{2,1,0:T(8,128)(2,1)S(1)} all-to-all(bf16[16,16,1024]{2,1,0:T(8,128)(2,1)S(1)} %get-tuple-element.19), channel_id=1, replica_groups={{0,2,4,6,8,10,12,14,64,66,68,70,72,74,76,78},{16,18,20,22,24,26,28,30,8..., dimensions={0} | all-to-all | bytes 1048576 | tf_op jit(solution)/shard_map/all_to_all | solution.py:51
  56.5 0.9 %gram_sum.1 = bf16[16,16,1024]{2,1,0:T(8,128)(2,1)S(1)} custom-call(s32[1]{0:T(128)} %get-tuple-element.16.place, bf16[16,16,1024]{2,1,0:T(8,128)(2,1)S(1)} %all_to_all.21.pieces, f32[4,1024]{1,0:T(4,128)S(1)} %get-tuple-element.20.stats), custom_call_target="tpu_custom_call" | custom-call | tf_op jit(solution)/shard_map/gram_sum/pallas_call | solution.py:252
  57.4 13.3 %all_to_all.22.gram = bf16[16,16,1024]{2,1,0:T(8,128)(2,1)S(1)} all-to-all(bf16[16,16,1024]{2,1,0:T(8,128)(2,1)S(1)} %gram_sum.1), channel_id=1, replica_groups={{0,2,4,6,8,10,12,14,64,66,68,70,72,74,76,78},{16,18,20,22,24,26,28,30,8..., dimensions={0} | all-to-all | bytes 1048576 | tf_op jit(solution)/shard_map/all_to_all | solution.py:51
  70.8 1.8 %grad_rows.1 = (bf16[16,16,1024]{2,1,0:T(8,128)(2,1)}, f32[8,128]{1,0:T(8,128)S(1)}) custom-call(bf16[16,16,1024]{2,1,0:T(8,128)(2,1)S(1)} %all_to_all.22.gram, bf16[1024,1024]{1,0:T(8,128)(2,1)S(1)} %get-tuple-element.21.rounded, bf16[16,16,1024]{2,1,0:T(8,128)(2,1)S(1)} %all_to_all.20.own, f32[4,1024]{1,0:T(4,128)S(1)} %get-tuple-element.20.stats), custom_call_target="tpu_custom_call" | custom-call | tf_op jit(solution)/shard_map/grad_rows/pallas_call | solution.py:262
  72.6 3.6 %all-to-all-start.3 = ((bf16[16,16,1024]{2,1,0:T(8,128)(2,1)}), bf16[16,16,1024]{2,1,0:T(8,128)(2,1)S(1)}, u32[]{:S(2)}, u32[]{:S(2)}) async-start(bf16[16,16,1024]{2,1,0:T(8,128)(2,1)} %get-tuple-element.22), calls=%async_computation.3 | async-start | bytes 1048576 | tf_op jit(solution)/shard_map/all_to_all | solution.py:51
  76.3 2.0 %collective-permute-start.8 = (f32[8,128]{1,0:T(8,128)S(1)}, f32[8,128]{1,0:T(8,128)S(1)}, u32[]{:S(2)}, u32[]{:S(2)}) collective-permute-start(f32[8,128]{1,0:T(8,128)S(1)} %get-tuple-element.23), channel_id=1, source_target_pairs={{48,0},{50,2},{52,4},{54,6},{56,8},{58,10},{60,12},{62,14},{112,64... | collective-permute-start | bytes 12296 | tf_op jit(solution)/shard_map/ppermute | solution.py:55
  78.3 1.6 %collective-permute-done.9 = f32[8,128]{1,0:T(8,128)S(1)} collective-permute-done((f32[8,128]{1,0:T(8,128)S(1)}, f32[8,128]{1,0:T(8,128)S(1)}, u32[]{:S(2)}, u32[]{:S(2)}) %collective-permute-start.9) | collective-permute-done | bytes 4128 | tf_op jit(solution)/shard_map/ppermute | solution.py:55
  79.9 1.3 %collective-permute-done.8 = f32[8,128]{1,0:T(8,128)S(1)} collective-permute-done((f32[8,128]{1,0:T(8,128)S(1)}, f32[8,128]{1,0:T(8,128)S(1)}, u32[]{:S(2)}, u32[]{:S(2)}) %collective-permute-start.8) | collective-permute-done | bytes 4128 | tf_op jit(solution)/shard_map/ppermute | solution.py:55
  81.2 2.2 %collective-permute-done.7 = f32[8,128]{1,0:T(8,128)S(1)} collective-permute-done((f32[8,128]{1,0:T(8,128)S(1)}, f32[8,128]{1,0:T(8,128)S(1)}, u32[]{:S(2)}, u32[]{:S(2)}) %collective-permute-start.7) | collective-permute-done | bytes 4128 | tf_op jit(solution)/shard_map/ppermute | solution.py:55
  83.4 2.8 %all-to-all-done.3.recv = bf16[16,16,1024]{2,1,0:T(8,128)(2,1)S(1)} async-done(((bf16[16,16,1024]{2,1,0:T(8,128)(2,1)}), bf16[16,16,1024]{2,1,0:T(8,128)(2,1)S(1)}, u32[]{:S(2)}, u32[]{:S(2)}) %all-to-all-start.3) | async-done | bytes 524320 | tf_op jit(solution)/shard_map/all_to_all | solution.py:51
  86.9 1.0 %collective-permute-done.11.other = f32[8,128]{1,0:T(8,128)S(1)} collective-permute-done((f32[8,128]{1,0:T(8,128)S(1)}, f32[8,128]{1,0:T(8,128)S(1)}, u32[]{:S(2)}, u32[]{:S(2)}) %collective-permute-start.11) | collective-permute-done | bytes 4128 | tf_op jit(solution)/shard_map/ppermute | solution.py:55
  87.9 1.1 %add_pull.1 = (f32[8,16384]{1,0:T(8,128)}, f32[8,16384]{1,0:T(8,128)}, f32[1]{0:T(128)}) custom-call(s32[1]{0:T(128)} %bitcast.core, bf16[16,16,1024]{2,1,0:T(8,128)(2,1)S(1)} %all-to-all-done.3.recv, bf16[16,8,1024]{2,1,0:T(8,128)(2,1)S(1)} %collective-permute-done.10.got, f32[8,128]{1,0:T(8,128)S(1)} %add_add_fusion.mine, ...), custom_call_target="tpu_custom_call" | custom-call | tf_op jit(solution)/shard_map/add_pull/pallas_call | solution.py:279
  (18 shorter events, 1.4 us)
Async XLA Ops:
  1.7 1.6 %collective-permute-start = (bf16[8,16384]{1,0:T(8,128)(2,1)S(1)}, bf16[8,16384]{1,0:T(8,128)(2,1)S(1)}, u32[]{:S(2)}, u32[]{:S(2)}) collective-permute-start(bf16[8,16384]{1,0:T(8,128)(2,1)S(1)} %get-tuple-element.31.give), channel_id=1, source_target_pairs={{0,1},{1,0},{2,3},{3,2},{4,5},{5,4},{6,7},{7,6},{8,9},{9,8},{10,11... | collective-permute-start | bytes 786440 | tf_op jit(solution)/shard_map/ppermute | solution.py:55
  22.3 6.4 %collective-permute-start.4 = (bf16[8,16,1024]{2,1,0:T(8,128)(2,1)S(1)}, bf16[8,16,1024]{2,1,0:T(8,128)(2,1)S(1)}, u32[]{:S(2)}, u32[]{:S(2)}) collective-permute-start(bf16[8,16,1024]{2,1,0:T(8,128)(2,1)S(1)} %get-tuple-element.29), channel_id=1, source_target_pairs={{16,0},{18,2},{20,4},{22,6},{24,8},{26,10},{28,12},{30,14},{80,64}... | collective-permute-start | bytes 786440 | tf_op jit(solution)/shard_map/ppermute | solution.py:55
  24.8 7.6 %collective-permute-start.1 = (bf16[8,16,1024]{2,1,0:T(8,128)(2,1)S(1)}, bf16[8,16,1024]{2,1,0:T(8,128)(2,1)S(1)}, u32[]{:S(2)}, u32[]{:S(2)}) collective-permute-start(bf16[8,16,1024]{2,1,0:T(8,128)(2,1)S(1)} %get-tuple-element.30), channel_id=1, source_target_pairs={{48,0},{50,2},{52,4},{54,6},{56,8},{58,10},{60,12},{62,14},{112,64... | collective-permute-start | bytes 786440 | tf_op jit(solution)/shard_map/ppermute | solution.py:55
  24.8 10.4 %collective-permute-start.2 = (bf16[8,16,1024]{2,1,0:T(8,128)(2,1)S(1)}, bf16[8,16,1024]{2,1,0:T(8,128)(2,1)S(1)}, u32[]{:S(2)}, u32[]{:S(2)}) collective-permute-start(bf16[8,16,1024]{2,1,0:T(8,128)(2,1)S(1)} %get-tuple-element.29), channel_id=1, source_target_pairs={{48,0},{50,2},{52,4},{54,6},{56,8},{58,10},{60,12},{62,14},{112,64... | collective-permute-start | bytes 786440 | tf_op jit(solution)/shard_map/ppermute | solution.py:55
  25.6 9.6 %collective-permute-start.3 = (bf16[8,16,1024]{2,1,0:T(8,128)(2,1)S(1)}, bf16[8,16,1024]{2,1,0:T(8,128)(2,1)S(1)}, u32[]{:S(2)}, u32[]{:S(2)}) collective-permute-start(bf16[8,16,1024]{2,1,0:T(8,128)(2,1)S(1)} %get-tuple-element.30), channel_id=1, source_target_pairs={{16,0},{18,2},{20,4},{22,6},{24,8},{26,10},{28,12},{30,14},{80,64}... | collective-permute-start | bytes 786440 | tf_op jit(solution)/shard_map/ppermute | solution.py:55
  28.7 7.5 %collective-permute-start.6 = (bf16[8,16,1024]{2,1,0:T(8,128)(2,1)S(1)}, bf16[8,16,1024]{2,1,0:T(8,128)(2,1)S(1)}, u32[]{:S(2)}, u32[]{:S(2)}) collective-permute-start(bf16[8,16,1024]{2,1,0:T(8,128)(2,1)S(1)} %collective-permute-done.4.refs_3_), channel_id=1, source_target_pairs={{16,0},{18,2},{20,4},{22,6},{24,8},{26,10},{28,12},{30,14},{80,64}... | collective-permute-start | bytes 786440 | tf_op jit(solution)/shard_map/ppermute | solution.py:55
  32.4 7.6 %collective-permute-start.5 = (bf16[8,16,1024]{2,1,0:T(8,128)(2,1)S(1)}, bf16[8,16,1024]{2,1,0:T(8,128)(2,1)S(1)}, u32[]{:S(2)}, u32[]{:S(2)}) collective-permute-start(bf16[8,16,1024]{2,1,0:T(8,128)(2,1)S(1)} %collective-permute-done.1.refs_0_), channel_id=1, source_target_pairs={{48,0},{50,2},{52,4},{54,6},{56,8},{58,10},{60,12},{62,14},{112,64... | collective-permute-start | bytes 786440 | tf_op jit(solution)/shard_map/ppermute | solution.py:55
  70.8 17.1 %copy-start = (bf16[8,16384]{1,0:T(8,128)(2,1)S(1)}, bf16[8,16384]{1,0:T(8,128)(2,1)}, u32[]{:S(2)}) copy-start(bf16[8,16384]{1,0:T(8,128)(2,1)} %view_two.1) | copy-start | bytes 786436
  70.8 17.1 %copy-start.1 = (bf16[8,16384]{1,0:T(8,128)(2,1)S(1)}, bf16[8,16384]{1,0:T(8,128)(2,1)}, u32[]{:S(2)}) copy-start(bf16[8,16384]{1,0:T(8,128)(2,1)} %view_one.1) | copy-start | bytes 786436
  72.6 13.6 %all-to-all-start.3 = ((bf16[16,16,1024]{2,1,0:T(8,128)(2,1)}), bf16[16,16,1024]{2,1,0:T(8,128)(2,1)S(1)}, u32[]{:S(2)}, u32[]{:S(2)}) async-start(bf16[16,16,1024]{2,1,0:T(8,128)(2,1)} %get-tuple-element.22), calls=%async_computation.3 | async-start | bytes 1048576 | tf_op jit(solution)/shard_map/all_to_all | solution.py:51
  76.2 3.7 %collective-permute-start.9 = (f32[8,128]{1,0:T(8,128)S(1)}, f32[8,128]{1,0:T(8,128)S(1)}, u32[]{:S(2)}, u32[]{:S(2)}) collective-permute-start(f32[8,128]{1,0:T(8,128)S(1)} %get-tuple-element.23), channel_id=1, source_target_pairs={{16,0},{18,2},{20,4},{22,6},{24,8},{26,10},{28,12},{30,14},{80,64}... | collective-permute-start | bytes 12296 | tf_op jit(solution)/shard_map/ppermute | solution.py:55
  76.3 4.9 %collective-permute-start.8 = (f32[8,128]{1,0:T(8,128)S(1)}, f32[8,128]{1,0:T(8,128)S(1)}, u32[]{:S(2)}, u32[]{:S(2)}) collective-permute-start(f32[8,128]{1,0:T(8,128)S(1)} %get-tuple-element.23), channel_id=1, source_target_pairs={{48,0},{50,2},{52,4},{54,6},{56,8},{58,10},{60,12},{62,14},{112,64... | collective-permute-start | bytes 12296 | tf_op jit(solution)/shard_map/ppermute | solution.py:55
  78.3 5.1 %collective-permute-start.7 = (f32[8,128]{1,0:T(8,128)S(1)}, f32[8,128]{1,0:T(8,128)S(1)}, u32[]{:S(2)}, u32[]{:S(2)}) collective-permute-start(f32[8,128]{1,0:T(8,128)S(1)} %get-tuple-element.23), channel_id=1, source_target_pairs={{32,0},{34,2},{36,4},{38,6},{40,8},{42,10},{44,12},{46,14},{96,64}... | collective-permute-start | bytes 12296 | tf_op jit(solution)/shard_map/ppermute | solution.py:55
  86.3 1.6 %collective-permute-start.10 = (bf16[16,8,1024]{2,1,0:T(8,128)(2,1)S(1)}, bf16[16,8,1024]{2,1,0:T(8,128)(2,1)S(1)}, u32[]{:S(2)}, u32[]{:S(2)}) collective-permute-start(bf16[16,8,1024]{2,1,0:T(8,128)(2,1)S(1)} %slice.14), channel_id=1, source_target_pairs={{0,1},{1,0},{2,3},{3,2},{4,5},{5,4},{6,7},{7,6},{8,9},{9,8},{10,11... | collective-permute-start | bytes 786440 | tf_op jit(solution)/shard_map/ppermute | solution.py:55
  86.4 1.5 %collective-permute-start.11 = (f32[8,128]{1,0:T(8,128)S(1)}, f32[8,128]{1,0:T(8,128)S(1)}, u32[]{:S(2)}, u32[]{:S(2)}) collective-permute-start(f32[8,128]{1,0:T(8,128)S(1)} %add_add_fusion.mine), channel_id=1, source_target_pairs={{0,1},{1,0},{2,3},{3,2},{4,5},{5,4},{6,7},{7,6},{8,9},{9,8},{10,11... | collective-permute-start | bytes 12296 | tf_op jit(solution)/shard_map/ppermute | solution.py:55

commit v7 on v6

--- a/solution.py
+++ b/solution.py
@@ -18,7 +18,7 @@
 FINE = ("zh", "x", "y", "zl", "core")
 SIZES = (2, 4, 4, 2, 2)
 LANES = 128
-CHUNK = 256
+CHUNK = 512
 CONTRACT_LAST = (((1,), (1,)), ((), ()))
 CONTRACT_FIRST = (((1,), (0,)), ((), ()))
 
@@ -63,16 +63,36 @@
     return jnp.where(core == 0, first, second)
 
 
-def pack_kernel(factor, place_in, keep, give, got, packed, squares, place):
+def choose_kernel(
+    factor, core, place_in, view_one, view_two, keep, squares, place, here, sems
+):
+    place[0] = place_in[0]
+    copies = [
+        pltpu.make_async_copy(view, here.at[v], sems.at[v])
+        for v, view in enumerate((view_one, view_two))
+    ]
+    for copy in copies:
+        copy.start()
+    for copy in copies:
+        copy.wait()
+    width = squares.shape[1]
+    total = 0.0
+    for start in range(0, keep.shape[1], width):
+        cut = pl.ds(start, width)
+        first = here[0, :, cut].astype(jnp.float32)
+        second = here[1, :, cut].astype(jnp.float32)
+        keep[:, cut] = pick(core[0], first, second).astype(jnp.bfloat16)
+        total += (first - second) ** 2
+    squares[...] = factor * total
+
+
+def pack_kernel(core, keep, got_one, got_two, packed):
     parts, rows, width = packed.shape
-    place[0] = place_in[0]
-    total = 0.0
     for c in range(parts):
         cut = pl.ds(c * width, width)
-        mine, other, more = [ref[:, cut].astype(jnp.float32) for ref in (keep, give, got)]
+        mine, first, second = [ref[:, cut].astype(jnp.float32) for ref in (keep, got_one, got_two)]
+        more = pick(core[0], first, second)
         packed[c] = jnp.concatenate([mine, more], axis=0).astype(jnp.bfloat16)
-        total += (mine - other) ** 2
-    squares[...] = factor * total
 
 
 def gram_kernel(sizes, pull, own, *refs):
@@ -214,20 +234,33 @@
     place = place.astype(jnp.int32).reshape(1)
     smem = pl.BlockSpec(memory_space=pltpu.SMEM)
     vmem = pl.BlockSpec(memory_space=pltpu.VMEM)
-
-    keep, give = pick(core[0], view_one, view_two), pick(core[0], view_two, view_one)
-    blocks, pull, place = pl.pallas_call(
-        functools.partial(pack_kernel, inv_weight / (batch_rows * feature_count)),
-        in_specs=[smem, vmem, vmem, vmem],
+    hbm = pl.BlockSpec(memory_space=pltpu.HBM)
+
+    got_one, got_two = move(view_one, SWAP), move(view_two, SWAP)
+    keep, pull, place = pl.pallas_call(
+        functools.partial(choose_kernel, inv_weight / (batch_rows * feature_count)),
+        in_specs=[smem, smem, hbm, hbm],
         out_specs=[vmem, vmem, smem],
+        scratch_shapes=[
+            pltpu.VMEM((2,) + view_one.shape, jnp.bfloat16),
+            pltpu.SemaphoreType.DMA((2,)),
+        ],
         out_shape=[
-            jax.ShapeDtypeStruct((feature_parts, rows, width), jnp.bfloat16),
+            jax.ShapeDtypeStruct(view_one.shape, jnp.bfloat16),
             jax.ShapeDtypeStruct((shard_rows, width), jnp.float32),
             jax.ShapeDtypeStruct((1,), jnp.int32),
         ],
         compiler_params=room(4),
+        name="choose_view",
+    )(core, place, *[pltpu.with_memory_space_constraint(v, pltpu.HBM) for v in (view_one, view_two)])
+    blocks = pl.pallas_call(
+        pack_kernel,
+        in_specs=[smem, vmem, vmem, vmem],
+        out_specs=vmem,
+        out_shape=jax.ShapeDtypeStruct((feature_parts, rows, width), jnp.bfloat16),
+        compiler_params=room(4),
         name="pack_rows",
-    )(place, keep, give, move(give, SWAP))
+    )(core, keep, got_one, got_two)
     own = exchange(blocks)
     half = feature_parts // 2
     first, second = own[:half], own[half:]

time: 90.5 us -> 89.5 us (0.989)
  waiting for transfers between devices: 18.7 us -> 17.3 us
  other arithmetic: 1.08 us -> 0.01 us
  Pallas kernels: 6.6 us -> 7.66 us
    ppermute x12 -> x13, waiting for transfers between devices: 15.9 us -> 14.4 us  [move(): return lax.ppermute(block, FINE, pairs)]
    select_n x1 -> x0, other arithmetic: 1.07 us -> none  [pick(): return jnp.where(core == 0, first, second)]
    pallas_call x1 -> x2, Pallas kernels: 0.56 us -> 1.62 us  [the longest x1 1.56 us: body(): pl.pallas_call(functools.partial(choose_kernel, inv_weight / (batch_rows...]
    ppermute x12 -> x13, starting transfers between devices: 12.2 us -> 12.7 us  [move(): return lax.ppermute(block, FINE, pairs)]
  transfers between devices with their start and end apart: 13 -> 14, of which waited for: 10 -> 9; matrix products, arithmetic and copies ran while one was open for 0% -> 0% of each run, Pallas kernels for 0% -> 2%
where the time goes in v7:
time: 89.5 us; the launch traced here: 88.1 us
  blocking collectives  46.1 us (52%)
  waiting for transfers between devices  17.3 us (19%)
  starting transfers between devices  16.3 us (18%)
  Pallas kernels  7.66 us (9%)
    all_to_all x3, blocking collectives, exchange(): lax.all_to_all(blocks, FINE, 0, 0, tiled=True, axis_index_groups=GROUPS)  46.1 us
    ppermute x13, waiting for transfers between devices, move(): return lax.ppermute(block, FINE, pairs)  14.4 us
    ppermute x13, starting transfers between devices, move(): return lax.ppermute(block, FINE, pairs)  12.7 us
    all_to_all x1, starting transfers between devices, exchange(): lax.all_to_all(blocks, FINE, 0, 0, tiled=True, axis_index_groups=GROUPS)  3.57 us
    all_to_all x1, waiting for transfers between devices, exchange(): lax.all_to_all(blocks, FINE, 0, 0, tiled=True, axis_index_groups=GROUPS)  2.85 us
    pallas_call x1, Pallas kernels, body(): pl.pallas_call(functools.partial(gram_kernel, sizes), in_specs=[vmem] * (...  2.15 us
    pallas_call x1, Pallas kernels, body(): pl.pallas_call(functools.partial(grad_kernel, sizes), in_specs=[vmem] * 4...  1.84 us
  transfers between devices with their start and end apart: 14, of which 9 were waited for; matrix products, arithmetic and copies ran while one was open for 0% of the time, Pallas kernels for 2%

profile of v7, /device:TPU:0, one launch (start us, length us, event | category | flops | bytes accessed | tf_op | source)
XLA Modules:
  0.0 88.1 jit_solution(1385411480049872670)
XLA Ops:
  1.2 1.6 %choose_view.1 = (bf16[8,16384]{1,0:T(8,128)(2,1)S(1)}, f32[8,1024]{1,0:T(8,128)S(1)}, s32[1]{0:T(128)}) custom-call(s32[1]{0:T(128)} %bitcast.core, s32[1]{0:T(128)} %bitcast.1.place_in, bf16[8,16384]{1,0:T(8,128)(2,1)} %view_one.3, bf16[8,16384]{1,0:T(8,128)(2,1)} %view_two.3), custom_call_target="tpu_custom_call" | custom-call | tf_op jit(solution)/shard_map/choose_view/pallas_call | solution.py:240
  2.9 18.3 %all_to_all.20.own = bf16[16,16,1024]{2,1,0:T(8,128)(2,1)S(1)} all-to-all(bf16[16,16,1024]{2,1,0:T(8,128)(2,1)S(1)} %pack_rows.1), channel_id=1, replica_groups={{0,2,4,6,8,10,12,14,64,66,68,70,72,74,76,78},{16,18,20,22,24,26,28,30,8..., dimensions={0} | all-to-all | bytes 1048576 | tf_op jit(solution)/shard_map/all_to_all | solution.py:51
  21.3 2.5 %collective-permute-start.5 = (bf16[8,16,1024]{2,1,0:T(8,128)(2,1)S(1)}, bf16[8,16,1024]{2,1,0:T(8,128)(2,1)S(1)}, u32[]{:S(2)}, u32[]{:S(2)}) collective-permute-start(bf16[8,16,1024]{2,1,0:T(8,128)(2,1)S(1)} %get-tuple-element.29), channel_id=1, source_target_pairs={{16,0},{18,2},{20,4},{22,6},{24,8},{26,10},{28,12},{30,14},{80,64}... | collective-permute-start | bytes 786440 | tf_op jit(solution)/shard_map/ppermute | solution.py:55
  23.8 0.8 collective-permute-start.3
  24.6 2.5 %collective-permute-start.4 = (bf16[8,16,1024]{2,1,0:T(8,128)(2,1)S(1)}, bf16[8,16,1024]{2,1,0:T(8,128)(2,1)S(1)}, u32[]{:S(2)}, u32[]{:S(2)}) collective-permute-start(bf16[8,16,1024]{2,1,0:T(8,128)(2,1)S(1)} %get-tuple-element.30), channel_id=1, source_target_pairs={{16,0},{18,2},{20,4},{22,6},{24,8},{26,10},{28,12},{30,14},{80,64}... | collective-permute-start | bytes 786440 | tf_op jit(solution)/shard_map/ppermute | solution.py:55
  27.1 0.7 collective-permute-done.5.refs_3_
  27.7 3.7 %collective-permute-start.7 = (bf16[8,16,1024]{2,1,0:T(8,128)(2,1)S(1)}, bf16[8,16,1024]{2,1,0:T(8,128)(2,1)S(1)}, u32[]{:S(2)}, u32[]{:S(2)}) collective-permute-start(bf16[8,16,1024]{2,1,0:T(8,128)(2,1)S(1)} %collective-permute-done.5.refs_3_), channel_id=1, source_target_pairs={{16,0},{18,2},{20,4},{22,6},{24,8},{26,10},{28,12},{30,14},{80,64}... | collective-permute-start | bytes 786440 | tf_op jit(solution)/shard_map/ppermute | solution.py:55
  31.4 2.8 %collective-permute-done.3.refs_1_ = bf16[8,16,1024]{2,1,0:T(8,128)(2,1)S(1)} collective-permute-done((bf16[8,16,1024]{2,1,0:T(8,128)(2,1)S(1)}, bf16[8,16,1024]{2,1,0:T(8,128)(2,1)S(1)}, u32[]{:S(2)}, u32[]{:S(2)}) %collective-permute-start.3) | collective-permute-done | bytes 262176 | tf_op jit(solution)/shard_map/ppermute | solution.py:55
  34.2 1.1 %collective-permute-done.7.refs_5_ = bf16[8,16,1024]{2,1,0:T(8,128)(2,1)S(1)} collective-permute-done((bf16[8,16,1024]{2,1,0:T(8,128)(2,1)S(1)}, bf16[8,16,1024]{2,1,0:T(8,128)(2,1)S(1)}, u32[]{:S(2)}, u32[]{:S(2)}) %collective-permute-start.7) | collective-permute-done | bytes 262176 | tf_op jit(solution)/shard_map/ppermute | solution.py:55
  35.3 3.7 %collective-permute-done.6.refs_4_ = bf16[8,16,1024]{2,1,0:T(8,128)(2,1)S(1)} collective-permute-done((bf16[8,16,1024]{2,1,0:T(8,128)(2,1)S(1)}, bf16[8,16,1024]{2,1,0:T(8,128)(2,1)S(1)}, u32[]{:S(2)}, u32[]{:S(2)}) %collective-permute-start.6) | collective-permute-done | bytes 262176 | tf_op jit(solution)/shard_map/ppermute | solution.py:55
  39.0 2.2 %gram_part.1 = (bf16[1024,1024]{1,0:T(8,128)(2,1)S(1)}, bf16[16,16,1024]{2,1,0:T(8,128)(2,1)S(1)}, f32[4,1024]{1,0:T(4,128)S(1)}) custom-call(f32[8,1024]{1,0:T(8,128)S(1)} %get-tuple-element.17.pull, bf16[16,16,1024]{2,1,0:T(8,128)(2,1)S(1)} %all_to_all.20.own, bf16[8,16,1024]{2,1,0:T(8,128)(2,1)S(1)} %collective-permute-done.2.refs_0_, ...), custom_call_target="tpu_custom_call" | custom-call | tf_op jit(solution)/shard_map/gram_part/pallas_call | solution.py:271
  41.1 14.4 %all_to_all.21.pieces = bf16[16,16,1024]{2,1,0:T(8,128)(2,1)S(1)} all-to-all(bf16[16,16,1024]{2,1,0:T(8,128)(2,1)S(1)} %get-tuple-element.19), channel_id=1, replica_groups={{0,2,4,6,8,10,12,14,64,66,68,70,72,74,76,78},{16,18,20,22,24,26,28,30,8..., dimensions={0} | all-to-all | bytes 1048576 | tf_op jit(solution)/shard_map/all_to_all | solution.py:51
  55.5 0.9 %gram_sum.1 = bf16[16,16,1024]{2,1,0:T(8,128)(2,1)S(1)} custom-call(s32[1]{0:T(128)} %get-tuple-element.16.place, bf16[16,16,1024]{2,1,0:T(8,128)(2,1)S(1)} %all_to_all.21.pieces, f32[4,1024]{1,0:T(4,128)S(1)} %get-tuple-element.20.stats), custom_call_target="tpu_custom_call" | custom-call | tf_op jit(solution)/shard_map/gram_sum/pallas_call | solution.py:285
  56.4 13.3 %all_to_all.22.gram = bf16[16,16,1024]{2,1,0:T(8,128)(2,1)S(1)} all-to-all(bf16[16,16,1024]{2,1,0:T(8,128)(2,1)S(1)} %gram_sum.1), channel_id=1, replica_groups={{0,2,4,6,8,10,12,14,64,66,68,70,72,74,76,78},{16,18,20,22,24,26,28,30,8..., dimensions={0} | all-to-all | bytes 1048576 | tf_op jit(solution)/shard_map/all_to_all | solution.py:51
  69.8 1.8 %grad_rows.1 = (bf16[16,16,1024]{2,1,0:T(8,128)(2,1)}, f32[8,128]{1,0:T(8,128)S(1)}) custom-call(bf16[16,16,1024]{2,1,0:T(8,128)(2,1)S(1)} %all_to_all.22.gram, bf16[1024,1024]{1,0:T(8,128)(2,1)S(1)} %get-tuple-element.21.rounded, bf16[16,16,1024]{2,1,0:T(8,128)(2,1)S(1)} %all_to_all.20.own, f32[4,1024]{1,0:T(4,128)S(1)} %get-tuple-element.20.stats), custom_call_target="tpu_custom_call" | custom-call | tf_op jit(solution)/shard_map/grad_rows/pallas_call | solution.py:295
  71.6 3.6 %all-to-all-start.3 = ((bf16[16,16,1024]{2,1,0:T(8,128)(2,1)}), bf16[16,16,1024]{2,1,0:T(8,128)(2,1)S(1)}, u32[]{:S(2)}, u32[]{:S(2)}) async-start(bf16[16,16,1024]{2,1,0:T(8,128)(2,1)} %get-tuple-element.22), calls=%async_computation.3 | async-start | bytes 1048576 | tf_op jit(solution)/shard_map/all_to_all | solution.py:51
  75.3 2.0 %collective-permute-start.9 = (f32[8,128]{1,0:T(8,128)S(1)}, f32[8,128]{1,0:T(8,128)S(1)}, u32[]{:S(2)}, u32[]{:S(2)}) collective-permute-start(f32[8,128]{1,0:T(8,128)S(1)} %get-tuple-element.23), channel_id=1, source_target_pairs={{48,0},{50,2},{52,4},{54,6},{56,8},{58,10},{60,12},{62,14},{112,64... | collective-permute-start | bytes 12296 | tf_op jit(solution)/shard_map/ppermute | solution.py:55
  77.3 1.6 %collective-permute-done.10 = f32[8,128]{1,0:T(8,128)S(1)} collective-permute-done((f32[8,128]{1,0:T(8,128)S(1)}, f32[8,128]{1,0:T(8,128)S(1)}, u32[]{:S(2)}, u32[]{:S(2)}) %collective-permute-start.10) | collective-permute-done | bytes 4128 | tf_op jit(solution)/shard_map/ppermute | solution.py:55
  78.9 1.3 %collective-permute-done.9 = f32[8,128]{1,0:T(8,128)S(1)} collective-permute-done((f32[8,128]{1,0:T(8,128)S(1)}, f32[8,128]{1,0:T(8,128)S(1)}, u32[]{:S(2)}, u32[]{:S(2)}) %collective-permute-start.9) | collective-permute-done | bytes 4128 | tf_op jit(solution)/shard_map/ppermute | solution.py:55
  80.2 2.2 %collective-permute-done.8 = f32[8,128]{1,0:T(8,128)S(1)} collective-permute-done((f32[8,128]{1,0:T(8,128)S(1)}, f32[8,128]{1,0:T(8,128)S(1)}, u32[]{:S(2)}, u32[]{:S(2)}) %collective-permute-start.8) | collective-permute-done | bytes 4128 | tf_op jit(solution)/shard_map/ppermute | solution.py:55
  82.4 2.8 %all-to-all-done.3.recv = bf16[16,16,1024]{2,1,0:T(8,128)(2,1)S(1)} async-done(((bf16[16,16,1024]{2,1,0:T(8,128)(2,1)}), bf16[16,16,1024]{2,1,0:T(8,128)(2,1)S(1)}, u32[]{:S(2)}, u32[]{:S(2)}) %all-to-all-start.3) | async-done | bytes 524320 | tf_op jit(solution)/shard_map/all_to_all | solution.py:51
  85.4 0.5 collective-permute-start.12
  85.9 1.0 %collective-permute-done.12.other = f32[8,128]{1,0:T(8,128)S(1)} collective-permute-done((f32[8,128]{1,0:T(8,128)S(1)}, f32[8,128]{1,0:T(8,128)S(1)}, u32[]{:S(2)}, u32[]{:S(2)}) %collective-permute-start.12) | collective-permute-done | bytes 4128 | tf_op jit(solution)/shard_map/ppermute | solution.py:55
  86.9 1.1 %add_pull.1 = (f32[8,16384]{1,0:T(8,128)}, f32[8,16384]{1,0:T(8,128)}, f32[1]{0:T(128)}) custom-call(s32[1]{0:T(128)} %bitcast.core, bf16[16,16,1024]{2,1,0:T(8,128)(2,1)S(1)} %all-to-all-done.3.recv, bf16[16,8,1024]{2,1,0:T(8,128)(2,1)S(1)} %collective-permute-done.11.got, f32[8,128]{1,0:T(8,128)S(1)} %add_add_fusion.mine, ...), custom_call_target="tpu_custom_call" | custom-call | tf_op jit(solution)/shard_map/add_pull/pallas_call | solution.py:312
  (20 shorter events, 0.9 us)
Async XLA Ops:
  0.6 2.2 %collective-permute-start = (bf16[8,16384]{1,0:T(8,128)(2,1)}, bf16[8,16384]{1,0:T(8,128)(2,1)S(1)}, u32[]{:S(2)}, u32[]{:S(2)}) collective-permute-start(bf16[8,16384]{1,0:T(8,128)(2,1)} %view_one.3), channel_id=1, source_target_pairs={{0,1},{1,0},{2,3},{3,2},{4,5},{5,4},{6,7},{7,6},{8,9},{9,8},{10,11... | collective-permute-start | bytes 786440 | tf_op jit(solution)/shard_map/ppermute | solution.py:55
  0.7 2.1 %collective-permute-start.1 = (bf16[8,16384]{1,0:T(8,128)(2,1)}, bf16[8,16384]{1,0:T(8,128)(2,1)S(1)}, u32[]{:S(2)}, u32[]{:S(2)}) collective-permute-start(bf16[8,16384]{1,0:T(8,128)(2,1)} %view_two.3), channel_id=1, source_target_pairs={{0,1},{1,0},{2,3},{3,2},{4,5},{5,4},{6,7},{7,6},{8,9},{9,8},{10,11... | collective-permute-start | bytes 786440 | tf_op jit(solution)/shard_map/ppermute | solution.py:55
  21.3 6.4 %collective-permute-start.5 = (bf16[8,16,1024]{2,1,0:T(8,128)(2,1)S(1)}, bf16[8,16,1024]{2,1,0:T(8,128)(2,1)S(1)}, u32[]{:S(2)}, u32[]{:S(2)}) collective-permute-start(bf16[8,16,1024]{2,1,0:T(8,128)(2,1)S(1)} %get-tuple-element.29), channel_id=1, source_target_pairs={{16,0},{18,2},{20,4},{22,6},{24,8},{26,10},{28,12},{30,14},{80,64}... | collective-permute-start | bytes 786440 | tf_op jit(solution)/shard_map/ppermute | solution.py:55
  23.8 7.6 %collective-permute-start.2 = (bf16[8,16,1024]{2,1,0:T(8,128)(2,1)S(1)}, bf16[8,16,1024]{2,1,0:T(8,128)(2,1)S(1)}, u32[]{:S(2)}, u32[]{:S(2)}) collective-permute-start(bf16[8,16,1024]{2,1,0:T(8,128)(2,1)S(1)} %get-tuple-element.30), channel_id=1, source_target_pairs={{48,0},{50,2},{52,4},{54,6},{56,8},{58,10},{60,12},{62,14},{112,64... | collective-permute-start | bytes 786440 | tf_op jit(solution)/shard_map/ppermute | solution.py:55
  23.8 10.4 %collective-permute-start.3 = (bf16[8,16,1024]{2,1,0:T(8,128)(2,1)S(1)}, bf16[8,16,1024]{2,1,0:T(8,128)(2,1)S(1)}, u32[]{:S(2)}, u32[]{:S(2)}) collective-permute-start(bf16[8,16,1024]{2,1,0:T(8,128)(2,1)S(1)} %get-tuple-element.29), channel_id=1, source_target_pairs={{48,0},{50,2},{52,4},{54,6},{56,8},{58,10},{60,12},{62,14},{112,64... | collective-permute-start | bytes 786440 | tf_op jit(solution)/shard_map/ppermute | solution.py:55
  24.6 9.6 %collective-permute-start.4 = (bf16[8,16,1024]{2,1,0:T(8,128)(2,1)S(1)}, bf16[8,16,1024]{2,1,0:T(8,128)(2,1)S(1)}, u32[]{:S(2)}, u32[]{:S(2)}) collective-permute-start(bf16[8,16,1024]{2,1,0:T(8,128)(2,1)S(1)} %get-tuple-element.30), channel_id=1, source_target_pairs={{16,0},{18,2},{20,4},{22,6},{24,8},{26,10},{28,12},{30,14},{80,64}... | collective-permute-start | bytes 786440 | tf_op jit(solution)/shard_map/ppermute | solution.py:55
  27.7 7.5 %collective-permute-start.7 = (bf16[8,16,1024]{2,1,0:T(8,128)(2,1)S(1)}, bf16[8,16,1024]{2,1,0:T(8,128)(2,1)S(1)}, u32[]{:S(2)}, u32[]{:S(2)}) collective-permute-start(bf16[8,16,1024]{2,1,0:T(8,128)(2,1)S(1)} %collective-permute-done.5.refs_3_), channel_id=1, source_target_pairs={{16,0},{18,2},{20,4},{22,6},{24,8},{26,10},{28,12},{30,14},{80,64}... | collective-permute-start | bytes 786440 | tf_op jit(solution)/shard_map/ppermute | solution.py:55
  31.4 7.6 %collective-permute-start.6 = (bf16[8,16,1024]{2,1,0:T(8,128)(2,1)S(1)}, bf16[8,16,1024]{2,1,0:T(8,128)(2,1)S(1)}, u32[]{:S(2)}, u32[]{:S(2)}) collective-permute-start(bf16[8,16,1024]{2,1,0:T(8,128)(2,1)S(1)} %collective-permute-done.2.refs_0_), channel_id=1, source_target_pairs={{48,0},{50,2},{52,4},{54,6},{56,8},{58,10},{60,12},{62,14},{112,64... | collective-permute-start | bytes 786440 | tf_op jit(solution)/shard_map/ppermute | solution.py:55
  69.8 17.1 %copy-start = (bf16[8,16384]{1,0:T(8,128)(2,1)S(1)}, bf16[8,16384]{1,0:T(8,128)(2,1)}, u32[]{:S(2)}) copy-start(bf16[8,16384]{1,0:T(8,128)(2,1)} %view_one.3) | copy-start | bytes 786436
  69.8 17.1 %copy-start.1 = (bf16[8,16384]{1,0:T(8,128)(2,1)S(1)}, bf16[8,16384]{1,0:T(8,128)(2,1)}, u32[]{:S(2)}) copy-start(bf16[8,16384]{1,0:T(8,128)(2,1)} %view_two.3) | copy-start | bytes 786436
  71.6 13.6 %all-to-all-start.3 = ((bf16[16,16,1024]{2,1,0:T(8,128)(2,1)}), bf16[16,16,1024]{2,1,0:T(8,128)(2,1)S(1)}, u32[]{:S(2)}, u32[]{:S(2)}) async-start(bf16[16,16,1024]{2,1,0:T(8,128)(2,1)} %get-tuple-element.22), calls=%async_computation.3 | async-start | bytes 1048576 | tf_op jit(solution)/shard_map/all_to_all | solution.py:51
  75.2 3.7 %collective-permute-start.10 = (f32[8,128]{1,0:T(8,128)S(1)}, f32[8,128]{1,0:T(8,128)S(1)}, u32[]{:S(2)}, u32[]{:S(2)}) collective-permute-start(f32[8,128]{1,0:T(8,128)S(1)} %get-tuple-element.23), channel_id=1, source_target_pairs={{16,0},{18,2},{20,4},{22,6},{24,8},{26,10},{28,12},{30,14},{80,64}... | collective-permute-start | bytes 12296 | tf_op jit(solution)/shard_map/ppermute | solution.py:55
  75.3 4.9 %collective-permute-start.9 = (f32[8,128]{1,0:T(8,128)S(1)}, f32[8,128]{1,0:T(8,128)S(1)}, u32[]{:S(2)}, u32[]{:S(2)}) collective-permute-start(f32[8,128]{1,0:T(8,128)S(1)} %get-tuple-element.23), channel_id=1, source_target_pairs={{48,0},{50,2},{52,4},{54,6},{56,8},{58,10},{60,12},{62,14},{112,64... | collective-permute-start | bytes 12296 | tf_op jit(solution)/shard_map/ppermute | solution.py:55
  77.3 5.1 %collective-permute-start.8 = (f32[8,128]{1,0:T(8,128)S(1)}, f32[8,128]{1,0:T(8,128)S(1)}, u32[]{:S(2)}, u32[]{:S(2)}) collective-permute-start(f32[8,128]{1,0:T(8,128)S(1)} %get-tuple-element.23), channel_id=1, source_target_pairs={{32,0},{34,2},{36,4},{38,6},{40,8},{42,10},{44,12},{46,14},{96,64}... | collective-permute-start | bytes 12296 | tf_op jit(solution)/shard_map/ppermute | solution.py:55
  85.3 1.6 %collective-permute-start.11 = (bf16[16,8,1024]{2,1,0:T(8,128)(2,1)S(1)}, bf16[16,8,1024]{2,1,0:T(8,128)(2,1)S(1)}, u32[]{:S(2)}, u32[]{:S(2)}) collective-permute-start(bf16[16,8,1024]{2,1,0:T(8,128)(2,1)S(1)} %slice.14), channel_id=1, source_target_pairs={{0,1},{1,0},{2,3},{3,2},{4,5},{5,4},{6,7},{7,6},{8,9},{9,8},{10,11... | collective-permute-start | bytes 786440 | tf_op jit(solution)/shard_map/ppermute | solution.py:55
  85.4 1.5 %collective-permute-start.12 = (f32[8,128]{1,0:T(8,128)S(1)}, f32[8,128]{1,0:T(8,128)S(1)}, u32[]{:S(2)}, u32[]{:S(2)}) collective-permute-start(f32[8,128]{1,0:T(8,128)S(1)} %add_add_fusion.mine), channel_id=1, source_target_pairs={{0,1},{1,0},{2,3},{3,2},{4,5},{5,4},{6,7},{7,6},{8,9},{9,8},{10,11... | collective-permute-start | bytes 12296 | tf_op jit(solution)/shard_map/ppermute | solution.py:55

commit v8 on v7

--- a/solution.py
+++ b/solution.py
@@ -95,6 +95,10 @@
         packed[c] = jnp.concatenate([mine, more], axis=0).astype(jnp.bfloat16)
 
 
+def folded(block):
+    return jnp.sum(block.reshape(-1, 8, block.shape[1]), axis=0)
+
+
 def gram_kernel(sizes, pull, own, *refs):
     copies, (rounded, part, stats) = refs[:-3], refs[-3:]
     batch_rows, feature_count, row_parts = sizes
@@ -102,19 +106,22 @@
     width = own.shape[2]
     for start in range(0, width, CHUNK):
         cut = pl.ds(start, CHUNK)
-        values = [ref[:, :, cut].reshape(-1, CHUNK).astype(jnp.float32) for ref in (own,) + copies]
-        mean = sum(jnp.sum(a, axis=0, keepdims=True) for a in values) / batch_rows
-        values = [a - mean for a in values]
-        square = sum(jnp.sum(a * a, axis=0, keepdims=True) for a in values)
+        blocks = [(ref, c) for ref in (own,) + copies for c in range(ref.shape[0])]
+        total = 0.0
+        for ref, c in blocks:
+            total += folded(ref[c, :, cut].astype(jnp.float32))
+        mean = jnp.sum(total, axis=0, keepdims=True) / batch_rows
+        square, energy = 0.0, 0.0
+        for i, (ref, c) in enumerate(blocks):
+            a = ref[c, :, cut].astype(jnp.float32) - mean
+            square += folded(a * a)
+            a = a.astype(jnp.bfloat16)
+            rounded[pl.ds(i * a.shape[0], a.shape[0]), cut] = a
+            a = a.astype(jnp.float32)
+            energy += folded(a * a)
+        square = jnp.sum(square, axis=0, keepdims=True)
+        energy = jnp.sum(energy, axis=0, keepdims=True)
         spread = jnp.sqrt(square / (batch_rows - 1) + epsilon)
-        energy = 0.0
-        row = 0
-        for a in values:
-            a = a.astype(jnp.bfloat16)
-            rounded[pl.ds(row, a.shape[0]), cut] = a
-            row += a.shape[0]
-            a = a.astype(jnp.float32)
-            energy += jnp.sum(a * a, axis=0, keepdims=True)
         share = var_weight / feature_count / row_parts * jnp.maximum(1.0 - spread, 0.0)
         share -= cov_weight / feature_count / row_parts * (energy / (batch_rows - 1)) ** 2
         share += jnp.sum(pull[:, cut], axis=0, keepdims=True)
@@ -262,12 +269,8 @@
         name="pack_rows",
     )(core, keep, got_one, got_two)
     own = exchange(blocks)
-    half = feature_parts // 2
-    first, second = own[:half], own[half:]
-    up_first, down_second = move(first, UP), move(second, DOWN)
-    up_second, down_first = move(second, UP), move(first, DOWN)
-    far_first, far_second = move(up_first, UP), move(down_second, DOWN)
-    copies = (up_first, up_second, down_first, down_second, far_first, far_second)
+    copies = (move(own, UP), move(own, DOWN), move(own, FAR))
+
     rounded, part, stats = pl.pallas_call(
         functools.partial(gram_kernel, sizes),
         in_specs=[vmem] * (2 + len(copies)),

time: 89.5 us -> 88.9 us (level)
  starting transfers between devices: 16.3 us -> 13.4 us
  waiting for transfers between devices: 17.3 us -> 18.9 us
  blocking collectives: 46.1 us -> 47 us
    ppermute x13 -> x10, starting transfers between devices: 12.7 us -> 9.67 us  [move(): return lax.ppermute(block, FINE, pairs)]
    ppermute x13 -> x10, waiting for transfers between devices: 14.4 us -> 16.1 us  [move(): return lax.ppermute(block, FINE, pairs)]
    all_to_all x3, blocking collectives: 46.1 us -> 47 us  [exchange(): lax.all_to_all(blocks, FINE, 0, 0, tiled=True, axis_index_groups=GROUPS)]
  transfers between devices with their start and end apart: 14 -> 11, of which waited for: 9 -> 7; matrix products, arithmetic and copies ran while one was open for 0% -> 0% of each run, Pallas kernels for 2% -> 2%
where the time goes in v8:
time: 88.9 us; the launch traced here: 87.5 us
  blocking collectives  47 us (53%)
  waiting for transfers between devices  18.9 us (21%)
  starting transfers between devices  13.4 us (15%)
  Pallas kernels  7.39 us (8%)
    all_to_all x3, blocking collectives, exchange(): lax.all_to_all(blocks, FINE, 0, 0, tiled=True, axis_index_groups=GROUPS)  47 us
    ppermute x10, waiting for transfers between devices, move(): return lax.ppermute(block, FINE, pairs)  16.1 us
    ppermute x10, starting transfers between devices, move(): return lax.ppermute(block, FINE, pairs)  9.67 us
    all_to_all x1, starting transfers between devices, exchange(): lax.all_to_all(blocks, FINE, 0, 0, tiled=True, axis_index_groups=GROUPS)  3.71 us
    all_to_all x1, waiting for transfers between devices, exchange(): lax.all_to_all(blocks, FINE, 0, 0, tiled=True, axis_index_groups=GROUPS)  2.88 us
    pallas_call x1, Pallas kernels, body(): pl.pallas_call(functools.partial(gram_kernel, sizes), in_specs=[vmem] * (...  1.89 us
    pallas_call x1, Pallas kernels, body(): pl.pallas_call(functools.partial(grad_kernel, sizes), in_specs=[vmem] * 4...  1.84 us
  transfers between devices with their start and end apart: 11, of which 7 were waited for; matrix products, arithmetic and copies ran while one was open for 0% of the time, Pallas kernels for 2%

profile of v8, /device:TPU:0, one launch (start us, length us, event | category | flops | bytes accessed | tf_op | source)
XLA Modules:
  0.0 87.5 jit_solution(3132512898578062735)
XLA Ops:
  0.7 0.5 collective-permute-start.1
  1.2 1.6 %choose_view.1 = (bf16[8,16384]{1,0:T(8,128)(2,1)S(1)}, f32[8,1024]{1,0:T(8,128)S(1)}, s32[1]{0:T(128)}) custom-call(s32[1]{0:T(128)} %bitcast.core, s32[1]{0:T(128)} %bitcast.1.place_in, bf16[8,16384]{1,0:T(8,128)(2,1)} %view_one.3, bf16[8,16384]{1,0:T(8,128)(2,1)} %view_two.3), custom_call_target="tpu_custom_call" | custom-call | tf_op jit(solution)/shard_map/choose_view/pallas_call | solution.py:247
  2.9 18.3 %all_to_all.20.own = bf16[16,16,1024]{2,1,0:T(8,128)(2,1)S(1)} all-to-all(bf16[16,16,1024]{2,1,0:T(8,128)(2,1)S(1)} %pack_rows.1), channel_id=1, replica_groups={{0,2,4,6,8,10,12,14,64,66,68,70,72,74,76,78},{16,18,20,22,24,26,28,30,8..., dimensions={0} | all-to-all | bytes 1048576 | tf_op jit(solution)/shard_map/all_to_all | solution.py:51
  21.2 2.7 %collective-permute-start.4 = (bf16[16,16,1024]{2,1,0:T(8,128)(2,1)S(1)}, bf16[16,16,1024]{2,1,0:T(8,128)(2,1)S(1)}, u32[]{:S(2)}, u32[]{:S(2)}) collective-permute-start(bf16[16,16,1024]{2,1,0:T(8,128)(2,1)S(1)} %all_to_all.20.own), channel_id=1, source_target_pairs={{32,0},{34,2},{36,4},{38,6},{40,8},{42,10},{44,12},{46,14},{96,64}... | collective-permute-start | bytes 1572872 | tf_op jit(solution)/shard_map/ppermute | solution.py:55
  24.0 1.1 %collective-permute-start.3 = (bf16[16,16,1024]{2,1,0:T(8,128)(2,1)S(1)}, bf16[16,16,1024]{2,1,0:T(8,128)(2,1)S(1)}, u32[]{:S(2)}, u32[]{:S(2)}) collective-permute-start(bf16[16,16,1024]{2,1,0:T(8,128)(2,1)S(1)} %all_to_all.20.own), channel_id=1, source_target_pairs={{16,0},{18,2},{20,4},{22,6},{24,8},{26,10},{28,12},{30,14},{80,64}... | collective-permute-start | bytes 1572872 | tf_op jit(solution)/shard_map/ppermute | solution.py:55
  25.1 0.9 %collective-permute-start.2 = (bf16[16,16,1024]{2,1,0:T(8,128)(2,1)S(1)}, bf16[16,16,1024]{2,1,0:T(8,128)(2,1)S(1)}, u32[]{:S(2)}, u32[]{:S(2)}) collective-permute-start(bf16[16,16,1024]{2,1,0:T(8,128)(2,1)S(1)} %all_to_all.20.own), channel_id=1, source_target_pairs={{48,0},{50,2},{52,4},{54,6},{56,8},{58,10},{60,12},{62,14},{112,64... | collective-permute-start | bytes 1572872 | tf_op jit(solution)/shard_map/ppermute | solution.py:55
  26.0 6.0 %collective-permute-done.4.refs_2_ = bf16[16,16,1024]{2,1,0:T(8,128)(2,1)S(1)} collective-permute-done((bf16[16,16,1024]{2,1,0:T(8,128)(2,1)S(1)}, bf16[16,16,1024]{2,1,0:T(8,128)(2,1)S(1)}, u32[]{:S(2)}, u32[]{:S(2)}) %collective-permute-start.4) | collective-permute-done | bytes 524320 | tf_op jit(solution)/shard_map/ppermute | solution.py:55
  32.0 5.3 %collective-permute-done.3.refs_1_ = bf16[16,16,1024]{2,1,0:T(8,128)(2,1)S(1)} collective-permute-done((bf16[16,16,1024]{2,1,0:T(8,128)(2,1)S(1)}, bf16[16,16,1024]{2,1,0:T(8,128)(2,1)S(1)}, u32[]{:S(2)}, u32[]{:S(2)}) %collective-permute-start.3) | collective-permute-done | bytes 524320 | tf_op jit(solution)/shard_map/ppermute | solution.py:55
  37.4 0.2 collective-permute-done.2.refs_0_
  37.5 1.9 %gram_part.1 = (bf16[1024,1024]{1,0:T(8,128)(2,1)S(1)}, bf16[16,16,1024]{2,1,0:T(8,128)(2,1)S(1)}, f32[4,1024]{1,0:T(4,128)S(1)}) custom-call(f32[8,1024]{1,0:T(8,128)S(1)} %get-tuple-element.17.pull, bf16[16,16,1024]{2,1,0:T(8,128)(2,1)S(1)} %all_to_all.20.own, bf16[16,16,1024]{2,1,0:T(8,128)(2,1)S(1)} %collective-permute-done.2.refs_0_, ...), custom_call_target="tpu_custom_call" | custom-call | tf_op jit(solution)/shard_map/gram_part/pallas_call | solution.py:274
  39.4 14.5 %all_to_all.21.pieces = bf16[16,16,1024]{2,1,0:T(8,128)(2,1)S(1)} all-to-all(bf16[16,16,1024]{2,1,0:T(8,128)(2,1)S(1)} %get-tuple-element.19), channel_id=1, replica_groups={{0,2,4,6,8,10,12,14,64,66,68,70,72,74,76,78},{16,18,20,22,24,26,28,30,8..., dimensions={0} | all-to-all | bytes 1048576 | tf_op jit(solution)/shard_map/all_to_all | solution.py:51
  54.0 0.9 %gram_sum.1 = bf16[16,16,1024]{2,1,0:T(8,128)(2,1)S(1)} custom-call(s32[1]{0:T(128)} %get-tuple-element.16.place, bf16[16,16,1024]{2,1,0:T(8,128)(2,1)S(1)} %all_to_all.21.pieces, f32[4,1024]{1,0:T(4,128)S(1)} %get-tuple-element.20.stats), custom_call_target="tpu_custom_call" | custom-call | tf_op jit(solution)/shard_map/gram_sum/pallas_call | solution.py:288
  54.9 14.1 %all_to_all.22.gram = bf16[16,16,1024]{2,1,0:T(8,128)(2,1)S(1)} all-to-all(bf16[16,16,1024]{2,1,0:T(8,128)(2,1)S(1)} %gram_sum.1), channel_id=1, replica_groups={{0,2,4,6,8,10,12,14,64,66,68,70,72,74,76,78},{16,18,20,22,24,26,28,30,8..., dimensions={0} | all-to-all | bytes 1048576 | tf_op jit(solution)/shard_map/all_to_all | solution.py:51
  69.0 1.8 %grad_rows.1 = (bf16[16,16,1024]{2,1,0:T(8,128)(2,1)}, f32[8,128]{1,0:T(8,128)S(1)}) custom-call(bf16[16,16,1024]{2,1,0:T(8,128)(2,1)S(1)} %all_to_all.22.gram, bf16[1024,1024]{1,0:T(8,128)(2,1)S(1)} %get-tuple-element.21.rounded, bf16[16,16,1024]{2,1,0:T(8,128)(2,1)S(1)} %all_to_all.20.own, f32[4,1024]{1,0:T(4,128)S(1)} %get-tuple-element.20.stats), custom_call_target="tpu_custom_call" | custom-call | tf_op jit(solution)/shard_map/grad_rows/pallas_call | solution.py:298
  70.9 3.7 %all-to-all-start.3 = ((bf16[16,16,1024]{2,1,0:T(8,128)(2,1)}), bf16[16,16,1024]{2,1,0:T(8,128)(2,1)S(1)}, u32[]{:S(2)}, u32[]{:S(2)}) async-start(bf16[16,16,1024]{2,1,0:T(8,128)(2,1)} %get-tuple-element.22), calls=%async_computation.3 | async-start | bytes 1048576 | tf_op jit(solution)/shard_map/all_to_all | solution.py:51
  74.6 1.5 %collective-permute-start.7 = (f32[8,128]{1,0:T(8,128)S(1)}, f32[8,128]{1,0:T(8,128)S(1)}, u32[]{:S(2)}, u32[]{:S(2)}) collective-permute-start(f32[8,128]{1,0:T(8,128)S(1)} %get-tuple-element.23), channel_id=1, source_target_pairs={{16,0},{18,2},{20,4},{22,6},{24,8},{26,10},{28,12},{30,14},{80,64}... | collective-permute-start | bytes 12296 | tf_op jit(solution)/shard_map/ppermute | solution.py:55
  76.0 0.6 collective-permute-start.6
  76.7 1.7 %collective-permute-start.5 = (f32[8,128]{1,0:T(8,128)S(1)}, f32[8,128]{1,0:T(8,128)S(1)}, u32[]{:S(2)}, u32[]{:S(2)}) collective-permute-start(f32[8,128]{1,0:T(8,128)S(1)} %get-tuple-element.23), channel_id=1, source_target_pairs={{32,0},{34,2},{36,4},{38,6},{40,8},{42,10},{44,12},{46,14},{96,64}... | collective-permute-start | bytes 12296 | tf_op jit(solution)/shard_map/ppermute | solution.py:55
  78.3 2.5 %collective-permute-done.6 = f32[8,128]{1,0:T(8,128)S(1)} collective-permute-done((f32[8,128]{1,0:T(8,128)S(1)}, f32[8,128]{1,0:T(8,128)S(1)}, u32[]{:S(2)}, u32[]{:S(2)}) %collective-permute-start.6) | collective-permute-done | bytes 4128 | tf_op jit(solution)/shard_map/ppermute | solution.py:55
  80.9 0.9 %collective-permute-done.5 = f32[8,128]{1,0:T(8,128)S(1)} collective-permute-done((f32[8,128]{1,0:T(8,128)S(1)}, f32[8,128]{1,0:T(8,128)S(1)}, u32[]{:S(2)}, u32[]{:S(2)}) %collective-permute-start.5) | collective-permute-done | bytes 4128 | tf_op jit(solution)/shard_map/ppermute | solution.py:55
  81.8 2.9 %all-to-all-done.3.recv = bf16[16,16,1024]{2,1,0:T(8,128)(2,1)S(1)} async-done(((bf16[16,16,1024]{2,1,0:T(8,128)(2,1)}), bf16[16,16,1024]{2,1,0:T(8,128)(2,1)S(1)}, u32[]{:S(2)}, u32[]{:S(2)}) %all-to-all-start.3) | async-done | bytes 524320 | tf_op jit(solution)/shard_map/all_to_all | solution.py:51
  84.8 0.5 collective-permute-start.9
  85.3 1.0 %collective-permute-done.9.other = f32[8,128]{1,0:T(8,128)S(1)} collective-permute-done((f32[8,128]{1,0:T(8,128)S(1)}, f32[8,128]{1,0:T(8,128)S(1)}, u32[]{:S(2)}, u32[]{:S(2)}) %collective-permute-start.9) | collective-permute-done | bytes 4128 | tf_op jit(solution)/shard_map/ppermute | solution.py:55
  86.3 1.1 %add_pull.1 = (f32[8,16384]{1,0:T(8,128)}, f32[8,16384]{1,0:T(8,128)}, f32[1]{0:T(128)}) custom-call(s32[1]{0:T(128)} %bitcast.core, bf16[16,16,1024]{2,1,0:T(8,128)(2,1)S(1)} %all-to-all-done.3.recv, bf16[16,8,1024]{2,1,0:T(8,128)(2,1)S(1)} %collective-permute-done.8.got, f32[8,128]{1,0:T(8,128)S(1)} %add_add_fusion.mine, ...), custom_call_target="tpu_custom_call" | custom-call | tf_op jit(solution)/shard_map/add_pull/pallas_call | solution.py:315
  (13 shorter events, 0.3 us)
Async XLA Ops:
  0.6 2.2 %collective-permute-start = (bf16[8,16384]{1,0:T(8,128)(2,1)}, bf16[8,16384]{1,0:T(8,128)(2,1)S(1)}, u32[]{:S(2)}, u32[]{:S(2)}) collective-permute-start(bf16[8,16384]{1,0:T(8,128)(2,1)} %view_one.3), channel_id=1, source_target_pairs={{0,1},{1,0},{2,3},{3,2},{4,5},{5,4},{6,7},{7,6},{8,9},{9,8},{10,11... | collective-permute-start | bytes 786440 | tf_op jit(solution)/shard_map/ppermute | solution.py:55
  0.7 2.1 %collective-permute-start.1 = (bf16[8,16384]{1,0:T(8,128)(2,1)}, bf16[8,16384]{1,0:T(8,128)(2,1)S(1)}, u32[]{:S(2)}, u32[]{:S(2)}) collective-permute-start(bf16[8,16384]{1,0:T(8,128)(2,1)} %view_two.3), channel_id=1, source_target_pairs={{0,1},{1,0},{2,3},{3,2},{4,5},{5,4},{6,7},{7,6},{8,9},{9,8},{10,11... | collective-permute-start | bytes 786440 | tf_op jit(solution)/shard_map/ppermute | solution.py:55
  21.2 10.8 %collective-permute-start.4 = (bf16[16,16,1024]{2,1,0:T(8,128)(2,1)S(1)}, bf16[16,16,1024]{2,1,0:T(8,128)(2,1)S(1)}, u32[]{:S(2)}, u32[]{:S(2)}) collective-permute-start(bf16[16,16,1024]{2,1,0:T(8,128)(2,1)S(1)} %all_to_all.20.own), channel_id=1, source_target_pairs={{32,0},{34,2},{36,4},{38,6},{40,8},{42,10},{44,12},{46,14},{96,64}... | collective-permute-start | bytes 1572872 | tf_op jit(solution)/shard_map/ppermute | solution.py:55
  24.0 13.4 %collective-permute-start.3 = (bf16[16,16,1024]{2,1,0:T(8,128)(2,1)S(1)}, bf16[16,16,1024]{2,1,0:T(8,128)(2,1)S(1)}, u32[]{:S(2)}, u32[]{:S(2)}) collective-permute-start(bf16[16,16,1024]{2,1,0:T(8,128)(2,1)S(1)} %all_to_all.20.own), channel_id=1, source_target_pairs={{16,0},{18,2},{20,4},{22,6},{24,8},{26,10},{28,12},{30,14},{80,64}... | collective-permute-start | bytes 1572872 | tf_op jit(solution)/shard_map/ppermute | solution.py:55
  25.1 12.4 %collective-permute-start.2 = (bf16[16,16,1024]{2,1,0:T(8,128)(2,1)S(1)}, bf16[16,16,1024]{2,1,0:T(8,128)(2,1)S(1)}, u32[]{:S(2)}, u32[]{:S(2)}) collective-permute-start(bf16[16,16,1024]{2,1,0:T(8,128)(2,1)S(1)} %all_to_all.20.own), channel_id=1, source_target_pairs={{48,0},{50,2},{52,4},{54,6},{56,8},{58,10},{60,12},{62,14},{112,64... | collective-permute-start | bytes 1572872 | tf_op jit(solution)/shard_map/ppermute | solution.py:55
  69.0 17.3 %copy-start = (bf16[8,16384]{1,0:T(8,128)(2,1)S(1)}, bf16[8,16384]{1,0:T(8,128)(2,1)}, u32[]{:S(2)}) copy-start(bf16[8,16384]{1,0:T(8,128)(2,1)} %view_one.3) | copy-start | bytes 786436
  69.0 17.3 %copy-start.1 = (bf16[8,16384]{1,0:T(8,128)(2,1)S(1)}, bf16[8,16384]{1,0:T(8,128)(2,1)}, u32[]{:S(2)}) copy-start(bf16[8,16384]{1,0:T(8,128)(2,1)} %view_two.3) | copy-start | bytes 786436
  70.9 13.8 %all-to-all-start.3 = ((bf16[16,16,1024]{2,1,0:T(8,128)(2,1)}), bf16[16,16,1024]{2,1,0:T(8,128)(2,1)S(1)}, u32[]{:S(2)}, u32[]{:S(2)}) async-start(bf16[16,16,1024]{2,1,0:T(8,128)(2,1)} %get-tuple-element.22), calls=%async_computation.3 | async-start | bytes 1048576 | tf_op jit(solution)/shard_map/all_to_all | solution.py:51
  74.6 3.8 %collective-permute-start.7 = (f32[8,128]{1,0:T(8,128)S(1)}, f32[8,128]{1,0:T(8,128)S(1)}, u32[]{:S(2)}, u32[]{:S(2)}) collective-permute-start(f32[8,128]{1,0:T(8,128)S(1)} %get-tuple-element.23), channel_id=1, source_target_pairs={{16,0},{18,2},{20,4},{22,6},{24,8},{26,10},{28,12},{30,14},{80,64}... | collective-permute-start | bytes 12296 | tf_op jit(solution)/shard_map/ppermute | solution.py:55
  76.0 4.8 %collective-permute-start.6 = (f32[8,128]{1,0:T(8,128)S(1)}, f32[8,128]{1,0:T(8,128)S(1)}, u32[]{:S(2)}, u32[]{:S(2)}) collective-permute-start(f32[8,128]{1,0:T(8,128)S(1)} %get-tuple-element.23), channel_id=1, source_target_pairs={{48,0},{50,2},{52,4},{54,6},{56,8},{58,10},{60,12},{62,14},{112,64... | collective-permute-start | bytes 12296 | tf_op jit(solution)/shard_map/ppermute | solution.py:55
  76.7 5.1 %collective-permute-start.5 = (f32[8,128]{1,0:T(8,128)S(1)}, f32[8,128]{1,0:T(8,128)S(1)}, u32[]{:S(2)}, u32[]{:S(2)}) collective-permute-start(f32[8,128]{1,0:T(8,128)S(1)} %get-tuple-element.23), channel_id=1, source_target_pairs={{32,0},{34,2},{36,4},{38,6},{40,8},{42,10},{44,12},{46,14},{96,64}... | collective-permute-start | bytes 12296 | tf_op jit(solution)/shard_map/ppermute | solution.py:55
  84.7 1.6 %collective-permute-start.8 = (bf16[16,8,1024]{2,1,0:T(8,128)(2,1)S(1)}, bf16[16,8,1024]{2,1,0:T(8,128)(2,1)S(1)}, u32[]{:S(2)}, u32[]{:S(2)}) collective-permute-start(bf16[16,8,1024]{2,1,0:T(8,128)(2,1)S(1)} %slice.4), channel_id=1, source_target_pairs={{0,1},{1,0},{2,3},{3,2},{4,5},{5,4},{6,7},{7,6},{8,9},{9,8},{10,11... | collective-permute-start | bytes 786440 | tf_op jit(solution)/shard_map/ppermute | solution.py:55
  84.8 1.5 %collective-permute-start.9 = (f32[8,128]{1,0:T(8,128)S(1)}, f32[8,128]{1,0:T(8,128)S(1)}, u32[]{:S(2)}, u32[]{:S(2)}) collective-permute-start(f32[8,128]{1,0:T(8,128)S(1)} %add_add_fusion.mine), channel_id=1, source_target_pairs={{0,1},{1,0},{2,3},{3,2},{4,5},{5,4},{6,7},{7,6},{8,9},{9,8},{10,11... | collective-permute-start | bytes 12296 | tf_op jit(solution)/shard_map/ppermute | solution.py:55

commit v9 on v8

--- a/solution.py
+++ b/solution.py
@@ -99,10 +99,9 @@
     return jnp.sum(block.reshape(-1, 8, block.shape[1]), axis=0)
 
 
-def gram_kernel(sizes, pull, own, *refs):
-    copies, (rounded, part, stats) = refs[:-3], refs[-3:]
+def center_kernel(sizes, pull, own, up, down, far, rounded, stats):
+    copies = (up, down, far)
     batch_rows, feature_count, row_parts = sizes
-    group_rows = batch_rows // row_parts
     width = own.shape[2]
     for start in range(0, width, CHUNK):
         cut = pl.ds(start, CHUNK)
@@ -129,9 +128,17 @@
         stats[1:2, cut] = energy
         stats[2:3, cut] = jnp.where(spread < 1.0, 1.0 / spread, 0.0)
         stats[3:4, cut] = share
-    product = lax.dot_general(
-        rounded[pl.ds(0, group_rows)], rounded[...], CONTRACT_LAST, preferred_element_type=jnp.float32
-    )
+
+
+def gram_kernel(sizes, pull, own, up, down, far, first, second, part, stats):
+    batch_rows, feature_count, row_parts = sizes
+    group_rows = batch_rows // row_parts
+    center_kernel(sizes, pull, own, up, down, far, second, stats)
+    product = 0.0
+    for half in (first, second):
+        product += lax.dot_general(
+            half[pl.ds(0, group_rows)], half[...], CONTRACT_LAST, preferred_element_type=jnp.float32
+        )
     part[...] = product.astype(jnp.bfloat16).reshape(part.shape)
 
 
@@ -151,7 +158,7 @@
     return jnp.where(row == 0, high, jnp.where(row == 1, middle, low))
 
 
-def sum_kernel(sizes, place, pieces, stats, sent):
+def sum_kernel(sizes, place, pieces, first_stats, second_stats, sent):
     batch_rows, feature_count, row_parts = sizes
     rows = pieces.shape[1]
     summed = jnp.sum(pieces[...].astype(jnp.float32), axis=0)
@@ -161,56 +168,69 @@
     diagonal = slots(shape, rows, first, 0)
     lost = jnp.sum(jnp.where(diagonal, summed - short, 0.0), axis=1, keepdims=True)
     factor = cov_weight / feature_count / (batch_rows - 1) ** 2
-    value = jnp.sum(factor * jnp.sum(summed * summed, axis=0, keepdims=True) + stats[3:4])
+    shares = jnp.concatenate([first_stats[3:4], second_stats[3:4]], axis=1)
+    value = jnp.sum(factor * jnp.sum(summed * summed, axis=0, keepdims=True) + shares)
     out = jnp.where(slots(shape, rows, first, rows - 1), lost, short)
     out = jnp.where(slots(shape, rows, first, rows - 2), three_parts(value, (rows, 1)), out)
     sent[...] = jnp.broadcast_to(out.astype(jnp.bfloat16)[None], sent.shape)
 
 
-def grad_kernel(sizes, gram, rounded, own, stats, sent, scalar):
+def grad_kernel(
+    sizes, gram, first, second, own, first_stats, second_stats, sent, scalar, left, ready, sems
+):
     batch_rows, feature_count, row_parts = sizes
     parts, rows, width = own.shape
     group_rows = parts * rows
     factor_cov = 4.0 * cov_weight * batch_rows / (batch_rows - 1) ** 2 / out_scale
     factor_var = var_weight * batch_rows / (batch_rows - 1) / out_scale
 
-    square = gram[:, :, pl.ds(0, group_rows)].reshape(group_rows, group_rows).astype(jnp.float32)
-    shape = square.shape
-    lane = lax.broadcasted_iota(jnp.int32, (1, group_rows), 1) % rows
-    restored = square
-    for shift in (1, 2):
-        mirror = jnp.sum(
-            jnp.where(slots(shape, rows, 0, shift), square, 0.0), axis=0, keepdims=True
-        )
-        ahead = pltpu.roll(mirror, group_rows - shift, 1)
-        around = pltpu.roll(mirror, rows - shift, 1)
-        mirror = jnp.where(lane < rows - shift, ahead, around)
-        here = slots(shape, rows, 0, rows - shift)
-        restored = jnp.where(here, mirror, restored)
-        taken = jnp.sum(jnp.where(here, square, 0.0), axis=1, keepdims=True)
-        if shift == 1:
-            lost = taken
-        else:
-            scalar[...] = jnp.full(scalar.shape, jnp.sum(taken), jnp.float32)
-    left = restored.astype(jnp.bfloat16)
+    left[...] = gram[:, :, pl.ds(0, group_rows)].reshape(left.shape)
+    shape = (LANES, LANES)
+    lane = lax.broadcasted_iota(jnp.int32, (1, LANES), 1) % rows
+    lost, shares = [], 0.0
+    for start in range(0, group_rows, LANES):
+        square = left[pl.ds(start, LANES), pl.ds(start, LANES)].astype(jnp.float32)
+        restored = square
+        for shift in (1, 2):
+            mirror = jnp.where(slots(shape, rows, 0, shift), square, 0.0)
+            mirror = jnp.sum(mirror, axis=0, keepdims=True)
+            ahead = pltpu.roll(mirror, LANES - shift, 1)
+            around = pltpu.roll(mirror, rows - shift, 1)
+            mirror = jnp.where(lane < rows - shift, ahead, around)
+            here = slots(shape, rows, 0, rows - shift)
+            restored = jnp.where(here, mirror, restored)
+            taken = jnp.where(here, square, 0.0)
+            if shift == 1:
+                lost.append(jnp.sum(taken, axis=1, keepdims=True))
+            else:
+                shares += jnp.sum(taken, axis=0, keepdims=True)
+        left[pl.ds(start, LANES), pl.ds(start, LANES)] = restored.astype(jnp.bfloat16)
+    lost = jnp.concatenate(lost, axis=0)
+    scalar[...] = jnp.full(scalar.shape, jnp.sum(shares), jnp.float32)
     right = gram[:, :, pl.ds(group_rows, batch_rows - group_rows)]
     right = right.reshape(group_rows, batch_rows - group_rows)
-    for start in range(0, width, CHUNK):
-        cut = pl.ds(start, CHUNK)
+    copies = []
+    half = width // 2
+    for i, (rounded, stats) in enumerate(((first, first_stats), (second, second_stats))):
+        cut = pl.ds(i * half, half)
         product = lax.dot_general(
-            left, rounded[pl.ds(0, group_rows), cut], CONTRACT_FIRST, preferred_element_type=jnp.float32
+            left[...], rounded[pl.ds(0, group_rows)], CONTRACT_FIRST, preferred_element_type=jnp.float32
         )
         product += lax.dot_general(
             right,
-            rounded[pl.ds(group_rows, batch_rows - group_rows), cut],
+            rounded[pl.ds(group_rows, batch_rows - group_rows)],
             CONTRACT_FIRST,
             preferred_element_type=jnp.float32,
         )
-        mine = rounded[pl.ds(0, group_rows), cut].astype(jnp.float32)
-        centered = own[:, :, cut].reshape(group_rows, CHUNK).astype(jnp.float32) - stats[0:1, cut]
-        product = product + (lost - stats[1:2, cut]) * mine
-        grad = factor_cov * product - factor_var * stats[2:3, cut] * centered
-        sent[:, :, cut] = grad.astype(jnp.bfloat16).reshape(parts, rows, CHUNK)
+        mine = rounded[pl.ds(0, group_rows)].astype(jnp.float32)
+        centered = own[:, :, cut].reshape(group_rows, half).astype(jnp.float32) - stats[0:1]
+        product = product + (lost - stats[1:2]) * mine
+        grad = factor_cov * product - factor_var * stats[2:3] * centered
+        ready[i] = grad.astype(jnp.bfloat16).reshape(parts, rows, half)
+        copies.append(pltpu.make_async_copy(ready.at[i], sent.at[:, :, cut], sems.at[i]))
+        copies[-1].start()
+    for copy in copies:
+        copy.wait()
 
 
 def final_kernel(core, recv, got, mine, other, view_one, view_two, grad_one, grad_two, loss):
@@ -269,43 +289,60 @@
         name="pack_rows",
     )(core, keep, got_one, got_two)
     own = exchange(blocks)
-    copies = (move(own, UP), move(own, DOWN), move(own, FAR))
-
-    rounded, part, stats = pl.pallas_call(
+    half = width // 2
+    halves = own[:, :, :half], own[:, :, half:]
+    copies = [[move(h, pairs) for pairs in (FAR, UP, DOWN)] for h in halves]
+    (far, up, down), (far_second, up_second, down_second) = copies
+    rounded_shape = jax.ShapeDtypeStruct((batch_rows, half), jnp.bfloat16)
+    stats_shape = jax.ShapeDtypeStruct((4, half), jnp.float32)
+    first, first_stats = pl.pallas_call(
+        functools.partial(center_kernel, sizes),
+        in_specs=[vmem] * 5,
+        out_specs=[vmem] * 2,
+        out_shape=[rounded_shape, stats_shape],
+        compiler_params=room(12),
+        name="center_first",
+    )(pull[:, :half], halves[0], up, down, far)
+    second, part, second_stats = pl.pallas_call(
         functools.partial(gram_kernel, sizes),
-        in_specs=[vmem] * (2 + len(copies)),
-        out_specs=[vmem, vmem, vmem],
+        in_specs=[vmem] * 6,
+        out_specs=[vmem] * 3,
         out_shape=[
-            jax.ShapeDtypeStruct((batch_rows, width), jnp.bfloat16),
+            rounded_shape,
             jax.ShapeDtypeStruct((feature_parts, rows, batch_rows), jnp.bfloat16),
-            jax.ShapeDtypeStruct((4, width), jnp.float32),
-        ],
-        compiler_params=room(24),
+            stats_shape,
+        ],
+        compiler_params=room(16),
         name="gram_part",
-    )(pull, own, *copies)
+    )(pull[:, half:], halves[1], up_second, down_second, far_second, first)
 
     pieces = exchange(part)
     sent = pl.pallas_call(
         functools.partial(sum_kernel, sizes),
-        in_specs=[smem, vmem, vmem],
+        in_specs=[smem, vmem, vmem, vmem],
         out_specs=vmem,
         out_shape=jax.ShapeDtypeStruct((feature_parts, rows, batch_rows), jnp.bfloat16),
         compiler_params=room(4),
         name="gram_sum",
-    )(place, pieces, stats)
+    )(place, pieces, first_stats, second_stats)
 
     gram = exchange(sent)
     grads, scalar = pl.pallas_call(
         functools.partial(grad_kernel, sizes),
-        in_specs=[vmem] * 4,
-        out_specs=[vmem] * 2,
+        in_specs=[vmem] * 6,
+        out_specs=[hbm, vmem],
         out_shape=[
             pltpu.HBM((feature_parts, rows, width), jnp.bfloat16),
             jax.ShapeDtypeStruct((8, LANES), jnp.float32),
         ],
+        scratch_shapes=[
+            pltpu.VMEM((group_rows, group_rows), jnp.bfloat16),
+            pltpu.VMEM((2, feature_parts, rows, half), jnp.bfloat16),
+            pltpu.SemaphoreType.DMA((2,)),
+        ],
         compiler_params=room(16),
         name="grad_rows",
-    )(gram, rounded, own, stats)
+    )(gram, first, second, own, first_stats, second_stats)
 
     grads = exchange(grads)
     far, before, after = [move(scalar, pairs) for pairs in (FAR, UP, DOWN)]

time: 88.9 us -> 88.4 us (level)
  starting transfers between devices: 13.4 us -> 17.5 us
  waiting for transfers between devices: 18.9 us -> 14.8 us
    ppermute x10 -> x13, starting transfers between devices: 9.67 us -> 13.9 us  [move(): return lax.ppermute(block, FINE, pairs)]
    ppermute x10 -> x13, waiting for transfers between devices: 16.1 us -> 11.9 us  [move(): return lax.ppermute(block, FINE, pairs)]
    pallas_call x2 -> x3, Pallas kernels: 3.72 us -> 3.56 us  [the longest x1 1.58 us: body(): pl.pallas_call(functools.partial(grad_kernel, sizes), in_specs=[vmem] * 6...]
  transfers between devices with their start and end apart: 11 -> 14, of which waited for: 7 -> 9; matrix products, arithmetic and copies ran while one was open for 0% -> 0% of each run, Pallas kernels for 2% -> 3%
where the time goes in v9:
time: 88.4 us; the launch traced here: 87 us
  blocking collectives  46.7 us (53%)
  starting transfers between devices  17.5 us (20%)
  waiting for transfers between devices  14.8 us (17%)
  Pallas kernels  7.23 us (8%)
    all_to_all x3, blocking collectives, exchange(): lax.all_to_all(blocks, FINE, 0, 0, tiled=True, axis_index_groups=GROUPS)  46.7 us
    ppermute x13, starting transfers between devices, move(): return lax.ppermute(block, FINE, pairs)  13.9 us
    ppermute x13, waiting for transfers between devices, move(): return lax.ppermute(block, FINE, pairs)  11.9 us
    all_to_all x1, starting transfers between devices, exchange(): lax.all_to_all(blocks, FINE, 0, 0, tiled=True, axis_index_groups=GROUPS)  3.59 us
    all_to_all x1, waiting for transfers between devices, exchange(): lax.all_to_all(blocks, FINE, 0, 0, tiled=True, axis_index_groups=GROUPS)  2.84 us
  transfers between devices with their start and end apart: 14, of which 9 were waited for; matrix products, arithmetic and copies ran while one was open for 0% of the time, Pallas kernels for 3%

profile of v9, /device:TPU:0, one launch (start us, length us, event | category | flops | bytes accessed | tf_op | source)
XLA Modules:
  0.0 87.0 jit_solution(3913348443354116446)
XLA Ops:
  1.2 1.6 %choose_view.1 = (bf16[8,16384]{1,0:T(8,128)(2,1)S(1)}, f32[8,1024]{1,0:T(8,128)S(1)}, s32[1]{0:T(128)}) custom-call(s32[1]{0:T(128)} %bitcast.core, s32[1]{0:T(128)} %bitcast.1.place_in, bf16[8,16384]{1,0:T(8,128)(2,1)} %view_one.3, bf16[8,16384]{1,0:T(8,128)(2,1)} %view_two.3), custom_call_target="tpu_custom_call" | custom-call | tf_op jit(solution)/shard_map/choose_view/pallas_call | solution.py:267
  2.9 18.3 %all_to_all.20.own = bf16[16,16,1024]{2,1,0:T(8,128)(2,1)S(1)} all-to-all(bf16[16,16,1024]{2,1,0:T(8,128)(2,1)S(1)} %pack_rows.1), channel_id=1, replica_groups={{0,2,4,6,8,10,12,14,64,66,68,70,72,74,76,78},{16,18,20,22,24,26,28,30,8..., dimensions={0} | all-to-all | bytes 1048576 | tf_op jit(solution)/shard_map/all_to_all | solution.py:51
  21.3 2.8 %collective-permute-start.7 = (bf16[16,16,512]{2,1,0:T(8,128)(2,1)S(1)}, bf16[16,16,512]{2,1,0:T(8,128)(2,1)S(1)}, u32[]{:S(2)}, u32[]{:S(2)}) collective-permute-start(bf16[16,16,512]{2,1,0:T(8,128)(2,1)S(1)} %get-tuple-element.33.own), channel_id=1, source_target_pairs={{32,0},{34,2},{36,4},{38,6},{40,8},{42,10},{44,12},{46,14},{96,64}... | collective-permute-start | bytes 786440 | tf_op jit(solution)/shard_map/ppermute | solution.py:55
  24.1 1.1 %collective-permute-start.6 = (bf16[16,16,512]{2,1,0:T(8,128)(2,1)S(1)}, bf16[16,16,512]{2,1,0:T(8,128)(2,1)S(1)}, u32[]{:S(2)}, u32[]{:S(2)}) collective-permute-start(bf16[16,16,512]{2,1,0:T(8,128)(2,1)S(1)} %get-tuple-element.33.own), channel_id=1, source_target_pairs={{16,0},{18,2},{20,4},{22,6},{24,8},{26,10},{28,12},{30,14},{80,64}... | collective-permute-start | bytes 786440 | tf_op jit(solution)/shard_map/ppermute | solution.py:55
  26.9 2.4 %collective-permute-start.3 = (bf16[16,16,512]{2,1,0:T(8,128)(2,1)S(1)}, bf16[16,16,512]{2,1,0:T(8,128)(2,1)S(1)}, u32[]{:S(2)}, u32[]{:S(2)}) collective-permute-start(bf16[16,16,512]{2,1,0:T(8,128)(2,1)S(1)} %get-tuple-element.34.own), channel_id=1, source_target_pairs={{16,0},{18,2},{20,4},{22,6},{24,8},{26,10},{28,12},{30,14},{80,64}... | collective-permute-start | bytes 786440 | tf_op jit(solution)/shard_map/ppermute | solution.py:55
  29.4 1.2 %collective-permute-start.2 = (bf16[16,16,512]{2,1,0:T(8,128)(2,1)S(1)}, bf16[16,16,512]{2,1,0:T(8,128)(2,1)S(1)}, u32[]{:S(2)}, u32[]{:S(2)}) collective-permute-start(bf16[16,16,512]{2,1,0:T(8,128)(2,1)S(1)} %get-tuple-element.34.own), channel_id=1, source_target_pairs={{48,0},{50,2},{52,4},{54,6},{56,8},{58,10},{60,12},{62,14},{112,64... | collective-permute-start | bytes 786440 | tf_op jit(solution)/shard_map/ppermute | solution.py:55
  30.5 1.3 %collective-permute-done.6.down = bf16[16,16,512]{2,1,0:T(8,128)(2,1)S(1)} collective-permute-done((bf16[16,16,512]{2,1,0:T(8,128)(2,1)S(1)}, bf16[16,16,512]{2,1,0:T(8,128)(2,1)S(1)}, u32[]{:S(2)}, u32[]{:S(2)}) %collective-permute-start.6) | collective-permute-done | bytes 262176 | tf_op jit(solution)/shard_map/ppermute | solution.py:55
  31.8 3.8 %collective-permute-done.5.up = bf16[16,16,512]{2,1,0:T(8,128)(2,1)S(1)} collective-permute-done((bf16[16,16,512]{2,1,0:T(8,128)(2,1)S(1)}, bf16[16,16,512]{2,1,0:T(8,128)(2,1)S(1)}, u32[]{:S(2)}, u32[]{:S(2)}) %collective-permute-start.5) | collective-permute-done | bytes 262176 | tf_op jit(solution)/shard_map/ppermute | solution.py:55
  36.3 1.2 %collective-permute-done.3.down = bf16[16,16,512]{2,1,0:T(8,128)(2,1)S(1)} collective-permute-done((bf16[16,16,512]{2,1,0:T(8,128)(2,1)S(1)}, bf16[16,16,512]{2,1,0:T(8,128)(2,1)S(1)}, u32[]{:S(2)}, u32[]{:S(2)}) %collective-permute-start.3) | collective-permute-done | bytes 262176 | tf_op jit(solution)/shard_map/ppermute | solution.py:55
  37.5 0.9 %collective-permute-done.2.up = bf16[16,16,512]{2,1,0:T(8,128)(2,1)S(1)} collective-permute-done((bf16[16,16,512]{2,1,0:T(8,128)(2,1)S(1)}, bf16[16,16,512]{2,1,0:T(8,128)(2,1)S(1)}, u32[]{:S(2)}, u32[]{:S(2)}) %collective-permute-start.2) | collective-permute-done | bytes 262176 | tf_op jit(solution)/shard_map/ppermute | solution.py:55
  38.4 1.3 %gram_part.1 = (bf16[1024,512]{1,0:T(8,128)(2,1)S(1)}, bf16[16,16,1024]{2,1,0:T(8,128)(2,1)S(1)}, f32[4,512]{1,0:T(4,128)S(1)}) custom-call(f32[8,512]{1,0:T(8,128)S(1)} %get-tuple-element.36.pull, bf16[16,16,512]{2,1,0:T(8,128)(2,1)S(1)} %get-tuple-element.34.own, bf16[16,16,512]{2,1,0:T(8,128)(2,1)S(1)} %collective-permute-done.2.up, ...), custom_call_target="tpu_custom_call" | custom-call | tf_op jit(solution)/shard_map/gram_part/pallas_call | solution.py:306
  39.7 14.5 %all_to_all.21.pieces = bf16[16,16,1024]{2,1,0:T(8,128)(2,1)S(1)} all-to-all(bf16[16,16,1024]{2,1,0:T(8,128)(2,1)S(1)} %get-tuple-element.22), channel_id=1, replica_groups={{0,2,4,6,8,10,12,14,64,66,68,70,72,74,76,78},{16,18,20,22,24,26,28,30,8..., dimensions={0} | all-to-all | bytes 1048576 | tf_op jit(solution)/shard_map/all_to_all | solution.py:51
  54.2 0.9 %gram_sum.1 = bf16[16,16,1024]{2,1,0:T(8,128)(2,1)S(1)} custom-call(s32[1]{0:T(128)} %get-tuple-element.18.place, bf16[16,16,1024]{2,1,0:T(8,128)(2,1)S(1)} %all_to_all.21.pieces, f32[4,512]{1,0:T(4,128)S(1)} %get-tuple-element.23.first_stats, f32[4,512]{1,0:T(4,128)S(1)} %get-tuple-element.24.second_stats), custom_call_target="tpu_custom_call" | custom-call | tf_op jit(solution)/shard_map/gram_sum/pallas_call | solution.py:320
  55.1 13.9 %all_to_all.22.gram = bf16[16,16,1024]{2,1,0:T(8,128)(2,1)S(1)} all-to-all(bf16[16,16,1024]{2,1,0:T(8,128)(2,1)S(1)} %gram_sum.1), channel_id=1, replica_groups={{0,2,4,6,8,10,12,14,64,66,68,70,72,74,76,78},{16,18,20,22,24,26,28,30,8..., dimensions={0} | all-to-all | bytes 1048576 | tf_op jit(solution)/shard_map/all_to_all | solution.py:51
  68.9 1.6 %grad_rows.1 = (bf16[16,16,1024]{2,1,0:T(8,128)(2,1)}, f32[8,128]{1,0:T(8,128)S(1)}) custom-call(bf16[16,16,1024]{2,1,0:T(8,128)(2,1)S(1)} %all_to_all.22.gram, bf16[1024,512]{1,0:T(8,128)(2,1)S(1)} %get-tuple-element.21.first, bf16[1024,512]{1,0:T(8,128)(2,1)S(1)} %get-tuple-element.25.second, bf16[16,16,1024]{2,1,0:T(8,128)(2,1)S(1)} %all_to_all.20.own, ...), custom_call_target="tpu_custom_call" | custom-call | tf_op jit(solution)/shard_map/grad_rows/pallas_call | solution.py:330
  70.5 3.6 %all-to-all-start.3 = ((bf16[16,16,1024]{2,1,0:T(8,128)(2,1)}), bf16[16,16,1024]{2,1,0:T(8,128)(2,1)S(1)}, u32[]{:S(2)}, u32[]{:S(2)}) async-start(bf16[16,16,1024]{2,1,0:T(8,128)(2,1)} %get-tuple-element.26), calls=%async_computation.3 | async-start | bytes 1048576 | tf_op jit(solution)/shard_map/all_to_all | solution.py:51
  74.1 1.2 %collective-permute-start.10 = (f32[8,128]{1,0:T(8,128)S(1)}, f32[8,128]{1,0:T(8,128)S(1)}, u32[]{:S(2)}, u32[]{:S(2)}) collective-permute-start(f32[8,128]{1,0:T(8,128)S(1)} %get-tuple-element.27), channel_id=1, source_target_pairs={{16,0},{18,2},{20,4},{22,6},{24,8},{26,10},{28,12},{30,14},{80,64}... | collective-permute-start | bytes 12296 | tf_op jit(solution)/shard_map/ppermute | solution.py:55
  75.3 0.9 %collective-permute-start.9 = (f32[8,128]{1,0:T(8,128)S(1)}, f32[8,128]{1,0:T(8,128)S(1)}, u32[]{:S(2)}, u32[]{:S(2)}) collective-permute-start(f32[8,128]{1,0:T(8,128)S(1)} %get-tuple-element.27), channel_id=1, source_target_pairs={{48,0},{50,2},{52,4},{54,6},{56,8},{58,10},{60,12},{62,14},{112,64... | collective-permute-start | bytes 12296 | tf_op jit(solution)/shard_map/ppermute | solution.py:55
  76.2 1.4 %collective-permute-start.8 = (f32[8,128]{1,0:T(8,128)S(1)}, f32[8,128]{1,0:T(8,128)S(1)}, u32[]{:S(2)}, u32[]{:S(2)}) collective-permute-start(f32[8,128]{1,0:T(8,128)S(1)} %get-tuple-element.27), channel_id=1, source_target_pairs={{32,0},{34,2},{36,4},{38,6},{40,8},{42,10},{44,12},{46,14},{96,64}... | collective-permute-start | bytes 12296 | tf_op jit(solution)/shard_map/ppermute | solution.py:55
  77.8 2.3 %collective-permute-done.9 = f32[8,128]{1,0:T(8,128)S(1)} collective-permute-done((f32[8,128]{1,0:T(8,128)S(1)}, f32[8,128]{1,0:T(8,128)S(1)}, u32[]{:S(2)}, u32[]{:S(2)}) %collective-permute-start.9) | collective-permute-done | bytes 4128 | tf_op jit(solution)/shard_map/ppermute | solution.py:55
  80.1 1.2 %collective-permute-done.8 = f32[8,128]{1,0:T(8,128)S(1)} collective-permute-done((f32[8,128]{1,0:T(8,128)S(1)}, f32[8,128]{1,0:T(8,128)S(1)}, u32[]{:S(2)}, u32[]{:S(2)}) %collective-permute-start.8) | collective-permute-done | bytes 4128 | tf_op jit(solution)/shard_map/ppermute | solution.py:55
  81.3 2.8 %all-to-all-done.3.recv = bf16[16,16,1024]{2,1,0:T(8,128)(2,1)S(1)} async-done(((bf16[16,16,1024]{2,1,0:T(8,128)(2,1)}), bf16[16,16,1024]{2,1,0:T(8,128)(2,1)S(1)}, u32[]{:S(2)}, u32[]{:S(2)}) %all-to-all-start.3) | async-done | bytes 524320 | tf_op jit(solution)/shard_map/all_to_all | solution.py:51
  84.8 1.0 %collective-permute-done.12.other = f32[8,128]{1,0:T(8,128)S(1)} collective-permute-done((f32[8,128]{1,0:T(8,128)S(1)}, f32[8,128]{1,0:T(8,128)S(1)}, u32[]{:S(2)}, u32[]{:S(2)}) %collective-permute-start.12) | collective-permute-done | bytes 4128 | tf_op jit(solution)/shard_map/ppermute | solution.py:55
  85.8 1.1 %add_pull.1 = (f32[8,16384]{1,0:T(8,128)}, f32[8,16384]{1,0:T(8,128)}, f32[1]{0:T(128)}) custom-call(s32[1]{0:T(128)} %bitcast.core, bf16[16,16,1024]{2,1,0:T(8,128)(2,1)S(1)} %all-to-all-done.3.recv, bf16[16,8,1024]{2,1,0:T(8,128)(2,1)S(1)} %collective-permute-done.11.got, f32[8,128]{1,0:T(8,128)S(1)} %add_add_fusion.mine, ...), custom_call_target="tpu_custom_call" | custom-call | tf_op jit(solution)/shard_map/add_pull/pallas_call | solution.py:352
  (22 shorter events, 3.9 us)
Async XLA Ops:
  0.6 2.2 %collective-permute-start = (bf16[8,16384]{1,0:T(8,128)(2,1)}, bf16[8,16384]{1,0:T(8,128)(2,1)S(1)}, u32[]{:S(2)}, u32[]{:S(2)}) collective-permute-start(bf16[8,16384]{1,0:T(8,128)(2,1)} %view_one.3), channel_id=1, source_target_pairs={{0,1},{1,0},{2,3},{3,2},{4,5},{5,4},{6,7},{7,6},{8,9},{9,8},{10,11... | collective-permute-start | bytes 786440 | tf_op jit(solution)/shard_map/ppermute | solution.py:55
  0.7 2.1 %collective-permute-start.1 = (bf16[8,16384]{1,0:T(8,128)(2,1)}, bf16[8,16384]{1,0:T(8,128)(2,1)S(1)}, u32[]{:S(2)}, u32[]{:S(2)}) collective-permute-start(bf16[8,16384]{1,0:T(8,128)(2,1)} %view_two.3), channel_id=1, source_target_pairs={{0,1},{1,0},{2,3},{3,2},{4,5},{5,4},{6,7},{7,6},{8,9},{9,8},{10,11... | collective-permute-start | bytes 786440 | tf_op jit(solution)/shard_map/ppermute | solution.py:55
  21.3 8.1 %collective-permute-start.7 = (bf16[16,16,512]{2,1,0:T(8,128)(2,1)S(1)}, bf16[16,16,512]{2,1,0:T(8,128)(2,1)S(1)}, u32[]{:S(2)}, u32[]{:S(2)}) collective-permute-start(bf16[16,16,512]{2,1,0:T(8,128)(2,1)S(1)} %get-tuple-element.33.own), channel_id=1, source_target_pairs={{32,0},{34,2},{36,4},{38,6},{40,8},{42,10},{44,12},{46,14},{96,64}... | collective-permute-start | bytes 786440 | tf_op jit(solution)/shard_map/ppermute | solution.py:55
  24.1 7.8 %collective-permute-start.6 = (bf16[16,16,512]{2,1,0:T(8,128)(2,1)S(1)}, bf16[16,16,512]{2,1,0:T(8,128)(2,1)S(1)}, u32[]{:S(2)}, u32[]{:S(2)}) collective-permute-start(bf16[16,16,512]{2,1,0:T(8,128)(2,1)S(1)} %get-tuple-element.33.own), channel_id=1, source_target_pairs={{16,0},{18,2},{20,4},{22,6},{24,8},{26,10},{28,12},{30,14},{80,64}... | collective-permute-start | bytes 786440 | tf_op jit(solution)/shard_map/ppermute | solution.py:55
  25.2 10.4 %collective-permute-start.5 = (bf16[16,16,512]{2,1,0:T(8,128)(2,1)S(1)}, bf16[16,16,512]{2,1,0:T(8,128)(2,1)S(1)}, u32[]{:S(2)}, u32[]{:S(2)}) collective-permute-start(bf16[16,16,512]{2,1,0:T(8,128)(2,1)S(1)} %get-tuple-element.33.own), channel_id=1, source_target_pairs={{48,0},{50,2},{52,4},{54,6},{56,8},{58,10},{60,12},{62,14},{112,64... | collective-permute-start | bytes 786440 | tf_op jit(solution)/shard_map/ppermute | solution.py:55
  26.1 10.2 %collective-permute-start.4 = (bf16[16,16,512]{2,1,0:T(8,128)(2,1)S(1)}, bf16[16,16,512]{2,1,0:T(8,128)(2,1)S(1)}, u32[]{:S(2)}, u32[]{:S(2)}) collective-permute-start(bf16[16,16,512]{2,1,0:T(8,128)(2,1)S(1)} %get-tuple-element.34.own), channel_id=1, source_target_pairs={{32,0},{34,2},{36,4},{38,6},{40,8},{42,10},{44,12},{46,14},{96,64}... | collective-permute-start | bytes 786440 | tf_op jit(solution)/shard_map/ppermute | solution.py:55
  26.9 10.6 %collective-permute-start.3 = (bf16[16,16,512]{2,1,0:T(8,128)(2,1)S(1)}, bf16[16,16,512]{2,1,0:T(8,128)(2,1)S(1)}, u32[]{:S(2)}, u32[]{:S(2)}) collective-permute-start(bf16[16,16,512]{2,1,0:T(8,128)(2,1)S(1)} %get-tuple-element.34.own), channel_id=1, source_target_pairs={{16,0},{18,2},{20,4},{22,6},{24,8},{26,10},{28,12},{30,14},{80,64}... | collective-permute-start | bytes 786440 | tf_op jit(solution)/shard_map/ppermute | solution.py:55
  29.4 9.0 %collective-permute-start.2 = (bf16[16,16,512]{2,1,0:T(8,128)(2,1)S(1)}, bf16[16,16,512]{2,1,0:T(8,128)(2,1)S(1)}, u32[]{:S(2)}, u32[]{:S(2)}) collective-permute-start(bf16[16,16,512]{2,1,0:T(8,128)(2,1)S(1)} %get-tuple-element.34.own), channel_id=1, source_target_pairs={{48,0},{50,2},{52,4},{54,6},{56,8},{58,10},{60,12},{62,14},{112,64... | collective-permute-start | bytes 786440 | tf_op jit(solution)/shard_map/ppermute | solution.py:55
  70.5 13.7 %all-to-all-start.3 = ((bf16[16,16,1024]{2,1,0:T(8,128)(2,1)}), bf16[16,16,1024]{2,1,0:T(8,128)(2,1)S(1)}, u32[]{:S(2)}, u32[]{:S(2)}) async-start(bf16[16,16,1024]{2,1,0:T(8,128)(2,1)} %get-tuple-element.26), calls=%async_computation.3 | async-start | bytes 1048576 | tf_op jit(solution)/shard_map/all_to_all | solution.py:51
  74.1 3.7 %collective-permute-start.10 = (f32[8,128]{1,0:T(8,128)S(1)}, f32[8,128]{1,0:T(8,128)S(1)}, u32[]{:S(2)}, u32[]{:S(2)}) collective-permute-start(f32[8,128]{1,0:T(8,128)S(1)} %get-tuple-element.27), channel_id=1, source_target_pairs={{16,0},{18,2},{20,4},{22,6},{24,8},{26,10},{28,12},{30,14},{80,64}... | collective-permute-start | bytes 12296 | tf_op jit(solution)/shard_map/ppermute | solution.py:55
  75.3 4.8 %collective-permute-start.9 = (f32[8,128]{1,0:T(8,128)S(1)}, f32[8,128]{1,0:T(8,128)S(1)}, u32[]{:S(2)}, u32[]{:S(2)}) collective-permute-start(f32[8,128]{1,0:T(8,128)S(1)} %get-tuple-element.27), channel_id=1, source_target_pairs={{48,0},{50,2},{52,4},{54,6},{56,8},{58,10},{60,12},{62,14},{112,64... | collective-permute-start | bytes 12296 | tf_op jit(solution)/shard_map/ppermute | solution.py:55
  76.2 5.1 %collective-permute-start.8 = (f32[8,128]{1,0:T(8,128)S(1)}, f32[8,128]{1,0:T(8,128)S(1)}, u32[]{:S(2)}, u32[]{:S(2)}) collective-permute-start(f32[8,128]{1,0:T(8,128)S(1)} %get-tuple-element.27), channel_id=1, source_target_pairs={{32,0},{34,2},{36,4},{38,6},{40,8},{42,10},{44,12},{46,14},{96,64}... | collective-permute-start | bytes 12296 | tf_op jit(solution)/shard_map/ppermute | solution.py:55
  81.3 4.5 %copy-start = (bf16[8,16384]{1,0:T(8,128)(2,1)S(1)}, bf16[8,16384]{1,0:T(8,128)(2,1)}, u32[]{:S(2)}) copy-start(bf16[8,16384]{1,0:T(8,128)(2,1)} %view_one.3) | copy-start | bytes 786436
  81.3 4.5 %copy-start.1 = (bf16[8,16384]{1,0:T(8,128)(2,1)S(1)}, bf16[8,16384]{1,0:T(8,128)(2,1)}, u32[]{:S(2)}) copy-start(bf16[8,16384]{1,0:T(8,128)(2,1)} %view_two.3) | copy-start | bytes 786436
  84.2 1.6 %collective-permute-start.11 = (bf16[16,8,1024]{2,1,0:T(8,128)(2,1)S(1)}, bf16[16,8,1024]{2,1,0:T(8,128)(2,1)S(1)}, u32[]{:S(2)}, u32[]{:S(2)}) collective-permute-start(bf16[16,8,1024]{2,1,0:T(8,128)(2,1)S(1)} %slice.22), channel_id=1, source_target_pairs={{0,1},{1,0},{2,3},{3,2},{4,5},{5,4},{6,7},{7,6},{8,9},{9,8},{10,11... | collective-permute-start | bytes 786440 | tf_op jit(solution)/shard_map/ppermute | solution.py:55
  84.3 1.5 %collective-permute-start.12 = (f32[8,128]{1,0:T(8,128)S(1)}, f32[8,128]{1,0:T(8,128)S(1)}, u32[]{:S(2)}, u32[]{:S(2)}) collective-permute-start(f32[8,128]{1,0:T(8,128)S(1)} %add_add_fusion.mine), channel_id=1, source_target_pairs={{0,1},{1,0},{2,3},{3,2},{4,5},{5,4},{6,7},{7,6},{8,9},{9,8},{10,11... | collective-permute-start | bytes 12296 | tf_op jit(solution)/shard_map/ppermute | solution.py:55

commit v10 on v9

--- a/solution.py
+++ b/solution.py
@@ -63,24 +63,14 @@
     return jnp.where(core == 0, first, second)
 
 
-def choose_kernel(
-    factor, core, place_in, view_one, view_two, keep, squares, place, here, sems
-):
+def choose_kernel(factor, core, place_in, view_one, view_two, keep, squares, place):
     place[0] = place_in[0]
-    copies = [
-        pltpu.make_async_copy(view, here.at[v], sems.at[v])
-        for v, view in enumerate((view_one, view_two))
-    ]
-    for copy in copies:
-        copy.start()
-    for copy in copies:
-        copy.wait()
     width = squares.shape[1]
     total = 0.0
     for start in range(0, keep.shape[1], width):
         cut = pl.ds(start, width)
-        first = here[0, :, cut].astype(jnp.float32)
-        second = here[1, :, cut].astype(jnp.float32)
+        first = view_one[:, cut].astype(jnp.float32)
+        second = view_two[:, cut].astype(jnp.float32)
         keep[:, cut] = pick(core[0], first, second).astype(jnp.bfloat16)
         total += (first - second) ** 2
     squares[...] = factor * total
@@ -266,12 +256,8 @@
     got_one, got_two = move(view_one, SWAP), move(view_two, SWAP)
     keep, pull, place = pl.pallas_call(
         functools.partial(choose_kernel, inv_weight / (batch_rows * feature_count)),
-        in_specs=[smem, smem, hbm, hbm],
+        in_specs=[smem, smem, vmem, vmem],
         out_specs=[vmem, vmem, smem],
-        scratch_shapes=[
-            pltpu.VMEM((2,) + view_one.shape, jnp.bfloat16),
-            pltpu.SemaphoreType.DMA((2,)),
-        ],
         out_shape=[
             jax.ShapeDtypeStruct(view_one.shape, jnp.bfloat16),
             jax.ShapeDtypeStruct((shard_rows, width), jnp.float32),

time: 88.4 us -> 88.4 us (level)
  no operation moved by 1% of the time
where the time goes in v10:
time: 88.4 us; the launch traced here: 87 us
  blocking collectives  46.7 us (53%)
  starting transfers between devices  17.5 us (20%)
  waiting for transfers between devices  14.8 us (17%)
  Pallas kernels  7.22 us (8%)
    all_to_all x3, blocking collectives, exchange(): lax.all_to_all(blocks, FINE, 0, 0, tiled=True, axis_index_groups=GROUPS)  46.7 us
    ppermute x13, starting transfers between devices, move(): return lax.ppermute(block, FINE, pairs)  13.9 us
    ppermute x13, waiting for transfers between devices, move(): return lax.ppermute(block, FINE, pairs)  11.9 us
    all_to_all x1, starting transfers between devices, exchange(): lax.all_to_all(blocks, FINE, 0, 0, tiled=True, axis_index_groups=GROUPS)  3.59 us
    all_to_all x1, waiting for transfers between devices, exchange(): lax.all_to_all(blocks, FINE, 0, 0, tiled=True, axis_index_groups=GROUPS)  2.84 us
  transfers between devices with their start and end apart: 14, of which 9 were waited for; matrix products, arithmetic and copies ran while one was open for 0% of the time, Pallas kernels for 3%

profile of v10, /device:TPU:0, one launch (start us, length us, event | category | flops | bytes accessed | tf_op | source)
XLA Modules:
  0.0 87.0 jit_solution(1906477797200524202)
XLA Ops:
  1.2 1.5 %choose_view.1 = (bf16[8,16384]{1,0:T(8,128)(2,1)S(1)}, f32[8,1024]{1,0:T(8,128)S(1)}, s32[1]{0:T(128)}) custom-call(s32[1]{0:T(128)} %bitcast.core, s32[1]{0:T(128)} %bitcast.1.place_in, bf16[8,16384]{1,0:T(8,128)(2,1)} %view_one.3, bf16[8,16384]{1,0:T(8,128)(2,1)} %view_two.3), custom_call_target="tpu_custom_call" | custom-call | tf_op jit(solution)/shard_map/choose_view/pallas_call | solution.py:257
  2.9 18.3 %all_to_all.20.own = bf16[16,16,1024]{2,1,0:T(8,128)(2,1)S(1)} all-to-all(bf16[16,16,1024]{2,1,0:T(8,128)(2,1)S(1)} %pack_rows.1), channel_id=1, replica_groups={{0,2,4,6,8,10,12,14,64,66,68,70,72,74,76,78},{16,18,20,22,24,26,28,30,8..., dimensions={0} | all-to-all | bytes 1048576 | tf_op jit(solution)/shard_map/all_to_all | solution.py:51
  21.3 2.8 %collective-permute-start.7 = (bf16[16,16,512]{2,1,0:T(8,128)(2,1)S(1)}, bf16[16,16,512]{2,1,0:T(8,128)(2,1)S(1)}, u32[]{:S(2)}, u32[]{:S(2)}) collective-permute-start(bf16[16,16,512]{2,1,0:T(8,128)(2,1)S(1)} %get-tuple-element.33.own), channel_id=1, source_target_pairs={{32,0},{34,2},{36,4},{38,6},{40,8},{42,10},{44,12},{46,14},{96,64}... | collective-permute-start | bytes 786440 | tf_op jit(solution)/shard_map/ppermute | solution.py:55
  24.1 1.1 %collective-permute-start.6 = (bf16[16,16,512]{2,1,0:T(8,128)(2,1)S(1)}, bf16[16,16,512]{2,1,0:T(8,128)(2,1)S(1)}, u32[]{:S(2)}, u32[]{:S(2)}) collective-permute-start(bf16[16,16,512]{2,1,0:T(8,128)(2,1)S(1)} %get-tuple-element.33.own), channel_id=1, source_target_pairs={{16,0},{18,2},{20,4},{22,6},{24,8},{26,10},{28,12},{30,14},{80,64}... | collective-permute-start | bytes 786440 | tf_op jit(solution)/shard_map/ppermute | solution.py:55
  26.9 2.4 %collective-permute-start.3 = (bf16[16,16,512]{2,1,0:T(8,128)(2,1)S(1)}, bf16[16,16,512]{2,1,0:T(8,128)(2,1)S(1)}, u32[]{:S(2)}, u32[]{:S(2)}) collective-permute-start(bf16[16,16,512]{2,1,0:T(8,128)(2,1)S(1)} %get-tuple-element.34.own), channel_id=1, source_target_pairs={{16,0},{18,2},{20,4},{22,6},{24,8},{26,10},{28,12},{30,14},{80,64}... | collective-permute-start | bytes 786440 | tf_op jit(solution)/shard_map/ppermute | solution.py:55
  29.4 1.2 %collective-permute-start.2 = (bf16[16,16,512]{2,1,0:T(8,128)(2,1)S(1)}, bf16[16,16,512]{2,1,0:T(8,128)(2,1)S(1)}, u32[]{:S(2)}, u32[]{:S(2)}) collective-permute-start(bf16[16,16,512]{2,1,0:T(8,128)(2,1)S(1)} %get-tuple-element.34.own), channel_id=1, source_target_pairs={{48,0},{50,2},{52,4},{54,6},{56,8},{58,10},{60,12},{62,14},{112,64... | collective-permute-start | bytes 786440 | tf_op jit(solution)/shard_map/ppermute | solution.py:55
  30.5 1.3 %collective-permute-done.6.down = bf16[16,16,512]{2,1,0:T(8,128)(2,1)S(1)} collective-permute-done((bf16[16,16,512]{2,1,0:T(8,128)(2,1)S(1)}, bf16[16,16,512]{2,1,0:T(8,128)(2,1)S(1)}, u32[]{:S(2)}, u32[]{:S(2)}) %collective-permute-start.6) | collective-permute-done | bytes 262176 | tf_op jit(solution)/shard_map/ppermute | solution.py:55
  31.8 3.8 %collective-permute-done.5.up = bf16[16,16,512]{2,1,0:T(8,128)(2,1)S(1)} collective-permute-done((bf16[16,16,512]{2,1,0:T(8,128)(2,1)S(1)}, bf16[16,16,512]{2,1,0:T(8,128)(2,1)S(1)}, u32[]{:S(2)}, u32[]{:S(2)}) %collective-permute-start.5) | collective-permute-done | bytes 262176 | tf_op jit(solution)/shard_map/ppermute | solution.py:55
  36.3 1.2 %collective-permute-done.3.down = bf16[16,16,512]{2,1,0:T(8,128)(2,1)S(1)} collective-permute-done((bf16[16,16,512]{2,1,0:T(8,128)(2,1)S(1)}, bf16[16,16,512]{2,1,0:T(8,128)(2,1)S(1)}, u32[]{:S(2)}, u32[]{:S(2)}) %collective-permute-start.3) | collective-permute-done | bytes 262176 | tf_op jit(solution)/shard_map/ppermute | solution.py:55
  37.5 0.9 %collective-permute-done.2.up = bf16[16,16,512]{2,1,0:T(8,128)(2,1)S(1)} collective-permute-done((bf16[16,16,512]{2,1,0:T(8,128)(2,1)S(1)}, bf16[16,16,512]{2,1,0:T(8,128)(2,1)S(1)}, u32[]{:S(2)}, u32[]{:S(2)}) %collective-permute-start.2) | collective-permute-done | bytes 262176 | tf_op jit(solution)/shard_map/ppermute | solution.py:55
  38.4 1.3 %gram_part.1 = (bf16[1024,512]{1,0:T(8,128)(2,1)S(1)}, bf16[16,16,1024]{2,1,0:T(8,128)(2,1)S(1)}, f32[4,512]{1,0:T(4,128)S(1)}) custom-call(f32[8,512]{1,0:T(8,128)S(1)} %get-tuple-element.36.pull, bf16[16,16,512]{2,1,0:T(8,128)(2,1)S(1)} %get-tuple-element.34.own, bf16[16,16,512]{2,1,0:T(8,128)(2,1)S(1)} %collective-permute-done.2.up, ...), custom_call_target="tpu_custom_call" | custom-call | tf_op jit(solution)/shard_map/gram_part/pallas_call | solution.py:292
  39.7 14.5 %all_to_all.21.pieces = bf16[16,16,1024]{2,1,0:T(8,128)(2,1)S(1)} all-to-all(bf16[16,16,1024]{2,1,0:T(8,128)(2,1)S(1)} %get-tuple-element.22), channel_id=1, replica_groups={{0,2,4,6,8,10,12,14,64,66,68,70,72,74,76,78},{16,18,20,22,24,26,28,30,8..., dimensions={0} | all-to-all | bytes 1048576 | tf_op jit(solution)/shard_map/all_to_all | solution.py:51
  54.2 0.9 %gram_sum.1 = bf16[16,16,1024]{2,1,0:T(8,128)(2,1)S(1)} custom-call(s32[1]{0:T(128)} %get-tuple-element.18.place, bf16[16,16,1024]{2,1,0:T(8,128)(2,1)S(1)} %all_to_all.21.pieces, f32[4,512]{1,0:T(4,128)S(1)} %get-tuple-element.23.first_stats, f32[4,512]{1,0:T(4,128)S(1)} %get-tuple-element.24.second_stats), custom_call_target="tpu_custom_call" | custom-call | tf_op jit(solution)/shard_map/gram_sum/pallas_call | solution.py:306
  55.1 13.9 %all_to_all.22.gram = bf16[16,16,1024]{2,1,0:T(8,128)(2,1)S(1)} all-to-all(bf16[16,16,1024]{2,1,0:T(8,128)(2,1)S(1)} %gram_sum.1), channel_id=1, replica_groups={{0,2,4,6,8,10,12,14,64,66,68,70,72,74,76,78},{16,18,20,22,24,26,28,30,8..., dimensions={0} | all-to-all | bytes 1048576 | tf_op jit(solution)/shard_map/all_to_all | solution.py:51
  68.9 1.6 %grad_rows.1 = (bf16[16,16,1024]{2,1,0:T(8,128)(2,1)}, f32[8,128]{1,0:T(8,128)S(1)}) custom-call(bf16[16,16,1024]{2,1,0:T(8,128)(2,1)S(1)} %all_to_all.22.gram, bf16[1024,512]{1,0:T(8,128)(2,1)S(1)} %get-tuple-element.21.first, bf16[1024,512]{1,0:T(8,128)(2,1)S(1)} %get-tuple-element.25.second, bf16[16,16,1024]{2,1,0:T(8,128)(2,1)S(1)} %all_to_all.20.own, ...), custom_call_target="tpu_custom_call" | custom-call | tf_op jit(solution)/shard_map/grad_rows/pallas_call | solution.py:316
  70.5 3.6 %all-to-all-start.3 = ((bf16[16,16,1024]{2,1,0:T(8,128)(2,1)}), bf16[16,16,1024]{2,1,0:T(8,128)(2,1)S(1)}, u32[]{:S(2)}, u32[]{:S(2)}) async-start(bf16[16,16,1024]{2,1,0:T(8,128)(2,1)} %get-tuple-element.26), calls=%async_computation.3 | async-start | bytes 1048576 | tf_op jit(solution)/shard_map/all_to_all | solution.py:51
  74.1 1.2 %collective-permute-start.10 = (f32[8,128]{1,0:T(8,128)S(1)}, f32[8,128]{1,0:T(8,128)S(1)}, u32[]{:S(2)}, u32[]{:S(2)}) collective-permute-start(f32[8,128]{1,0:T(8,128)S(1)} %get-tuple-element.27), channel_id=1, source_target_pairs={{16,0},{18,2},{20,4},{22,6},{24,8},{26,10},{28,12},{30,14},{80,64}... | collective-permute-start | bytes 12296 | tf_op jit(solution)/shard_map/ppermute | solution.py:55
  75.3 0.9 %collective-permute-start.9 = (f32[8,128]{1,0:T(8,128)S(1)}, f32[8,128]{1,0:T(8,128)S(1)}, u32[]{:S(2)}, u32[]{:S(2)}) collective-permute-start(f32[8,128]{1,0:T(8,128)S(1)} %get-tuple-element.27), channel_id=1, source_target_pairs={{48,0},{50,2},{52,4},{54,6},{56,8},{58,10},{60,12},{62,14},{112,64... | collective-permute-start | bytes 12296 | tf_op jit(solution)/shard_map/ppermute | solution.py:55
  76.2 1.4 %collective-permute-start.8 = (f32[8,128]{1,0:T(8,128)S(1)}, f32[8,128]{1,0:T(8,128)S(1)}, u32[]{:S(2)}, u32[]{:S(2)}) collective-permute-start(f32[8,128]{1,0:T(8,128)S(1)} %get-tuple-element.27), channel_id=1, source_target_pairs={{32,0},{34,2},{36,4},{38,6},{40,8},{42,10},{44,12},{46,14},{96,64}... | collective-permute-start | bytes 12296 | tf_op jit(solution)/shard_map/ppermute | solution.py:55
  77.8 2.3 %collective-permute-done.9 = f32[8,128]{1,0:T(8,128)S(1)} collective-permute-done((f32[8,128]{1,0:T(8,128)S(1)}, f32[8,128]{1,0:T(8,128)S(1)}, u32[]{:S(2)}, u32[]{:S(2)}) %collective-permute-start.9) | collective-permute-done | bytes 4128 | tf_op jit(solution)/shard_map/ppermute | solution.py:55
  80.1 1.2 %collective-permute-done.8 = f32[8,128]{1,0:T(8,128)S(1)} collective-permute-done((f32[8,128]{1,0:T(8,128)S(1)}, f32[8,128]{1,0:T(8,128)S(1)}, u32[]{:S(2)}, u32[]{:S(2)}) %collective-permute-start.8) | collective-permute-done | bytes 4128 | tf_op jit(solution)/shard_map/ppermute | solution.py:55
  81.3 2.8 %all-to-all-done.3.recv = bf16[16,16,1024]{2,1,0:T(8,128)(2,1)S(1)} async-done(((bf16[16,16,1024]{2,1,0:T(8,128)(2,1)}), bf16[16,16,1024]{2,1,0:T(8,128)(2,1)S(1)}, u32[]{:S(2)}, u32[]{:S(2)}) %all-to-all-start.3) | async-done | bytes 524320 | tf_op jit(solution)/shard_map/all_to_all | solution.py:51
  84.8 1.0 %collective-permute-done.12.other = f32[8,128]{1,0:T(8,128)S(1)} collective-permute-done((f32[8,128]{1,0:T(8,128)S(1)}, f32[8,128]{1,0:T(8,128)S(1)}, u32[]{:S(2)}, u32[]{:S(2)}) %collective-permute-start.12) | collective-permute-done | bytes 4128 | tf_op jit(solution)/shard_map/ppermute | solution.py:55
  85.8 1.1 %add_pull.1 = (f32[8,16384]{1,0:T(8,128)}, f32[8,16384]{1,0:T(8,128)}, f32[1]{0:T(128)}) custom-call(s32[1]{0:T(128)} %bitcast.core, bf16[16,16,1024]{2,1,0:T(8,128)(2,1)S(1)} %all-to-all-done.3.recv, bf16[16,8,1024]{2,1,0:T(8,128)(2,1)S(1)} %collective-permute-done.11.got, f32[8,128]{1,0:T(8,128)S(1)} %add_add_fusion.mine, ...), custom_call_target="tpu_custom_call" | custom-call | tf_op jit(solution)/shard_map/add_pull/pallas_call | solution.py:338
  (22 shorter events, 3.9 us)
Async XLA Ops:
  0.6 2.1 %collective-permute-start = (bf16[8,16384]{1,0:T(8,128)(2,1)}, bf16[8,16384]{1,0:T(8,128)(2,1)S(1)}, u32[]{:S(2)}, u32[]{:S(2)}) collective-permute-start(bf16[8,16384]{1,0:T(8,128)(2,1)} %view_one.3), channel_id=1, source_target_pairs={{0,1},{1,0},{2,3},{3,2},{4,5},{5,4},{6,7},{7,6},{8,9},{9,8},{10,11... | collective-permute-start | bytes 786440 | tf_op jit(solution)/shard_map/ppermute | solution.py:55
  0.7 2.1 %collective-permute-start.1 = (bf16[8,16384]{1,0:T(8,128)(2,1)}, bf16[8,16384]{1,0:T(8,128)(2,1)S(1)}, u32[]{:S(2)}, u32[]{:S(2)}) collective-permute-start(bf16[8,16384]{1,0:T(8,128)(2,1)} %view_two.3), channel_id=1, source_target_pairs={{0,1},{1,0},{2,3},{3,2},{4,5},{5,4},{6,7},{7,6},{8,9},{9,8},{10,11... | collective-permute-start | bytes 786440 | tf_op jit(solution)/shard_map/ppermute | solution.py:55
  21.3 8.1 %collective-permute-start.7 = (bf16[16,16,512]{2,1,0:T(8,128)(2,1)S(1)}, bf16[16,16,512]{2,1,0:T(8,128)(2,1)S(1)}, u32[]{:S(2)}, u32[]{:S(2)}) collective-permute-start(bf16[16,16,512]{2,1,0:T(8,128)(2,1)S(1)} %get-tuple-element.33.own), channel_id=1, source_target_pairs={{32,0},{34,2},{36,4},{38,6},{40,8},{42,10},{44,12},{46,14},{96,64}... | collective-permute-start | bytes 786440 | tf_op jit(solution)/shard_map/ppermute | solution.py:55
  24.1 7.8 %collective-permute-start.6 = (bf16[16,16,512]{2,1,0:T(8,128)(2,1)S(1)}, bf16[16,16,512]{2,1,0:T(8,128)(2,1)S(1)}, u32[]{:S(2)}, u32[]{:S(2)}) collective-permute-start(bf16[16,16,512]{2,1,0:T(8,128)(2,1)S(1)} %get-tuple-element.33.own), channel_id=1, source_target_pairs={{16,0},{18,2},{20,4},{22,6},{24,8},{26,10},{28,12},{30,14},{80,64}... | collective-permute-start | bytes 786440 | tf_op jit(solution)/shard_map/ppermute | solution.py:55
  25.2 10.4 %collective-permute-start.5 = (bf16[16,16,512]{2,1,0:T(8,128)(2,1)S(1)}, bf16[16,16,512]{2,1,0:T(8,128)(2,1)S(1)}, u32[]{:S(2)}, u32[]{:S(2)}) collective-permute-start(bf16[16,16,512]{2,1,0:T(8,128)(2,1)S(1)} %get-tuple-element.33.own), channel_id=1, source_target_pairs={{48,0},{50,2},{52,4},{54,6},{56,8},{58,10},{60,12},{62,14},{112,64... | collective-permute-start | bytes 786440 | tf_op jit(solution)/shard_map/ppermute | solution.py:55
  26.1 10.2 %collective-permute-start.4 = (bf16[16,16,512]{2,1,0:T(8,128)(2,1)S(1)}, bf16[16,16,512]{2,1,0:T(8,128)(2,1)S(1)}, u32[]{:S(2)}, u32[]{:S(2)}) collective-permute-start(bf16[16,16,512]{2,1,0:T(8,128)(2,1)S(1)} %get-tuple-element.34.own), channel_id=1, source_target_pairs={{32,0},{34,2},{36,4},{38,6},{40,8},{42,10},{44,12},{46,14},{96,64}... | collective-permute-start | bytes 786440 | tf_op jit(solution)/shard_map/ppermute | solution.py:55
  26.9 10.6 %collective-permute-start.3 = (bf16[16,16,512]{2,1,0:T(8,128)(2,1)S(1)}, bf16[16,16,512]{2,1,0:T(8,128)(2,1)S(1)}, u32[]{:S(2)}, u32[]{:S(2)}) collective-permute-start(bf16[16,16,512]{2,1,0:T(8,128)(2,1)S(1)} %get-tuple-element.34.own), channel_id=1, source_target_pairs={{16,0},{18,2},{20,4},{22,6},{24,8},{26,10},{28,12},{30,14},{80,64}... | collective-permute-start | bytes 786440 | tf_op jit(solution)/shard_map/ppermute | solution.py:55
  29.4 9.0 %collective-permute-start.2 = (bf16[16,16,512]{2,1,0:T(8,128)(2,1)S(1)}, bf16[16,16,512]{2,1,0:T(8,128)(2,1)S(1)}, u32[]{:S(2)}, u32[]{:S(2)}) collective-permute-start(bf16[16,16,512]{2,1,0:T(8,128)(2,1)S(1)} %get-tuple-element.34.own), channel_id=1, source_target_pairs={{48,0},{50,2},{52,4},{54,6},{56,8},{58,10},{60,12},{62,14},{112,64... | collective-permute-start | bytes 786440 | tf_op jit(solution)/shard_map/ppermute | solution.py:55
  70.5 13.7 %all-to-all-start.3 = ((bf16[16,16,1024]{2,1,0:T(8,128)(2,1)}), bf16[16,16,1024]{2,1,0:T(8,128)(2,1)S(1)}, u32[]{:S(2)}, u32[]{:S(2)}) async-start(bf16[16,16,1024]{2,1,0:T(8,128)(2,1)} %get-tuple-element.26), calls=%async_computation.3 | async-start | bytes 1048576 | tf_op jit(solution)/shard_map/all_to_all | solution.py:51
  74.1 3.7 %collective-permute-start.10 = (f32[8,128]{1,0:T(8,128)S(1)}, f32[8,128]{1,0:T(8,128)S(1)}, u32[]{:S(2)}, u32[]{:S(2)}) collective-permute-start(f32[8,128]{1,0:T(8,128)S(1)} %get-tuple-element.27), channel_id=1, source_target_pairs={{16,0},{18,2},{20,4},{22,6},{24,8},{26,10},{28,12},{30,14},{80,64}... | collective-permute-start | bytes 12296 | tf_op jit(solution)/shard_map/ppermute | solution.py:55
  75.3 4.8 %collective-permute-start.9 = (f32[8,128]{1,0:T(8,128)S(1)}, f32[8,128]{1,0:T(8,128)S(1)}, u32[]{:S(2)}, u32[]{:S(2)}) collective-permute-start(f32[8,128]{1,0:T(8,128)S(1)} %get-tuple-element.27), channel_id=1, source_target_pairs={{48,0},{50,2},{52,4},{54,6},{56,8},{58,10},{60,12},{62,14},{112,64... | collective-permute-start | bytes 12296 | tf_op jit(solution)/shard_map/ppermute | solution.py:55
  76.2 5.1 %collective-permute-start.8 = (f32[8,128]{1,0:T(8,128)S(1)}, f32[8,128]{1,0:T(8,128)S(1)}, u32[]{:S(2)}, u32[]{:S(2)}) collective-permute-start(f32[8,128]{1,0:T(8,128)S(1)} %get-tuple-element.27), channel_id=1, source_target_pairs={{32,0},{34,2},{36,4},{38,6},{40,8},{42,10},{44,12},{46,14},{96,64}... | collective-permute-start | bytes 12296 | tf_op jit(solution)/shard_map/ppermute | solution.py:55
  81.3 4.5 %copy-start = (bf16[8,16384]{1,0:T(8,128)(2,1)S(1)}, bf16[8,16384]{1,0:T(8,128)(2,1)}, u32[]{:S(2)}) copy-start(bf16[8,16384]{1,0:T(8,128)(2,1)} %view_one.3) | copy-start | bytes 786436
  81.3 4.5 %copy-start.1 = (bf16[8,16384]{1,0:T(8,128)(2,1)S(1)}, bf16[8,16384]{1,0:T(8,128)(2,1)}, u32[]{:S(2)}) copy-start(bf16[8,16384]{1,0:T(8,128)(2,1)} %view_two.3) | copy-start | bytes 786436
  84.2 1.6 %collective-permute-start.11 = (bf16[16,8,1024]{2,1,0:T(8,128)(2,1)S(1)}, bf16[16,8,1024]{2,1,0:T(8,128)(2,1)S(1)}, u32[]{:S(2)}, u32[]{:S(2)}) collective-permute-start(bf16[16,8,1024]{2,1,0:T(8,128)(2,1)S(1)} %slice.22), channel_id=1, source_target_pairs={{0,1},{1,0},{2,3},{3,2},{4,5},{5,4},{6,7},{7,6},{8,9},{9,8},{10,11... | collective-permute-start | bytes 786440 | tf_op jit(solution)/shard_map/ppermute | solution.py:55
  84.3 1.5 %collective-permute-start.12 = (f32[8,128]{1,0:T(8,128)S(1)}, f32[8,128]{1,0:T(8,128)S(1)}, u32[]{:S(2)}, u32[]{:S(2)}) collective-permute-start(f32[8,128]{1,0:T(8,128)S(1)} %add_add_fusion.mine), channel_id=1, source_target_pairs={{0,1},{1,0},{2,3},{3,2},{4,5},{5,4},{6,7},{7,6},{8,9},{9,8},{10,11... | collective-permute-start | bytes 12296 | tf_op jit(solution)/shard_map/ppermute | solution.py:55

commit v11 on v10

--- a/solution.py
+++ b/solution.py
@@ -333,8 +333,11 @@
     grads = exchange(grads)
     far, before, after = [move(scalar, pairs) for pairs in (FAR, UP, DOWN)]
     scalar = (scalar + far) + (before + after)
-    cut, scalar = lax.optimization_barrier((grads[:, shard_rows:], scalar))
-    others, other_scalar = move(cut, SWAP), move(scalar, SWAP)
+    other_scalar = move(scalar, SWAP)
+    cut, scalar, other_scalar = lax.optimization_barrier(
+        (grads[:, shard_rows:], scalar, other_scalar)
+    )
+    others = move(cut, SWAP)
     grad_one, grad_two, loss = pl.pallas_call(
         final_kernel,
         in_specs=[smem] + [vmem] * 6,

time: 88.4 us -> 88.4 us (level)
  no operation moved by 1% of the time
where the time goes in v11:
time: 88.4 us; the launch traced here: 87 us
  blocking collectives  46.7 us (53%)
  starting transfers between devices  17.1 us (19%)
  waiting for transfers between devices  15.2 us (17%)
  Pallas kernels  7.22 us (8%)
    all_to_all x3, blocking collectives, exchange(): lax.all_to_all(blocks, FINE, 0, 0, tiled=True, axis_index_groups=GROUPS)  46.7 us
    ppermute x13, starting transfers between devices, move(): return lax.ppermute(block, FINE, pairs)  13.5 us
    ppermute x13, waiting for transfers between devices, move(): return lax.ppermute(block, FINE, pairs)  12.4 us
    all_to_all x1, starting transfers between devices, exchange(): lax.all_to_all(blocks, FINE, 0, 0, tiled=True, axis_index_groups=GROUPS)  3.59 us
    all_to_all x1, waiting for transfers between devices, exchange(): lax.all_to_all(blocks, FINE, 0, 0, tiled=True, axis_index_groups=GROUPS)  2.74 us
  transfers between devices with their start and end apart: 14, of which 9 were waited for; matrix products, arithmetic and copies ran while one was open for 0% of the time, Pallas kernels for 3%

profile of v11, /device:TPU:0, one launch (start us, length us, event | category | flops | bytes accessed | tf_op | source)
XLA Modules:
  0.0 87.0 jit_solution(16265892144515657859)
XLA Ops:
  1.2 1.5 %choose_view.1 = (bf16[8,16384]{1,0:T(8,128)(2,1)S(1)}, f32[8,1024]{1,0:T(8,128)S(1)}, s32[1]{0:T(128)}) custom-call(s32[1]{0:T(128)} %bitcast.core, s32[1]{0:T(128)} %bitcast.1.place_in, bf16[8,16384]{1,0:T(8,128)(2,1)} %view_one.3, bf16[8,16384]{1,0:T(8,128)(2,1)} %view_two.3), custom_call_target="tpu_custom_call" | custom-call | tf_op jit(solution)/shard_map/choose_view/pallas_call | solution.py:257
  2.9 18.3 %all_to_all.20.own = bf16[16,16,1024]{2,1,0:T(8,128)(2,1)S(1)} all-to-all(bf16[16,16,1024]{2,1,0:T(8,128)(2,1)S(1)} %pack_rows.1), channel_id=1, replica_groups={{0,2,4,6,8,10,12,14,64,66,68,70,72,74,76,78},{16,18,20,22,24,26,28,30,8..., dimensions={0} | all-to-all | bytes 1048576 | tf_op jit(solution)/shard_map/all_to_all | solution.py:51
  21.3 2.8 %collective-permute-start.7 = (bf16[16,16,512]{2,1,0:T(8,128)(2,1)S(1)}, bf16[16,16,512]{2,1,0:T(8,128)(2,1)S(1)}, u32[]{:S(2)}, u32[]{:S(2)}) collective-permute-start(bf16[16,16,512]{2,1,0:T(8,128)(2,1)S(1)} %get-tuple-element.35.own), channel_id=1, source_target_pairs={{32,0},{34,2},{36,4},{38,6},{40,8},{42,10},{44,12},{46,14},{96,64}... | collective-permute-start | bytes 786440 | tf_op jit(solution)/shard_map/ppermute | solution.py:55
  24.1 1.1 %collective-permute-start.6 = (bf16[16,16,512]{2,1,0:T(8,128)(2,1)S(1)}, bf16[16,16,512]{2,1,0:T(8,128)(2,1)S(1)}, u32[]{:S(2)}, u32[]{:S(2)}) collective-permute-start(bf16[16,16,512]{2,1,0:T(8,128)(2,1)S(1)} %get-tuple-element.35.own), channel_id=1, source_target_pairs={{16,0},{18,2},{20,4},{22,6},{24,8},{26,10},{28,12},{30,14},{80,64}... | collective-permute-start | bytes 786440 | tf_op jit(solution)/shard_map/ppermute | solution.py:55
  26.9 2.4 %collective-permute-start.3 = (bf16[16,16,512]{2,1,0:T(8,128)(2,1)S(1)}, bf16[16,16,512]{2,1,0:T(8,128)(2,1)S(1)}, u32[]{:S(2)}, u32[]{:S(2)}) collective-permute-start(bf16[16,16,512]{2,1,0:T(8,128)(2,1)S(1)} %get-tuple-element.36.own), channel_id=1, source_target_pairs={{16,0},{18,2},{20,4},{22,6},{24,8},{26,10},{28,12},{30,14},{80,64}... | collective-permute-start | bytes 786440 | tf_op jit(solution)/shard_map/ppermute | solution.py:55
  29.4 1.2 %collective-permute-start.2 = (bf16[16,16,512]{2,1,0:T(8,128)(2,1)S(1)}, bf16[16,16,512]{2,1,0:T(8,128)(2,1)S(1)}, u32[]{:S(2)}, u32[]{:S(2)}) collective-permute-start(bf16[16,16,512]{2,1,0:T(8,128)(2,1)S(1)} %get-tuple-element.36.own), channel_id=1, source_target_pairs={{48,0},{50,2},{52,4},{54,6},{56,8},{58,10},{60,12},{62,14},{112,64... | collective-permute-start | bytes 786440 | tf_op jit(solution)/shard_map/ppermute | solution.py:55
  30.5 1.3 %collective-permute-done.6.down = bf16[16,16,512]{2,1,0:T(8,128)(2,1)S(1)} collective-permute-done((bf16[16,16,512]{2,1,0:T(8,128)(2,1)S(1)}, bf16[16,16,512]{2,1,0:T(8,128)(2,1)S(1)}, u32[]{:S(2)}, u32[]{:S(2)}) %collective-permute-start.6) | collective-permute-done | bytes 262176 | tf_op jit(solution)/shard_map/ppermute | solution.py:55
  31.8 3.8 %collective-permute-done.5.up = bf16[16,16,512]{2,1,0:T(8,128)(2,1)S(1)} collective-permute-done((bf16[16,16,512]{2,1,0:T(8,128)(2,1)S(1)}, bf16[16,16,512]{2,1,0:T(8,128)(2,1)S(1)}, u32[]{:S(2)}, u32[]{:S(2)}) %collective-permute-start.5) | collective-permute-done | bytes 262176 | tf_op jit(solution)/shard_map/ppermute | solution.py:55
  36.3 1.2 %collective-permute-done.3.down = bf16[16,16,512]{2,1,0:T(8,128)(2,1)S(1)} collective-permute-done((bf16[16,16,512]{2,1,0:T(8,128)(2,1)S(1)}, bf16[16,16,512]{2,1,0:T(8,128)(2,1)S(1)}, u32[]{:S(2)}, u32[]{:S(2)}) %collective-permute-start.3) | collective-permute-done | bytes 262176 | tf_op jit(solution)/shard_map/ppermute | solution.py:55
  37.5 0.9 %collective-permute-done.2.up = bf16[16,16,512]{2,1,0:T(8,128)(2,1)S(1)} collective-permute-done((bf16[16,16,512]{2,1,0:T(8,128)(2,1)S(1)}, bf16[16,16,512]{2,1,0:T(8,128)(2,1)S(1)}, u32[]{:S(2)}, u32[]{:S(2)}) %collective-permute-start.2) | collective-permute-done | bytes 262176 | tf_op jit(solution)/shard_map/ppermute | solution.py:55
  38.4 1.3 %gram_part.1 = (bf16[1024,512]{1,0:T(8,128)(2,1)S(1)}, bf16[16,16,1024]{2,1,0:T(8,128)(2,1)S(1)}, f32[4,512]{1,0:T(4,128)S(1)}) custom-call(f32[8,512]{1,0:T(8,128)S(1)} %get-tuple-element.38.pull, bf16[16,16,512]{2,1,0:T(8,128)(2,1)S(1)} %get-tuple-element.36.own, bf16[16,16,512]{2,1,0:T(8,128)(2,1)S(1)} %collective-permute-done.2.up, ...), custom_call_target="tpu_custom_call" | custom-call | tf_op jit(solution)/shard_map/gram_part/pallas_call | solution.py:292
  39.7 14.5 %all_to_all.21.pieces = bf16[16,16,1024]{2,1,0:T(8,128)(2,1)S(1)} all-to-all(bf16[16,16,1024]{2,1,0:T(8,128)(2,1)S(1)} %get-tuple-element.23), channel_id=1, replica_groups={{0,2,4,6,8,10,12,14,64,66,68,70,72,74,76,78},{16,18,20,22,24,26,28,30,8..., dimensions={0} | all-to-all | bytes 1048576 | tf_op jit(solution)/shard_map/all_to_all | solution.py:51
  54.2 0.9 %gram_sum.1 = bf16[16,16,1024]{2,1,0:T(8,128)(2,1)S(1)} custom-call(s32[1]{0:T(128)} %get-tuple-element.19.place, bf16[16,16,1024]{2,1,0:T(8,128)(2,1)S(1)} %all_to_all.21.pieces, f32[4,512]{1,0:T(4,128)S(1)} %get-tuple-element.24.first_stats, f32[4,512]{1,0:T(4,128)S(1)} %get-tuple-element.25.second_stats), custom_call_target="tpu_custom_call" | custom-call | tf_op jit(solution)/shard_map/gram_sum/pallas_call | solution.py:306
  55.1 13.9 %all_to_all.22.gram = bf16[16,16,1024]{2,1,0:T(8,128)(2,1)S(1)} all-to-all(bf16[16,16,1024]{2,1,0:T(8,128)(2,1)S(1)} %gram_sum.1), channel_id=1, replica_groups={{0,2,4,6,8,10,12,14,64,66,68,70,72,74,76,78},{16,18,20,22,24,26,28,30,8..., dimensions={0} | all-to-all | bytes 1048576 | tf_op jit(solution)/shard_map/all_to_all | solution.py:51
  68.9 1.6 %grad_rows.1 = (bf16[16,16,1024]{2,1,0:T(8,128)(2,1)}, f32[8,128]{1,0:T(8,128)S(1)}) custom-call(bf16[16,16,1024]{2,1,0:T(8,128)(2,1)S(1)} %all_to_all.22.gram, bf16[1024,512]{1,0:T(8,128)(2,1)S(1)} %get-tuple-element.22.first, bf16[1024,512]{1,0:T(8,128)(2,1)S(1)} %get-tuple-element.26.second, bf16[16,16,1024]{2,1,0:T(8,128)(2,1)S(1)} %all_to_all.20.own, ...), custom_call_target="tpu_custom_call" | custom-call | tf_op jit(solution)/shard_map/grad_rows/pallas_call | solution.py:316
  70.5 3.6 %all-to-all-start.3 = ((bf16[16,16,1024]{2,1,0:T(8,128)(2,1)}), bf16[16,16,1024]{2,1,0:T(8,128)(2,1)S(1)}, u32[]{:S(2)}, u32[]{:S(2)}) async-start(bf16[16,16,1024]{2,1,0:T(8,128)(2,1)} %get-tuple-element.27), calls=%async_computation.3 | async-start | bytes 1048576 | tf_op jit(solution)/shard_map/all_to_all | solution.py:51
  74.1 1.2 %collective-permute-start.10 = (f32[8,128]{1,0:T(8,128)S(1)}, f32[8,128]{1,0:T(8,128)S(1)}, u32[]{:S(2)}, u32[]{:S(2)}) collective-permute-start(f32[8,128]{1,0:T(8,128)S(1)} %get-tuple-element.28), channel_id=1, source_target_pairs={{16,0},{18,2},{20,4},{22,6},{24,8},{26,10},{28,12},{30,14},{80,64}... | collective-permute-start | bytes 12296 | tf_op jit(solution)/shard_map/ppermute | solution.py:55
  75.3 0.9 %collective-permute-start.9 = (f32[8,128]{1,0:T(8,128)S(1)}, f32[8,128]{1,0:T(8,128)S(1)}, u32[]{:S(2)}, u32[]{:S(2)}) collective-permute-start(f32[8,128]{1,0:T(8,128)S(1)} %get-tuple-element.28), channel_id=1, source_target_pairs={{48,0},{50,2},{52,4},{54,6},{56,8},{58,10},{60,12},{62,14},{112,64... | collective-permute-start | bytes 12296 | tf_op jit(solution)/shard_map/ppermute | solution.py:55
  76.2 1.4 %collective-permute-start.8 = (f32[8,128]{1,0:T(8,128)S(1)}, f32[8,128]{1,0:T(8,128)S(1)}, u32[]{:S(2)}, u32[]{:S(2)}) collective-permute-start(f32[8,128]{1,0:T(8,128)S(1)} %get-tuple-element.28), channel_id=1, source_target_pairs={{32,0},{34,2},{36,4},{38,6},{40,8},{42,10},{44,12},{46,14},{96,64}... | collective-permute-start | bytes 12296 | tf_op jit(solution)/shard_map/ppermute | solution.py:55
  77.8 2.3 %collective-permute-done.9 = f32[8,128]{1,0:T(8,128)S(1)} collective-permute-done((f32[8,128]{1,0:T(8,128)S(1)}, f32[8,128]{1,0:T(8,128)S(1)}, u32[]{:S(2)}, u32[]{:S(2)}) %collective-permute-start.9) | collective-permute-done | bytes 4128 | tf_op jit(solution)/shard_map/ppermute | solution.py:55
  80.1 1.2 %collective-permute-done.8 = f32[8,128]{1,0:T(8,128)S(1)} collective-permute-done((f32[8,128]{1,0:T(8,128)S(1)}, f32[8,128]{1,0:T(8,128)S(1)}, u32[]{:S(2)}, u32[]{:S(2)}) %collective-permute-start.8) | collective-permute-done | bytes 4128 | tf_op jit(solution)/shard_map/ppermute | solution.py:55
  81.4 2.7 %all-to-all-done.3.recv = bf16[16,16,1024]{2,1,0:T(8,128)(2,1)S(1)} async-done(((bf16[16,16,1024]{2,1,0:T(8,128)(2,1)}), bf16[16,16,1024]{2,1,0:T(8,128)(2,1)S(1)}, u32[]{:S(2)}, u32[]{:S(2)}) %all-to-all-start.3) | async-done | bytes 524320 | tf_op jit(solution)/shard_map/all_to_all | solution.py:51
  84.3 1.5 %collective-permute-done.12.got = bf16[16,8,1024]{2,1,0:T(8,128)(2,1)S(1)} collective-permute-done((bf16[16,8,1024]{2,1,0:T(8,128)(2,1)S(1)}, bf16[16,8,1024]{2,1,0:T(8,128)(2,1)S(1)}, u32[]{:S(2)}, u32[]{:S(2)}) %collective-permute-start.12) | collective-permute-done | bytes 262176 | tf_op jit(solution)/shard_map/ppermute | solution.py:55
  85.8 1.1 %add_pull.1 = (f32[8,16384]{1,0:T(8,128)}, f32[8,16384]{1,0:T(8,128)}, f32[1]{0:T(128)}) custom-call(s32[1]{0:T(128)} %bitcast.core, bf16[16,16,1024]{2,1,0:T(8,128)(2,1)S(1)} %all-to-all-done.3.recv, bf16[16,8,1024]{2,1,0:T(8,128)(2,1)S(1)} %collective-permute-done.12.got, f32[8,128]{1,0:T(8,128)S(1)} %add_add_fusion.mine, ...), custom_call_target="tpu_custom_call" | custom-call | tf_op jit(solution)/shard_map/add_pull/pallas_call | solution.py:341
  (22 shorter events, 3.5 us)
Async XLA Ops:
  0.6 2.1 %collective-permute-start = (bf16[8,16384]{1,0:T(8,128)(2,1)}, bf16[8,16384]{1,0:T(8,128)(2,1)S(1)}, u32[]{:S(2)}, u32[]{:S(2)}) collective-permute-start(bf16[8,16384]{1,0:T(8,128)(2,1)} %view_one.3), channel_id=1, source_target_pairs={{0,1},{1,0},{2,3},{3,2},{4,5},{5,4},{6,7},{7,6},{8,9},{9,8},{10,11... | collective-permute-start | bytes 786440 | tf_op jit(solution)/shard_map/ppermute | solution.py:55
  0.7 2.1 %collective-permute-start.1 = (bf16[8,16384]{1,0:T(8,128)(2,1)}, bf16[8,16384]{1,0:T(8,128)(2,1)S(1)}, u32[]{:S(2)}, u32[]{:S(2)}) collective-permute-start(bf16[8,16384]{1,0:T(8,128)(2,1)} %view_two.3), channel_id=1, source_target_pairs={{0,1},{1,0},{2,3},{3,2},{4,5},{5,4},{6,7},{7,6},{8,9},{9,8},{10,11... | collective-permute-start | bytes 786440 | tf_op jit(solution)/shard_map/ppermute | solution.py:55
  21.3 8.1 %collective-permute-start.7 = (bf16[16,16,512]{2,1,0:T(8,128)(2,1)S(1)}, bf16[16,16,512]{2,1,0:T(8,128)(2,1)S(1)}, u32[]{:S(2)}, u32[]{:S(2)}) collective-permute-start(bf16[16,16,512]{2,1,0:T(8,128)(2,1)S(1)} %get-tuple-element.35.own), channel_id=1, source_target_pairs={{32,0},{34,2},{36,4},{38,6},{40,8},{42,10},{44,12},{46,14},{96,64}... | collective-permute-start | bytes 786440 | tf_op jit(solution)/shard_map/ppermute | solution.py:55
  24.1 7.8 %collective-permute-start.6 = (bf16[16,16,512]{2,1,0:T(8,128)(2,1)S(1)}, bf16[16,16,512]{2,1,0:T(8,128)(2,1)S(1)}, u32[]{:S(2)}, u32[]{:S(2)}) collective-permute-start(bf16[16,16,512]{2,1,0:T(8,128)(2,1)S(1)} %get-tuple-element.35.own), channel_id=1, source_target_pairs={{16,0},{18,2},{20,4},{22,6},{24,8},{26,10},{28,12},{30,14},{80,64}... | collective-permute-start | bytes 786440 | tf_op jit(solution)/shard_map/ppermute | solution.py:55
  25.2 10.4 %collective-permute-start.5 = (bf16[16,16,512]{2,1,0:T(8,128)(2,1)S(1)}, bf16[16,16,512]{2,1,0:T(8,128)(2,1)S(1)}, u32[]{:S(2)}, u32[]{:S(2)}) collective-permute-start(bf16[16,16,512]{2,1,0:T(8,128)(2,1)S(1)} %get-tuple-element.35.own), channel_id=1, source_target_pairs={{48,0},{50,2},{52,4},{54,6},{56,8},{58,10},{60,12},{62,14},{112,64... | collective-permute-start | bytes 786440 | tf_op jit(solution)/shard_map/ppermute | solution.py:55
  26.1 10.2 %collective-permute-start.4 = (bf16[16,16,512]{2,1,0:T(8,128)(2,1)S(1)}, bf16[16,16,512]{2,1,0:T(8,128)(2,1)S(1)}, u32[]{:S(2)}, u32[]{:S(2)}) collective-permute-start(bf16[16,16,512]{2,1,0:T(8,128)(2,1)S(1)} %get-tuple-element.36.own), channel_id=1, source_target_pairs={{32,0},{34,2},{36,4},{38,6},{40,8},{42,10},{44,12},{46,14},{96,64}... | collective-permute-start | bytes 786440 | tf_op jit(solution)/shard_map/ppermute | solution.py:55
  26.9 10.6 %collective-permute-start.3 = (bf16[16,16,512]{2,1,0:T(8,128)(2,1)S(1)}, bf16[16,16,512]{2,1,0:T(8,128)(2,1)S(1)}, u32[]{:S(2)}, u32[]{:S(2)}) collective-permute-start(bf16[16,16,512]{2,1,0:T(8,128)(2,1)S(1)} %get-tuple-element.36.own), channel_id=1, source_target_pairs={{16,0},{18,2},{20,4},{22,6},{24,8},{26,10},{28,12},{30,14},{80,64}... | collective-permute-start | bytes 786440 | tf_op jit(solution)/shard_map/ppermute | solution.py:55
  29.4 9.0 %collective-permute-start.2 = (bf16[16,16,512]{2,1,0:T(8,128)(2,1)S(1)}, bf16[16,16,512]{2,1,0:T(8,128)(2,1)S(1)}, u32[]{:S(2)}, u32[]{:S(2)}) collective-permute-start(bf16[16,16,512]{2,1,0:T(8,128)(2,1)S(1)} %get-tuple-element.36.own), channel_id=1, source_target_pairs={{48,0},{50,2},{52,4},{54,6},{56,8},{58,10},{60,12},{62,14},{112,64... | collective-permute-start | bytes 786440 | tf_op jit(solution)/shard_map/ppermute | solution.py:55
  70.5 13.7 %all-to-all-start.3 = ((bf16[16,16,1024]{2,1,0:T(8,128)(2,1)}), bf16[16,16,1024]{2,1,0:T(8,128)(2,1)S(1)}, u32[]{:S(2)}, u32[]{:S(2)}) async-start(bf16[16,16,1024]{2,1,0:T(8,128)(2,1)} %get-tuple-element.27), calls=%async_computation.3 | async-start | bytes 1048576 | tf_op jit(solution)/shard_map/all_to_all | solution.py:51
  74.1 3.7 %collective-permute-start.10 = (f32[8,128]{1,0:T(8,128)S(1)}, f32[8,128]{1,0:T(8,128)S(1)}, u32[]{:S(2)}, u32[]{:S(2)}) collective-permute-start(f32[8,128]{1,0:T(8,128)S(1)} %get-tuple-element.28), channel_id=1, source_target_pairs={{16,0},{18,2},{20,4},{22,6},{24,8},{26,10},{28,12},{30,14},{80,64}... | collective-permute-start | bytes 12296 | tf_op jit(solution)/shard_map/ppermute | solution.py:55
  75.3 4.8 %collective-permute-start.9 = (f32[8,128]{1,0:T(8,128)S(1)}, f32[8,128]{1,0:T(8,128)S(1)}, u32[]{:S(2)}, u32[]{:S(2)}) collective-permute-start(f32[8,128]{1,0:T(8,128)S(1)} %get-tuple-element.28), channel_id=1, source_target_pairs={{48,0},{50,2},{52,4},{54,6},{56,8},{58,10},{60,12},{62,14},{112,64... | collective-permute-start | bytes 12296 | tf_op jit(solution)/shard_map/ppermute | solution.py:55
  76.2 5.1 %collective-permute-start.8 = (f32[8,128]{1,0:T(8,128)S(1)}, f32[8,128]{1,0:T(8,128)S(1)}, u32[]{:S(2)}, u32[]{:S(2)}) collective-permute-start(f32[8,128]{1,0:T(8,128)S(1)} %get-tuple-element.28), channel_id=1, source_target_pairs={{32,0},{34,2},{36,4},{38,6},{40,8},{42,10},{44,12},{46,14},{96,64}... | collective-permute-start | bytes 12296 | tf_op jit(solution)/shard_map/ppermute | solution.py:55
  81.3 4.5 %copy-start = (bf16[8,16384]{1,0:T(8,128)(2,1)S(1)}, bf16[8,16384]{1,0:T(8,128)(2,1)}, u32[]{:S(2)}) copy-start(bf16[8,16384]{1,0:T(8,128)(2,1)} %view_one.3) | copy-start | bytes 786436
  81.3 4.5 %copy-start.1 = (bf16[8,16384]{1,0:T(8,128)(2,1)S(1)}, bf16[8,16384]{1,0:T(8,128)(2,1)}, u32[]{:S(2)}) copy-start(bf16[8,16384]{1,0:T(8,128)(2,1)} %view_two.3) | copy-start | bytes 786436
  81.3 2.9 %collective-permute-start.11 = (f32[8,128]{1,0:T(8,128)S(1)}, f32[8,128]{1,0:T(8,128)S(1)}, u32[]{:S(2)}, u32[]{:S(2)}) collective-permute-start(f32[8,128]{1,0:T(8,128)S(1)} %add_add_fusion.mine), channel_id=1, source_target_pairs={{0,1},{1,0},{2,3},{3,2},{4,5},{5,4},{6,7},{7,6},{8,9},{9,8},{10,11... | collective-permute-start | bytes 12296 | tf_op jit(solution)/shard_map/ppermute | solution.py:55
  84.2 1.6 %collective-permute-start.12 = (bf16[16,8,1024]{2,1,0:T(8,128)(2,1)S(1)}, bf16[16,8,1024]{2,1,0:T(8,128)(2,1)S(1)}, u32[]{:S(2)}, u32[]{:S(2)}) collective-permute-start(bf16[16,8,1024]{2,1,0:T(8,128)(2,1)S(1)} %slice.22), channel_id=1, source_target_pairs={{0,1},{1,0},{2,3},{3,2},{4,5},{5,4},{6,7},{7,6},{8,9},{9,8},{10,11... | collective-permute-start | bytes 786440 | tf_op jit(solution)/shard_map/ppermute | solution.py:55

commit v12 on v10

--- a/solution.py
+++ b/solution.py
@@ -120,15 +120,21 @@
         stats[3:4, cut] = share
 
 
-def gram_kernel(sizes, pull, own, up, down, far, first, second, part, stats):
+def first_kernel(sizes, pull, own, up, down, far, rounded, stats, product):
+    center_kernel(sizes, pull, own, up, down, far, rounded, stats)
+    mine = rounded[pl.ds(0, product.shape[0])]
+    product[...] = lax.dot_general(
+        mine, rounded[...], CONTRACT_LAST, preferred_element_type=jnp.float32
+    )
+
+
+def gram_kernel(sizes, pull, own, up, down, far, partial, second, part, stats):
     batch_rows, feature_count, row_parts = sizes
     group_rows = batch_rows // row_parts
     center_kernel(sizes, pull, own, up, down, far, second, stats)
-    product = 0.0
-    for half in (first, second):
-        product += lax.dot_general(
-            half[pl.ds(0, group_rows)], half[...], CONTRACT_LAST, preferred_element_type=jnp.float32
-        )
+    product = partial[...] + lax.dot_general(
+        second[pl.ds(0, group_rows)], second[...], CONTRACT_LAST, preferred_element_type=jnp.float32
+    )
     part[...] = product.astype(jnp.bfloat16).reshape(part.shape)
 
 
@@ -281,11 +287,15 @@
     (far, up, down), (far_second, up_second, down_second) = copies
     rounded_shape = jax.ShapeDtypeStruct((batch_rows, half), jnp.bfloat16)
     stats_shape = jax.ShapeDtypeStruct((4, half), jnp.float32)
-    first, first_stats = pl.pallas_call(
-        functools.partial(center_kernel, sizes),
+    first, first_stats, partial = pl.pallas_call(
+        functools.partial(first_kernel, sizes),
         in_specs=[vmem] * 5,
-        out_specs=[vmem] * 2,
-        out_shape=[rounded_shape, stats_shape],
+        out_specs=[vmem] * 3,
+        out_shape=[
+            rounded_shape,
+            stats_shape,
+            jax.ShapeDtypeStruct((batch_rows // row_parts, batch_rows), jnp.float32),
+        ],
         compiler_params=room(12),
         name="center_first",
     )(pull[:, :half], halves[0], up, down, far)
@@ -300,7 +310,7 @@
         ],
         compiler_params=room(16),
         name="gram_part",
-    )(pull[:, half:], halves[1], up_second, down_second, far_second, first)
+    )(pull[:, half:], halves[1], up_second, down_second, far_second, partial)
 
     pieces = exchange(part)
     sent = pl.pallas_call(

time: 88.4 us -> 88.1 us (level)
  no operation moved by 1% of the time
where the time goes in v12:
time: 88.1 us; the launch traced here: 86.7 us
  blocking collectives  46.7 us (53%)
  starting transfers between devices  17.5 us (20%)
  waiting for transfers between devices  14.5 us (16%)
  Pallas kernels  7.27 us (8%)
    all_to_all x3, blocking collectives, exchange(): lax.all_to_all(blocks, FINE, 0, 0, tiled=True, axis_index_groups=GROUPS)  46.7 us
    ppermute x13, starting transfers between devices, move(): return lax.ppermute(block, FINE, pairs)  13.9 us
    ppermute x13, waiting for transfers between devices, move(): return lax.ppermute(block, FINE, pairs)  11.6 us
    all_to_all x1, starting transfers between devices, exchange(): lax.all_to_all(blocks, FINE, 0, 0, tiled=True, axis_index_groups=GROUPS)  3.59 us
    all_to_all x1, waiting for transfers between devices, exchange(): lax.all_to_all(blocks, FINE, 0, 0, tiled=True, axis_index_groups=GROUPS)  2.84 us
  transfers between devices with their start and end apart: 14, of which 9 were waited for; matrix products, arithmetic and copies ran while one was open for 0% of the time, Pallas kernels for 3%

profile of v12, /device:TPU:0, one launch (start us, length us, event | category | flops | bytes accessed | tf_op | source)
XLA Modules:
  0.0 86.7 jit_solution(11336614089450567312)
XLA Ops:
  1.2 1.5 %choose_view.1 = (bf16[8,16384]{1,0:T(8,128)(2,1)S(1)}, f32[8,1024]{1,0:T(8,128)S(1)}, s32[1]{0:T(128)}) custom-call(s32[1]{0:T(128)} %bitcast.core, s32[1]{0:T(128)} %bitcast.1.place_in, bf16[8,16384]{1,0:T(8,128)(2,1)} %view_one.3, bf16[8,16384]{1,0:T(8,128)(2,1)} %view_two.3), custom_call_target="tpu_custom_call" | custom-call | tf_op jit(solution)/shard_map/choose_view/pallas_call | solution.py:263
  2.9 18.3 %all_to_all.20.own = bf16[16,16,1024]{2,1,0:T(8,128)(2,1)S(1)} all-to-all(bf16[16,16,1024]{2,1,0:T(8,128)(2,1)S(1)} %pack_rows.1), channel_id=1, replica_groups={{0,2,4,6,8,10,12,14,64,66,68,70,72,74,76,78},{16,18,20,22,24,26,28,30,8..., dimensions={0} | all-to-all | bytes 1048576 | tf_op jit(solution)/shard_map/all_to_all | solution.py:51
  21.3 2.8 %collective-permute-start.7 = (bf16[16,16,512]{2,1,0:T(8,128)(2,1)S(1)}, bf16[16,16,512]{2,1,0:T(8,128)(2,1)S(1)}, u32[]{:S(2)}, u32[]{:S(2)}) collective-permute-start(bf16[16,16,512]{2,1,0:T(8,128)(2,1)S(1)} %get-tuple-element.35.own), channel_id=1, source_target_pairs={{32,0},{34,2},{36,4},{38,6},{40,8},{42,10},{44,12},{46,14},{96,64}... | collective-permute-start | bytes 786440 | tf_op jit(solution)/shard_map/ppermute | solution.py:55
  24.1 1.1 %collective-permute-start.6 = (bf16[16,16,512]{2,1,0:T(8,128)(2,1)S(1)}, bf16[16,16,512]{2,1,0:T(8,128)(2,1)S(1)}, u32[]{:S(2)}, u32[]{:S(2)}) collective-permute-start(bf16[16,16,512]{2,1,0:T(8,128)(2,1)S(1)} %get-tuple-element.35.own), channel_id=1, source_target_pairs={{16,0},{18,2},{20,4},{22,6},{24,8},{26,10},{28,12},{30,14},{80,64}... | collective-permute-start | bytes 786440 | tf_op jit(solution)/shard_map/ppermute | solution.py:55
  26.9 2.4 %collective-permute-start.3 = (bf16[16,16,512]{2,1,0:T(8,128)(2,1)S(1)}, bf16[16,16,512]{2,1,0:T(8,128)(2,1)S(1)}, u32[]{:S(2)}, u32[]{:S(2)}) collective-permute-start(bf16[16,16,512]{2,1,0:T(8,128)(2,1)S(1)} %get-tuple-element.36.own), channel_id=1, source_target_pairs={{16,0},{18,2},{20,4},{22,6},{24,8},{26,10},{28,12},{30,14},{80,64}... | collective-permute-start | bytes 786440 | tf_op jit(solution)/shard_map/ppermute | solution.py:55
  29.4 1.2 %collective-permute-start.2 = (bf16[16,16,512]{2,1,0:T(8,128)(2,1)S(1)}, bf16[16,16,512]{2,1,0:T(8,128)(2,1)S(1)}, u32[]{:S(2)}, u32[]{:S(2)}) collective-permute-start(bf16[16,16,512]{2,1,0:T(8,128)(2,1)S(1)} %get-tuple-element.36.own), channel_id=1, source_target_pairs={{48,0},{50,2},{52,4},{54,6},{56,8},{58,10},{60,12},{62,14},{112,64... | collective-permute-start | bytes 786440 | tf_op jit(solution)/shard_map/ppermute | solution.py:55
  30.5 1.3 %collective-permute-done.6.down = bf16[16,16,512]{2,1,0:T(8,128)(2,1)S(1)} collective-permute-done((bf16[16,16,512]{2,1,0:T(8,128)(2,1)S(1)}, bf16[16,16,512]{2,1,0:T(8,128)(2,1)S(1)}, u32[]{:S(2)}, u32[]{:S(2)}) %collective-permute-start.6) | collective-permute-done | bytes 262176 | tf_op jit(solution)/shard_map/ppermute | solution.py:55
  31.8 3.8 %collective-permute-done.5.up = bf16[16,16,512]{2,1,0:T(8,128)(2,1)S(1)} collective-permute-done((bf16[16,16,512]{2,1,0:T(8,128)(2,1)S(1)}, bf16[16,16,512]{2,1,0:T(8,128)(2,1)S(1)}, u32[]{:S(2)}, u32[]{:S(2)}) %collective-permute-start.5) | collective-permute-done | bytes 262176 | tf_op jit(solution)/shard_map/ppermute | solution.py:55
  35.6 1.0 %center_first.1 = (bf16[1024,512]{1,0:T(8,128)(2,1)S(1)}, f32[4,512]{1,0:T(4,128)S(1)}, f32[256,1024]{1,0:T(8,128)S(1)}) custom-call(f32[8,512]{1,0:T(8,128)S(1)} %get-tuple-element.37.pull, bf16[16,16,512]{2,1,0:T(8,128)(2,1)S(1)} %get-tuple-element.35.own, bf16[16,16,512]{2,1,0:T(8,128)(2,1)S(1)} %collective-permute-done.5.up, ...), custom_call_target="tpu_custom_call" | custom-call | tf_op jit(solution)/shard_map/center_first/pallas_call | solution.py:290
  37.5 0.9 %collective-permute-done.2.up = bf16[16,16,512]{2,1,0:T(8,128)(2,1)S(1)} collective-permute-done((bf16[16,16,512]{2,1,0:T(8,128)(2,1)S(1)}, bf16[16,16,512]{2,1,0:T(8,128)(2,1)S(1)}, u32[]{:S(2)}, u32[]{:S(2)}) %collective-permute-start.2) | collective-permute-done | bytes 262176 | tf_op jit(solution)/shard_map/ppermute | solution.py:55
  38.4 1.0 %gram_part.1 = (bf16[1024,512]{1,0:T(8,128)(2,1)S(1)}, bf16[16,16,1024]{2,1,0:T(8,128)(2,1)S(1)}, f32[4,512]{1,0:T(4,128)S(1)}) custom-call(f32[8,512]{1,0:T(8,128)S(1)} %get-tuple-element.38.pull, bf16[16,16,512]{2,1,0:T(8,128)(2,1)S(1)} %get-tuple-element.36.own, bf16[16,16,512]{2,1,0:T(8,128)(2,1)S(1)} %collective-permute-done.2.up, ...), custom_call_target="tpu_custom_call" | custom-call | tf_op jit(solution)/shard_map/gram_part/pallas_call | solution.py:302
  39.4 14.5 %all_to_all.21.pieces = bf16[16,16,1024]{2,1,0:T(8,128)(2,1)S(1)} all-to-all(bf16[16,16,1024]{2,1,0:T(8,128)(2,1)S(1)} %get-tuple-element.23), channel_id=1, replica_groups={{0,2,4,6,8,10,12,14,64,66,68,70,72,74,76,78},{16,18,20,22,24,26,28,30,8..., dimensions={0} | all-to-all | bytes 1048576 | tf_op jit(solution)/shard_map/all_to_all | solution.py:51
  53.9 0.9 %gram_sum.1 = bf16[16,16,1024]{2,1,0:T(8,128)(2,1)S(1)} custom-call(s32[1]{0:T(128)} %get-tuple-element.19.place, bf16[16,16,1024]{2,1,0:T(8,128)(2,1)S(1)} %all_to_all.21.pieces, f32[4,512]{1,0:T(4,128)S(1)} %get-tuple-element.24.first_stats, f32[4,512]{1,0:T(4,128)S(1)} %get-tuple-element.25.second_stats), custom_call_target="tpu_custom_call" | custom-call | tf_op jit(solution)/shard_map/gram_sum/pallas_call | solution.py:316
  54.8 13.9 %all_to_all.22.gram = bf16[16,16,1024]{2,1,0:T(8,128)(2,1)S(1)} all-to-all(bf16[16,16,1024]{2,1,0:T(8,128)(2,1)S(1)} %gram_sum.1), channel_id=1, replica_groups={{0,2,4,6,8,10,12,14,64,66,68,70,72,74,76,78},{16,18,20,22,24,26,28,30,8..., dimensions={0} | all-to-all | bytes 1048576 | tf_op jit(solution)/shard_map/all_to_all | solution.py:51
  68.7 1.6 %grad_rows.1 = (bf16[16,16,1024]{2,1,0:T(8,128)(2,1)}, f32[8,128]{1,0:T(8,128)S(1)}) custom-call(bf16[16,16,1024]{2,1,0:T(8,128)(2,1)S(1)} %all_to_all.22.gram, bf16[1024,512]{1,0:T(8,128)(2,1)S(1)} %get-tuple-element.26.first, bf16[1024,512]{1,0:T(8,128)(2,1)S(1)} %get-tuple-element.27.second, bf16[16,16,1024]{2,1,0:T(8,128)(2,1)S(1)} %all_to_all.20.own, ...), custom_call_target="tpu_custom_call" | custom-call | tf_op jit(solution)/shard_map/grad_rows/pallas_call | solution.py:326
  70.3 3.6 %all-to-all-start.3 = ((bf16[16,16,1024]{2,1,0:T(8,128)(2,1)}), bf16[16,16,1024]{2,1,0:T(8,128)(2,1)S(1)}, u32[]{:S(2)}, u32[]{:S(2)}) async-start(bf16[16,16,1024]{2,1,0:T(8,128)(2,1)} %get-tuple-element.28), calls=%async_computation.3 | async-start | bytes 1048576 | tf_op jit(solution)/shard_map/all_to_all | solution.py:51
  73.9 1.2 %collective-permute-start.10 = (f32[8,128]{1,0:T(8,128)S(1)}, f32[8,128]{1,0:T(8,128)S(1)}, u32[]{:S(2)}, u32[]{:S(2)}) collective-permute-start(f32[8,128]{1,0:T(8,128)S(1)} %get-tuple-element.29), channel_id=1, source_target_pairs={{16,0},{18,2},{20,4},{22,6},{24,8},{26,10},{28,12},{30,14},{80,64}... | collective-permute-start | bytes 12296 | tf_op jit(solution)/shard_map/ppermute | solution.py:55
  75.1 0.9 %collective-permute-start.9 = (f32[8,128]{1,0:T(8,128)S(1)}, f32[8,128]{1,0:T(8,128)S(1)}, u32[]{:S(2)}, u32[]{:S(2)}) collective-permute-start(f32[8,128]{1,0:T(8,128)S(1)} %get-tuple-element.29), channel_id=1, source_target_pairs={{48,0},{50,2},{52,4},{54,6},{56,8},{58,10},{60,12},{62,14},{112,64... | collective-permute-start | bytes 12296 | tf_op jit(solution)/shard_map/ppermute | solution.py:55
  76.0 1.4 %collective-permute-start.8 = (f32[8,128]{1,0:T(8,128)S(1)}, f32[8,128]{1,0:T(8,128)S(1)}, u32[]{:S(2)}, u32[]{:S(2)}) collective-permute-start(f32[8,128]{1,0:T(8,128)S(1)} %get-tuple-element.29), channel_id=1, source_target_pairs={{32,0},{34,2},{36,4},{38,6},{40,8},{42,10},{44,12},{46,14},{96,64}... | collective-permute-start | bytes 12296 | tf_op jit(solution)/shard_map/ppermute | solution.py:55
  77.5 2.3 %collective-permute-done.9 = f32[8,128]{1,0:T(8,128)S(1)} collective-permute-done((f32[8,128]{1,0:T(8,128)S(1)}, f32[8,128]{1,0:T(8,128)S(1)}, u32[]{:S(2)}, u32[]{:S(2)}) %collective-permute-start.9) | collective-permute-done | bytes 4128 | tf_op jit(solution)/shard_map/ppermute | solution.py:55
  79.9 1.2 %collective-permute-done.8 = f32[8,128]{1,0:T(8,128)S(1)} collective-permute-done((f32[8,128]{1,0:T(8,128)S(1)}, f32[8,128]{1,0:T(8,128)S(1)}, u32[]{:S(2)}, u32[]{:S(2)}) %collective-permute-start.8) | collective-permute-done | bytes 4128 | tf_op jit(solution)/shard_map/ppermute | solution.py:55
  81.1 2.8 %all-to-all-done.3.recv = bf16[16,16,1024]{2,1,0:T(8,128)(2,1)S(1)} async-done(((bf16[16,16,1024]{2,1,0:T(8,128)(2,1)}), bf16[16,16,1024]{2,1,0:T(8,128)(2,1)S(1)}, u32[]{:S(2)}, u32[]{:S(2)}) %all-to-all-start.3) | async-done | bytes 524320 | tf_op jit(solution)/shard_map/all_to_all | solution.py:51
  84.5 1.0 %collective-permute-done.12.other = f32[8,128]{1,0:T(8,128)S(1)} collective-permute-done((f32[8,128]{1,0:T(8,128)S(1)}, f32[8,128]{1,0:T(8,128)S(1)}, u32[]{:S(2)}, u32[]{:S(2)}) %collective-permute-start.12) | collective-permute-done | bytes 4128 | tf_op jit(solution)/shard_map/ppermute | solution.py:55
  85.6 1.1 %add_pull.1 = (f32[8,16384]{1,0:T(8,128)}, f32[8,16384]{1,0:T(8,128)}, f32[1]{0:T(128)}) custom-call(s32[1]{0:T(128)} %bitcast.core, bf16[16,16,1024]{2,1,0:T(8,128)(2,1)S(1)} %all-to-all-done.3.recv, bf16[16,8,1024]{2,1,0:T(8,128)(2,1)S(1)} %collective-permute-done.11.got, f32[8,128]{1,0:T(8,128)S(1)} %add_add_fusion.mine, ...), custom_call_target="tpu_custom_call" | custom-call | tf_op jit(solution)/shard_map/add_pull/pallas_call | solution.py:348
  (22 shorter events, 4.1 us)
Async XLA Ops:
  0.6 2.1 %collective-permute-start = (bf16[8,16384]{1,0:T(8,128)(2,1)}, bf16[8,16384]{1,0:T(8,128)(2,1)S(1)}, u32[]{:S(2)}, u32[]{:S(2)}) collective-permute-start(bf16[8,16384]{1,0:T(8,128)(2,1)} %view_one.3), channel_id=1, source_target_pairs={{0,1},{1,0},{2,3},{3,2},{4,5},{5,4},{6,7},{7,6},{8,9},{9,8},{10,11... | collective-permute-start | bytes 786440 | tf_op jit(solution)/shard_map/ppermute | solution.py:55
  0.7 2.1 %collective-permute-start.1 = (bf16[8,16384]{1,0:T(8,128)(2,1)}, bf16[8,16384]{1,0:T(8,128)(2,1)S(1)}, u32[]{:S(2)}, u32[]{:S(2)}) collective-permute-start(bf16[8,16384]{1,0:T(8,128)(2,1)} %view_two.3), channel_id=1, source_target_pairs={{0,1},{1,0},{2,3},{3,2},{4,5},{5,4},{6,7},{7,6},{8,9},{9,8},{10,11... | collective-permute-start | bytes 786440 | tf_op jit(solution)/shard_map/ppermute | solution.py:55
  21.3 8.1 %collective-permute-start.7 = (bf16[16,16,512]{2,1,0:T(8,128)(2,1)S(1)}, bf16[16,16,512]{2,1,0:T(8,128)(2,1)S(1)}, u32[]{:S(2)}, u32[]{:S(2)}) collective-permute-start(bf16[16,16,512]{2,1,0:T(8,128)(2,1)S(1)} %get-tuple-element.35.own), channel_id=1, source_target_pairs={{32,0},{34,2},{36,4},{38,6},{40,8},{42,10},{44,12},{46,14},{96,64}... | collective-permute-start | bytes 786440 | tf_op jit(solution)/shard_map/ppermute | solution.py:55
  24.1 7.8 %collective-permute-start.6 = (bf16[16,16,512]{2,1,0:T(8,128)(2,1)S(1)}, bf16[16,16,512]{2,1,0:T(8,128)(2,1)S(1)}, u32[]{:S(2)}, u32[]{:S(2)}) collective-permute-start(bf16[16,16,512]{2,1,0:T(8,128)(2,1)S(1)} %get-tuple-element.35.own), channel_id=1, source_target_pairs={{16,0},{18,2},{20,4},{22,6},{24,8},{26,10},{28,12},{30,14},{80,64}... | collective-permute-start | bytes 786440 | tf_op jit(solution)/shard_map/ppermute | solution.py:55
  25.2 10.4 %collective-permute-start.5 = (bf16[16,16,512]{2,1,0:T(8,128)(2,1)S(1)}, bf16[16,16,512]{2,1,0:T(8,128)(2,1)S(1)}, u32[]{:S(2)}, u32[]{:S(2)}) collective-permute-start(bf16[16,16,512]{2,1,0:T(8,128)(2,1)S(1)} %get-tuple-element.35.own), channel_id=1, source_target_pairs={{48,0},{50,2},{52,4},{54,6},{56,8},{58,10},{60,12},{62,14},{112,64... | collective-permute-start | bytes 786440 | tf_op jit(solution)/shard_map/ppermute | solution.py:55
  26.1 10.5 %collective-permute-start.4 = (bf16[16,16,512]{2,1,0:T(8,128)(2,1)S(1)}, bf16[16,16,512]{2,1,0:T(8,128)(2,1)S(1)}, u32[]{:S(2)}, u32[]{:S(2)}) collective-permute-start(bf16[16,16,512]{2,1,0:T(8,128)(2,1)S(1)} %get-tuple-element.36.own), channel_id=1, source_target_pairs={{32,0},{34,2},{36,4},{38,6},{40,8},{42,10},{44,12},{46,14},{96,64}... | collective-permute-start | bytes 786440 | tf_op jit(solution)/shard_map/ppermute | solution.py:55
  26.9 10.6 %collective-permute-start.3 = (bf16[16,16,512]{2,1,0:T(8,128)(2,1)S(1)}, bf16[16,16,512]{2,1,0:T(8,128)(2,1)S(1)}, u32[]{:S(2)}, u32[]{:S(2)}) collective-permute-start(bf16[16,16,512]{2,1,0:T(8,128)(2,1)S(1)} %get-tuple-element.36.own), channel_id=1, source_target_pairs={{16,0},{18,2},{20,4},{22,6},{24,8},{26,10},{28,12},{30,14},{80,64}... | collective-permute-start | bytes 786440 | tf_op jit(solution)/shard_map/ppermute | solution.py:55
  29.4 9.0 %collective-permute-start.2 = (bf16[16,16,512]{2,1,0:T(8,128)(2,1)S(1)}, bf16[16,16,512]{2,1,0:T(8,128)(2,1)S(1)}, u32[]{:S(2)}, u32[]{:S(2)}) collective-permute-start(bf16[16,16,512]{2,1,0:T(8,128)(2,1)S(1)} %get-tuple-element.36.own), channel_id=1, source_target_pairs={{48,0},{50,2},{52,4},{54,6},{56,8},{58,10},{60,12},{62,14},{112,64... | collective-permute-start | bytes 786440 | tf_op jit(solution)/shard_map/ppermute | solution.py:55
  70.3 13.7 %all-to-all-start.3 = ((bf16[16,16,1024]{2,1,0:T(8,128)(2,1)}), bf16[16,16,1024]{2,1,0:T(8,128)(2,1)S(1)}, u32[]{:S(2)}, u32[]{:S(2)}) async-start(bf16[16,16,1024]{2,1,0:T(8,128)(2,1)} %get-tuple-element.28), calls=%async_computation.3 | async-start | bytes 1048576 | tf_op jit(solution)/shard_map/all_to_all | solution.py:51
  73.9 3.7 %collective-permute-start.10 = (f32[8,128]{1,0:T(8,128)S(1)}, f32[8,128]{1,0:T(8,128)S(1)}, u32[]{:S(2)}, u32[]{:S(2)}) collective-permute-start(f32[8,128]{1,0:T(8,128)S(1)} %get-tuple-element.29), channel_id=1, source_target_pairs={{16,0},{18,2},{20,4},{22,6},{24,8},{26,10},{28,12},{30,14},{80,64}... | collective-permute-start | bytes 12296 | tf_op jit(solution)/shard_map/ppermute | solution.py:55
  75.1 4.8 %collective-permute-start.9 = (f32[8,128]{1,0:T(8,128)S(1)}, f32[8,128]{1,0:T(8,128)S(1)}, u32[]{:S(2)}, u32[]{:S(2)}) collective-permute-start(f32[8,128]{1,0:T(8,128)S(1)} %get-tuple-element.29), channel_id=1, source_target_pairs={{48,0},{50,2},{52,4},{54,6},{56,8},{58,10},{60,12},{62,14},{112,64... | collective-permute-start | bytes 12296 | tf_op jit(solution)/shard_map/ppermute | solution.py:55
  76.0 5.1 %collective-permute-start.8 = (f32[8,128]{1,0:T(8,128)S(1)}, f32[8,128]{1,0:T(8,128)S(1)}, u32[]{:S(2)}, u32[]{:S(2)}) collective-permute-start(f32[8,128]{1,0:T(8,128)S(1)} %get-tuple-element.29), channel_id=1, source_target_pairs={{32,0},{34,2},{36,4},{38,6},{40,8},{42,10},{44,12},{46,14},{96,64}... | collective-permute-start | bytes 12296 | tf_op jit(solution)/shard_map/ppermute | solution.py:55
  81.1 4.5 %copy-start = (bf16[8,16384]{1,0:T(8,128)(2,1)S(1)}, bf16[8,16384]{1,0:T(8,128)(2,1)}, u32[]{:S(2)}) copy-start(bf16[8,16384]{1,0:T(8,128)(2,1)} %view_one.3) | copy-start | bytes 786436
  81.1 4.5 %copy-start.1 = (bf16[8,16384]{1,0:T(8,128)(2,1)S(1)}, bf16[8,16384]{1,0:T(8,128)(2,1)}, u32[]{:S(2)}) copy-start(bf16[8,16384]{1,0:T(8,128)(2,1)} %view_two.3) | copy-start | bytes 786436
  83.9 1.6 %collective-permute-start.11 = (bf16[16,8,1024]{2,1,0:T(8,128)(2,1)S(1)}, bf16[16,8,1024]{2,1,0:T(8,128)(2,1)S(1)}, u32[]{:S(2)}, u32[]{:S(2)}) collective-permute-start(bf16[16,8,1024]{2,1,0:T(8,128)(2,1)S(1)} %slice.22), channel_id=1, source_target_pairs={{0,1},{1,0},{2,3},{3,2},{4,5},{5,4},{6,7},{7,6},{8,9},{9,8},{10,11... | collective-permute-start | bytes 786440 | tf_op jit(solution)/shard_map/ppermute | solution.py:55
  84.0 1.5 %collective-permute-start.12 = (f32[8,128]{1,0:T(8,128)S(1)}, f32[8,128]{1,0:T(8,128)S(1)}, u32[]{:S(2)}, u32[]{:S(2)}) collective-permute-start(f32[8,128]{1,0:T(8,128)S(1)} %add_add_fusion.mine), channel_id=1, source_target_pairs={{0,1},{1,0},{2,3},{3,2},{4,5},{5,4},{6,7},{7,6},{8,9},{9,8},{10,11... | collective-permute-start | bytes 12296 | tf_op jit(solution)/shard_map/ppermute | solution.py:55
